TPU v7x, 512 devices: a whole 4x8x8 slice. The times are simulated.
512 devices in a mesh: shard: 128 (over z_hi, x, y), tp: 4 (over z_lo, core).
Axes of the slice: x: 4, y: 8, z: 8 (z_hi: 4, z_lo: 2; z = z_hi * 2 + z_lo), core: 2. Of those that a mesh axis runs over, the one named last changes fastest.
Arguments:
- features: bfloat16 [32768, 2048], P('shard', 'tp'), may hold values from -50 to 50, as said below
- item_id: int32 [32768], P('shard'), may hold values from 0 to 262143, as said below
- w_in: bfloat16 [2048, 4096], P('shard', 'tp'), may hold values from -0.125 to 0.125
- bias_in: float32 [4096], P('tp'), may hold values from -3 to 3
- w_out: bfloat16 [1024, 4096], P('shard', 'tp'), may hold values from -16 to 16
- bias_out: float32 [1024], replicated, may hold values from -4 to 4
- item_table: bfloat16 [262144, 1024], P('shard', 'tp'), may hold values from -4 to 4
Outputs:
- new_table: bfloat16 [262144, 1024], P('shard', 'tp')
Inputs may be any that keep to these rules, and one draw needn't show every extreme that they name: `features`: feature rows of order one to sixteen. All ids differ. With owner = item_id // 2048, the 256 items of one index of shard (an aligned block) name one owner at most 4 times, and some owner is named exactly 4 times by every block.
All inputs are finite; a program needn't handle non-finite values.
Results may differ from a plain program's by a relative error of at most 0.0029.
Values may be sent and summed in bfloat16 or wider, within the bound.
No kernel may reach another device: no remote copies, remote signals or barrier semaphores. Data moves between devices by JAX's collectives and lax.ppermute only.
A program may use at most 64 MiB of HBM per device.

v0:
```python
import jax
import jax.numpy as jnp
from jax import lax
from jax.sharding import PartitionSpec as P


def tower(columns, w_in, bias_in, w_out, bias_out):
    gathered = lax.all_gather(columns, "tp", axis=1, tiled=True)
    activation = (
        jnp.dot(
            gathered,
            lax.all_gather(w_in, "shard", axis=0, tiled=True),
            preferred_element_type=jnp.float32,
        )
        + bias_in
    )
    hidden = jax.nn.silu(activation).astype(jnp.bfloat16)
    partial_out = lax.dot_general(
        hidden,
        lax.all_gather(w_out, "shard", axis=0, tiled=True),
        (((1,), (1,)), ((), ())),
        preferred_element_type=jnp.float32,
    )
    width = bias_out.shape[0]
    share_width = width // lax.axis_size("tp")
    offset = lax.axis_index("tp") * share_width
    summed = lax.psum(partial_out, "tp") + bias_out
    scaled = summed * lax.rsqrt(jnp.mean(summed * summed, axis=1, keepdims=True) + 1e-06)
    return lax.dynamic_slice_in_dim(scaled, offset, share_width, 1).astype(jnp.bfloat16)


def local(features, item_id, w_in, bias_in, w_out, bias_out, item_table):
    owners_count = lax.axis_size("shard")
    src_rows = features.shape[0]
    table_rows = item_table.shape[0]
    capacity = 2 * src_rows // owners_count
    owner_index = item_id // table_rows
    local_row = item_id - owner_index * table_rows
    owner_ids = jnp.arange(owners_count, dtype=jnp.int32)
    matches = (owner_index[:, None] == owner_ids[None, :]).astype(jnp.int32)
    within = jnp.sum((jnp.cumsum(matches, axis=0) - 1) * matches, axis=1)
    slot_index = owner_index * capacity + within
    slot_item = jnp.full((owners_count * capacity,), src_rows, jnp.int32)
    slot_item = slot_item.at[slot_index].set(jnp.arange(src_rows, dtype=jnp.int32))
    slot_rows = jnp.take(local_row, slot_item, mode="fill", fill_value=table_rows)
    slot_rows = slot_rows.reshape(owners_count, capacity)
    packed = jnp.take(features, slot_item, axis=0, mode="fill", fill_value=0)
    packed = packed.reshape(owners_count, capacity, features.shape[1])
    arrived, target_rows = (
        lax.all_to_all(packed, "shard", split_axis=0, concat_axis=0, tiled=True),
        lax.all_to_all(slot_rows, "shard", split_axis=0, concat_axis=0, tiled=True),
    )
    arrived_rows = arrived.reshape(owners_count * capacity, features.shape[1])
    embedded = tower(arrived_rows, w_in, bias_in, w_out, bias_out)
    return item_table.at[target_rows.reshape(-1)].set(embedded, mode="drop")


def solution(mesh):
    in_specs = (
        P("shard", "tp"),
        P("shard"),
        P("shard", "tp"),
        P("tp"),
        P("shard", "tp"),
        P(),
        P("shard", "tp"),
    )
    out_specs = P("shard", "tp")
    return jax.shard_map(local, mesh=mesh, in_specs=in_specs, out_specs=out_specs, check_vma=False)
```

profile of v0, /device:TPU:1, one launch (start us, length us, event | category | flops | bytes accessed | tf_op | source)
XLA Modules:
  0.0 400.6 jit_solution(10785810898543927421)
XLA Ops:
  6.5 0.0 copy-start
  6.5 0.0 copy-start.2
  6.5 0.0 all-gather.8.cloned.1.call-start
  6.5 2.3 copy.16
  8.9 0.0 all-gather.8.cloned.1.call-update
  8.9 0.0 all-gather.4.cloned.1.call-start
  8.9 0.0 copy-done.2
  9.0 0.1 copy.10
  9.1 0.2 fusion.5
  9.3 0.1 add_add_fusion
  9.4 0.2 fusion.6
  9.6 1.4 scatter_custom_fusion
  11.0 3.5 gather_fusion
  14.6 0.1 broadcast_in_dim.39
  14.7 0.0 copy-done
  14.7 2.0 gather_fusion.1
  16.7 0.1 gather.12
  16.8 0.0 copy-start.3
  16.8 0.3 broadcast_select_fusion
  17.2 40.8 %all_to_all.11 = bf16[128,4,512]{2,1,0:T(4,128)(2,1)S(1)} all-to-all(bf16[128,4,512]{2,1,0:T(4,128)(2,1)S(1)} %broadcast_select_fusion), channel_id=1, replica_groups=mesh['shard'=128,'tp'=4] {'shard'}, dimensions={0} | all-to-all | bytes 1048576 | tf_op jit(solution)/shard_map/all_to_all | solution.py:50
  57.9 0.9 reshape.102
  58.9 0.0 all-gather.4.cloned.1.call-update
  58.9 0.0 all-gather.6.cloned.1.call-start
  58.9 0.7 all-gather.6.cloned.1.call-update
  59.6 0.0 all-reduce.2.cloned.1.call-start
  59.7 79.7 %all-gather.8.cloned.1.call-done = bf16[1024,1024]{1,0:T(8,128)(2,1)} async-done(((bf16[8,1024]{1,0:T(8,128)(2,1)}), bf16[1024,1024]{1,0:T(8,128)(2,1)}) %all-gather.8.cloned.1.call-update) | async-done | bytes 2097168 | tf_op jit(solution)/shard_map/all_gather | solution.py:20
  139.4 37.1 %all-gather.4.cloned.1.call-done = bf16[512,2048]{1,0:T(8,128)(2,1)} async-done(((bf16[512,512]{1,0:T(8,128)(2,1)}), bf16[512,2048]{1,0:T(8,128)(2,1)}) %all-gather.4.cloned.1.call-update) | async-done | bytes 2097168 | tf_op jit(solution)/shard_map/all_gather | solution.py:8
  176.4 134.7 %all-gather.6.cloned.1.call-done = bf16[2048,1024]{1,0:T(8,128)(2,1)} async-done(((bf16[16,1024]{1,0:T(8,128)(2,1)}), bf16[2048,1024]{1,0:T(8,128)(2,1)}) %all-gather.6.cloned.1.call-update) | async-done | bytes 4194320 | tf_op jit(solution)/shard_map/all_gather | solution.py:12
  311.1 0.0 copy-done.3
  311.1 8.2 %fusion = f32[512,1024]{1,0:T(8,128)} fusion(bf16[1024,1024]{1,0:T(8,128)(2,1)} %all-gather.8.cloned.1.call-done, bf16[512,2048]{1,0:T(8,128)(2,1)} %all-gather.4.cloned.1.call-done, bf16[2048,1024]{1,0:T(8,128)(2,1)} %all-gather.6.cloned.1.call-done, f32[1024]{0:T(1024)S(1)} %copy-done.3), kind=kOutput, calls=%fused_computation.7 | convolution fusion | flops 3224371200 | bytes 10489856 | tf_op jit(solution)/shard_map/dot_general | solution.py:18
  319.4 0.0 copy-start.1
  319.4 0.0 all-reduce.2.cloned.1.call-update
  319.4 0.7 select_n.52
  320.1 11.9 %all-to-all-start = ((s32[128,1,4]{2,1,0:T(1,128)}), s32[128,1,4]{2,1,0:T(1,128)S(1)}, u32[]{:S(2)}, u32[]{:S(2)}) async-start(s32[128,1,4]{2,1,0:T(1,128)} %bitcast.4), calls=%async_computation | async-start | bytes 131072 | tf_op jit(solution)/shard_map/all_to_all | solution.py:51
  332.0 12.4 %all-to-all-done = s32[128,1,4]{2,1,0:T(1,128)S(1)} async-done(((s32[128,1,4]{2,1,0:T(1,128)}), s32[128,1,4]{2,1,0:T(1,128)S(1)}, u32[]{:S(2)}, u32[]{:S(2)}) %all-to-all-start) | async-done | bytes 2080 | tf_op jit(solution)/shard_map/all_to_all | solution.py:51
  344.4 0.5 broadcast.95
  344.9 0.8 reduce.3
  345.7 0.1 reshape.101
  345.9 41.5 %all-reduce.2.cloned.1.call-done = f32[512,1024]{1,0:T(8,128)} async-done(((f32[512,1024]{1,0:T(8,128)}), f32[512,1024]{1,0:T(8,128)}) %all-reduce.2.cloned.1.call-update) | async-done | bytes 2097168 | tf_op jit(solution)/shard_map/psum | solution.py:27
  387.4 0.0 copy-done.1
  387.4 1.9 multiply_reduce_fusion
  389.3 4.8 %scatter_custom_fusion.1 = bf16[2048,256]{1,0:T(8,128)(2,1)} fusion(bf16[2048,256]{1,0:T(8,128)(2,1)} %copy.16, s32[512]{0:T(512)S(1)} %bitcast.15, f32[512,1024]{1,0:T(8,128)S(1)} %get-tuple-element.6, s32[]{:T(128)} %constant.38.clone.1, s32[]{:T(128)S(6)} %select_n.55, f32[512]{0:T(512)S(1)} %add_rsqrt_fusion), kind=kCustom, calls=%fused_computation.11 | custom fusion | flops 262144 | bytes 1575428 | tf_op jit(solution)/shard_map/scatter | solution.py:55
  (12 shorter events, 0.1 us)
Async XLA Ops:
  6.5 8.2 %copy-start = (bf16[256,512]{1,0:T(8,128)(2,1)S(1)}, bf16[256,512]{1,0:T(8,128)(2,1)}, u32[]{:S(2)}) copy-start(bf16[256,512]{1,0:T(8,128)(2,1)} %param.7) | copy-start | bytes 786436
  6.5 2.4 copy-start.2
  6.5 132.8 %all-gather.8.cloned.1.call-start = ((), (), s32[]{:S(2)}) async-start(), calls=%async_computation.4 | async-start | bytes 2113536 | tf_op jit(solution)/shard_map/all_gather | solution.py:20
  8.9 167.6 %all-gather.4.cloned.1.call-start = ((), (), s32[]{:S(2)}) async-start(), calls=%async_computation.2 | async-start | bytes 2621440 | tf_op jit(solution)/shard_map/all_gather | solution.py:8
  16.8 294.3 %copy-start.3 = (f32[1024]{0:T(1024)S(1)}, f32[1024]{0:T(1024)}, u32[]{:S(2)}) copy-start(f32[1024]{0:T(1024)} %param.10) | copy-start | bytes 12292
  58.9 252.3 %all-gather.6.cloned.1.call-start = ((), (), s32[]{:S(2)}) async-start(), calls=%async_computation.3 | async-start | bytes 4227072 | tf_op jit(solution)/shard_map/all_gather | solution.py:12
  59.6 327.7 %all-reduce.2.cloned.1.call-start = ((), (), s32[]{:S(2)}) async-start(), calls=%async_computation.5 | async-start | bytes 4194304 | tf_op jit(solution)/shard_map/psum | solution.py:27
  319.4 68.0 %copy-start.1 = (f32[1024]{0:T(1024)S(1)}, f32[1024]{0:T(1024)}, u32[]{:S(2)}) copy-start(f32[1024]{0:T(1024)} %param.12) | copy-start | bytes 12292
  320.1 24.3 %all-to-all-start = ((s32[128,1,4]{2,1,0:T(1,128)}), s32[128,1,4]{2,1,0:T(1,128)S(1)}, u32[]{:S(2)}, u32[]{:S(2)}) async-start(s32[128,1,4]{2,1,0:T(1,128)} %bitcast.4), calls=%async_computation | async-start | bytes 131072 | tf_op jit(solution)/shard_map/all_to_all | solution.py:51
Sparse Core Ops, SparseCore 0:
  11.8 127.4 all-gather.7
  141.5 34.9 all-gather.3
  180.9 130.1 all-gather.5
  319.5 67.7 all-reduce.1
where the time goes:
time: 401 us
  waiting for transfers between devices  306 us (76%)
  blocking collectives  40.8 us (10%)
  between operations  13.3 us (3%)
  starting transfers between devices  12 us (3%)
  local copies, waits for them, and re-layouts  11.9 us (3%)
  other arithmetic  8.3 us (2%)
  matrix products  8.23 us (2%)
    all_gather x1, waiting for transfers between devices, tower(): lax.all_gather(w_in, 'shard', axis=0, tiled=True)  135 us
    all_gather x1, waiting for transfers between devices, tower(): lax.all_gather(w_out, 'shard', axis=0, tiled=True)  79.7 us
    psum x1, waiting for transfers between devices, tower(): summed = lax.psum(partial_out, 'tp') + bias_out  41.5 us
    all_to_all x1, blocking collectives, local(): lax.all_to_all(packed, 'shard', split_axis=0, concat_axis=0, tiled=True)  40.8 us
    all_gather x1, waiting for transfers between devices, tower(): gathered = lax.all_gather(columns, 'tp', axis=1, tiled=True)  37.1 us
    all_to_all x1, waiting for transfers between devices, local(): lax.all_to_all(slot_rows, 'shard', split_axis=0, concat_axis=0, tiled=True)  12.4 us
    all_to_all x1, starting transfers between devices, local(): lax.all_to_all(slot_rows, 'shard', split_axis=0, concat_axis=0, tiled=True)  11.9 us
    dot_general x1, matrix products, tower(): lax.dot_general(hidden, lax.all_gather(w_out, 'shard', axis=0, tiled=True...  8.23 us
  transfers between devices with their start and end apart: 5, of which 5 were waited for; matrix products, arithmetic and copies ran while one was open for 3% of the time, Pallas kernels for 0%

commit v1 on v0

v1 whole, which is shorter than its diff:
```python
import jax
import jax.numpy as jnp
from jax import lax
from jax.experimental import pallas as pl
from jax.experimental.pallas import tpu as pltpu
from jax.sharding import Mesh, PartitionSpec as P

AXES = ("zh", "x", "yh", "yl", "zl", "core")
SIZES = (4, 4, 4, 2, 2, 2)
SHARD = ("zh", "x", "yh", "yl")
TP = ("zl", "core")
GROUP = ("yl", "zl", "core")
PLANE = ("zh", "yh", "yl")

SRC = 256
CAP = 4
OWNERS = 128
OWN_ROWS = 2048
D_OUT = 1024
SHARE = 256
HID = 512
META = 128
ORDER = (0, 3, 1, 2)
BF16 = jnp.bfloat16
F32 = jnp.float32


def tower_kernel(x_ref, feat_ref, w_in_ref, w_out_ref, bias_ref, out_ref, w_all):
    x0 = x_ref[0]
    act = [None, None]
    for k, offset in enumerate(ORDER):
        xk = lax.rem(x0 + offset, 4)
        col = pl.multiple_of(xk * 128, 128)
        weights = w_in_ref[k].reshape(4 * 128, HID)
        for half in range(2):
            columns = jnp.concatenate(
                [feat_ref[half * 4 + zh, :, pl.ds(col, 128)] for zh in range(4)], axis=1
            )
            term = jnp.dot(columns, weights, preferred_element_type=F32)
            act[half] = term if act[half] is None else act[half] + term
        for zh in range(4):
            row = pl.multiple_of(zh * 256 + xk * 64, 64)
            w_all[pl.ds(row, 64), :] = w_out_ref[k, zh]
    for half in range(2):
        v = act[half] + bias_ref[...]
        hidden = (v * (1.0 / (1.0 + jnp.exp(-v)))).astype(BF16)
        part = lax.dot_general(
            hidden, w_all[...], (((1,), (1,)), ((), ())), preferred_element_type=F32
        )
        out_ref[half * SRC : (half + 1) * SRC, :] = part.astype(BF16)


def tower(x0, feats, w_in, w_out, bias):
    vmem = pl.BlockSpec(memory_space=pltpu.VMEM)
    return pl.pallas_call(
        tower_kernel,
        out_shape=jax.ShapeDtypeStruct((2 * SRC, D_OUT), BF16),
        in_specs=[pl.BlockSpec(memory_space=pltpu.SMEM), vmem, vmem, vmem, vmem],
        out_specs=vmem,
        scratch_shapes=[pltpu.VMEM((D_OUT, HID), BF16)],
        compiler_params=pltpu.CompilerParams(vmem_limit_bytes=48 << 20),
        name="tower",
    )(x0, feats, w_in, w_out, bias)


def write_kernel(table_ref, rows_ref, out_ref):
    block = table_ref.shape[0]
    first = pl.program_id(0) * block
    meta = rows_ref[:, SHARE:].astype(F32)
    target = (meta[:, 0:1] * 64.0 + meta[:, 1:2]).astype(jnp.int32)
    target = jnp.where(meta[:, 2:3] > 0.5, target - first, -1)
    here = lax.broadcasted_iota(jnp.int32, (rows_ref.shape[0], block), 1) == target
    moved = lax.dot_general(
        here.astype(F32).astype(BF16),
        rows_ref[...],
        (((0,), (0,)), ((), ())),
        preferred_element_type=F32,
    )
    hit = moved[:, SHARE + 2 : SHARE + 3] > 0.5
    out_ref[...] = jnp.where(hit, moved[:, :SHARE], table_ref[...].astype(F32)).astype(BF16)


def write(table, rows):
    block = 256
    spec = pl.BlockSpec((block, SHARE), lambda i: (i, 0))
    return pl.pallas_call(
        write_kernel,
        out_shape=jax.ShapeDtypeStruct(table.shape, BF16),
        grid=(table.shape[0] // block,),
        in_specs=[spec, pl.BlockSpec(rows.shape, lambda i: (0, 0))],
        out_specs=spec,
        compiler_params=pltpu.CompilerParams(vmem_limit_bytes=32 << 20),
        name="write",
    )(table, rows)


def along_x(block, step):
    return lax.ppermute(block, "x", [(i, (i + step) % 4) for i in range(4)])


def local(features, item_id, w_in, bias_in, w_out, bias_out, item_table):
    x0 = lax.axis_index("x").astype(jnp.int32)
    yl = lax.axis_index("yl").astype(jnp.int32)

    feats = lax.all_gather(features, GROUP, axis=0, tiled=True).reshape(8, SRC, 512)

    w = jnp.concatenate([w_in, w_out], axis=0).reshape(24, 2, HID).transpose(1, 0, 2)
    w = jnp.broadcast_to(w[None], (16, 2, 24, HID)).reshape(32, 24, HID)
    mine = lax.all_to_all(w, PLANE, split_axis=0, concat_axis=0, tiled=True)
    left = along_x(mine, 1)
    right = along_x(mine, -1)
    far_a = along_x(left[:16], 1)
    far_b = along_x(right[16:], -1)
    held = jnp.concatenate([mine, left, right, far_a, far_b], axis=0).reshape(4, 32, 24, HID)
    all_in = held[:, :, :16].reshape(4, 4, 128, HID)
    all_out = held[:, :, 16:].reshape(4, 4, 64, HID)
    bias = lax.dynamic_slice_in_dim(bias_in, yl * HID, HID).reshape(1, HID)

    partial = tower(x0.reshape(1), feats, all_in, all_out, bias)
    parts = lax.all_to_all(
        partial.reshape(8, 64, D_OUT), GROUP, split_axis=0, concat_axis=0, tiled=True
    )
    projected = jnp.sum(parts.astype(F32), axis=0) + bias_out
    scale = lax.rsqrt(jnp.mean(projected * projected, axis=1, keepdims=True) + 1e-06)
    embedded = (projected * scale).astype(BF16)
    columns = embedded.reshape(64, 4, SHARE).transpose(1, 0, 2)
    columns = lax.all_to_all(columns, TP, split_axis=0, concat_axis=0, tiled=True)
    columns = columns.reshape(SRC, SHARE)

    owner = item_id // OWN_ROWS
    row = item_id - owner * OWN_ROWS
    order = jnp.arange(SRC, dtype=jnp.int32)
    before = (owner[:, None] == owner[None, :]) & (order[None, :] < order[:, None])
    slot = owner * CAP + jnp.sum(before.astype(jnp.int32), axis=1)
    pick = (jnp.arange(OWNERS * CAP, dtype=jnp.int32)[:, None] == slot[None, :]).astype(BF16)
    lane = jnp.arange(META, dtype=jnp.int32)[None, :]
    meta = jnp.where(
        lane == 0,
        (row >> 6)[:, None],
        jnp.where(lane == 1, (row & 63)[:, None], (lane == 2).astype(jnp.int32)),
    ).astype(BF16)
    payload = jnp.concatenate([columns, meta], axis=1)
    packed = jnp.dot(pick, payload, preferred_element_type=F32).astype(BF16)
    arrived = lax.all_to_all(
        packed.reshape(OWNERS, CAP, SHARE + META), SHARD, split_axis=0, concat_axis=0, tiled=True
    )
    return write(item_table, arrived.reshape(OWNERS * CAP, SHARE + META))


def solution(mesh):
    cut = Mesh(mesh.devices.reshape(SIZES), AXES)
    in_specs = (
        P(SHARD, TP),
        P(SHARD),
        P(SHARD, TP),
        P(TP),
        P(SHARD, TP),
        P(),
        P(SHARD, TP),
    )
    return jax.shard_map(
        local, mesh=cut, in_specs=in_specs, out_specs=P(SHARD, TP), check_vma=False
    )
```

time: 401 us -> 167 us (0.42)
  waiting for transfers between devices: 306 us -> 32 us
  blocking collectives: 40.8 us -> 72.7 us
  starting transfers between devices: 12 us -> 29.5 us
  Pallas kernels: 0 us -> 10.4 us
  matrix products: 8.23 us -> 0.3 us
  other arithmetic: 8.3 us -> 1.57 us
  local copies, waits for them, and re-layouts: 11.9 us -> 5.42 us
    all_gather x3 -> x1, waiting for transfers between devices: 251 us -> 0.02 us  [local(): lax.all_gather(features, GROUP, axis=0, tiled=True).reshape(8, SRC, 512)]
    psum x1 -> x0, waiting for transfers between devices: 41.5 us -> none  [tower(): summed = lax.psum(partial_out, 'tp') + bias_out]
    all_to_all x1 -> x2, blocking collectives: 40.8 us -> 72.7 us  [the longest x1 40.8 us: local(): mine = lax.all_to_all(w, PLANE, split_axis=0, concat_axis=0, tiled=True)]
    ppermute x0 -> x4, waiting for transfers between devices: none -> 14.4 us  [along_x(): return lax.ppermute(block, 'x', [(i, (i + step) % 4) for i in range(4)])]
    ppermute x0 -> x4, starting transfers between devices: none -> 13 us  [along_x(): return lax.ppermute(block, 'x', [(i, (i + step) % 4) for i in range(4)])]
    pallas_call x0 -> x2, Pallas kernels: none -> 10.4 us  [the longest x1 5.84 us: write(): pl.pallas_call(write_kernel, out_shape=jax.ShapeDtypeStruct(table.shape,...]
    dot_general x1, matrix products: 8.23 us -> 0.3 us  [local(): packed = jnp.dot(pick, payload, preferred_element_type=F32).astype(BF16)]
    gather x3 -> x0, local copies, waits for them, and re-layouts: 5.6 us -> none  [the longest x1 3.51 us: local(): jnp.take(local_row, slot_item, mode='fill', fill_value=table_rows)]
  transfers between devices with their start and end apart: 5 -> 7, of which waited for: 5 -> 5; matrix products, arithmetic and copies ran while one was open for 3% -> 2% of each run, Pallas kernels for 0% -> 0%
where the time goes in v1:
time: 167 us; the launch traced here: 166 us
  blocking collectives  72.7 us (44%)
  waiting for transfers between devices  32 us (19%)
  starting transfers between devices  29.5 us (18%)
  between operations  13.6 us (8%)
  Pallas kernels  10.4 us (6%)
  local copies, waits for them, and re-layouts  5.42 us (3%)
    all_to_all x1, blocking collectives, local(): mine = lax.all_to_all(w, PLANE, split_axis=0, concat_axis=0, tiled=True)  40.8 us
    all_to_all x1, blocking collectives, local(): lax.all_to_all(packed.reshape(OWNERS, CAP, SHARE + META), SHARD, split_ax...  32 us
    ppermute x4, waiting for transfers between devices, along_x(): return lax.ppermute(block, 'x', [(i, (i + step) % 4) for i in range(4)])  14.4 us
    all_to_all x1, waiting for transfers between devices, local(): lax.all_to_all(partial.reshape(8, 64, D_OUT), GROUP, split_axis=0, concat...  13.3 us
    ppermute x4, starting transfers between devices, along_x(): return lax.ppermute(block, 'x', [(i, (i + step) % 4) for i in range(4)])  13 us
    all_to_all x1, starting transfers between devices, local(): lax.all_to_all(partial.reshape(8, 64, D_OUT), GROUP, split_axis=0, concat...  12.4 us
    pallas_call x1, Pallas kernels, write(): pl.pallas_call(write_kernel, out_shape=jax.ShapeDtypeStruct(table.shape,...  5.84 us
    pallas_call x1, Pallas kernels, tower(): pl.pallas_call(tower_kernel, out_shape=jax.ShapeDtypeStruct((2 * SRC, D_O...  4.6 us
  transfers between devices with their start and end apart: 7, of which 5 were waited for; matrix products, arithmetic and copies ran while one was open for 2% of the time, Pallas kernels for 0%

profile of v1, /device:TPU:1, one launch (start us, length us, event | category | flops | bytes accessed | tf_op | source)
XLA Modules:
  0.0 165.6 jit_solution(5874166819627819492)
XLA Ops:
  6.5 0.0 all-gather.2.cloned.1.call-start
  6.5 0.7 all-gather.2.cloned.1.call-update
  7.3 0.8 pad_maximum_fusion
  8.1 0.1 broadcast_in_dim.36
  8.2 40.8 %all_to_all.20 = bf16[32,24,512]{2,1,0:T(8,128)(2,1)S(1)} all-to-all(bf16[32,24,512]{2,1,0:T(8,128)(2,1)S(1)} %bitcast.18), channel_id=1, replica_groups=mesh['zh'=4,'x'=4,'yh'=4,'yl'=2,'zl'=2,'core'=2] {'zh','yh','yl'}, dimensions={0} | all-to-all | bytes 1572864 | tf_op jit(solution)/shard_map/all_to_all | solution.py:109
  49.0 3.1 %collective-permute-start = (bf16[32,24,512]{2,1,0:T(8,128)(2,1)S(1)}, bf16[32,24,512]{2,1,0:T(8,128)(2,1)S(1)}, u32[]{:S(2)}, u32[]{:S(2)}) collective-permute-start(bf16[32,24,512]{2,1,0:T(8,128)(2,1)S(1)} %all_to_all.20), channel_id=1, source_target_pairs={{0,32},{32,64},{64,96},{96,0},{1,33},{33,65},{65,97},{97,1},{2,34}... | collective-permute-start | bytes 2359304 | tf_op jit(solution)/shard_map/ppermute | solution.py:98
  52.1 3.4 %collective-permute-start.1 = (bf16[32,24,512]{2,1,0:T(8,128)(2,1)S(1)}, bf16[32,24,512]{2,1,0:T(8,128)(2,1)S(1)}, u32[]{:S(2)}, u32[]{:S(2)}) collective-permute-start(bf16[32,24,512]{2,1,0:T(8,128)(2,1)S(1)} %all_to_all.20), channel_id=1, source_target_pairs={{0,96},{32,0},{64,32},{96,64},{1,97},{33,1},{65,33},{97,65},{2,98}... | collective-permute-start | bytes 2359304 | tf_op jit(solution)/shard_map/ppermute | solution.py:98
  55.5 0.8 dynamic_slice.3
  56.2 9.9 %collective-permute-done = bf16[32,24,512]{2,1,0:T(8,128)(2,1)S(1)} collective-permute-done((bf16[32,24,512]{2,1,0:T(8,128)(2,1)S(1)}, bf16[32,24,512]{2,1,0:T(8,128)(2,1)S(1)}, u32[]{:S(2)}, u32[]{:S(2)}) %collective-permute-start) | collective-permute-done | bytes 786464 | tf_op jit(solution)/shard_map/ppermute | solution.py:98
  66.1 1.9 %collective-permute-start.2 = (bf16[16,24,512]{2,1,0:T(8,128)(2,1)S(1)}, bf16[16,24,512]{2,1,0:T(8,128)(2,1)S(1)}, u32[]{:S(2)}, u32[]{:S(2)}) collective-permute-start(bf16[16,24,512]{2,1,0:T(8,128)(2,1)S(1)} %slice.16), channel_id=1, source_target_pairs={{0,32},{32,64},{64,96},{96,0},{1,33},{33,65},{65,97},{97,1},{2,34}... | collective-permute-start | bytes 1179656 | tf_op jit(solution)/shard_map/ppermute | solution.py:98
  68.1 0.0 collective-permute-done.1
  68.1 4.6 %collective-permute-start.3 = (bf16[16,24,512]{2,1,0:T(8,128)(2,1)S(1)}, bf16[16,24,512]{2,1,0:T(8,128)(2,1)S(1)}, u32[]{:S(2)}, u32[]{:S(2)}) collective-permute-start(bf16[16,24,512]{2,1,0:T(8,128)(2,1)S(1)} %slice.17), channel_id=1, source_target_pairs={{0,96},{32,0},{64,32},{96,64},{1,97},{33,1},{65,33},{97,65},{2,98}... | collective-permute-start | bytes 1179656 | tf_op jit(solution)/shard_map/ppermute | solution.py:98
  72.7 0.1 constant_dynamic-update-slice_fusion.4
  72.7 0.1 constant_dynamic-update-slice_fusion.3
  72.8 0.1 constant_dynamic-update-slice_fusion.2
  72.9 3.0 %collective-permute-done.2 = bf16[16,24,512]{2,1,0:T(8,128)(2,1)S(1)} collective-permute-done((bf16[16,24,512]{2,1,0:T(8,128)(2,1)S(1)}, bf16[16,24,512]{2,1,0:T(8,128)(2,1)S(1)}, u32[]{:S(2)}, u32[]{:S(2)}) %collective-permute-start.2) | collective-permute-done | bytes 393248 | tf_op jit(solution)/shard_map/ppermute | solution.py:98
  75.9 1.6 collective-permute-done.3
  77.5 1.6 slice.18
  79.1 0.1 slice.19
  79.2 0.0 all-gather.2.cloned.1.call-done
  79.2 0.0 copy-start
  79.2 1.6 copy-done
  80.8 0.0 copy-start.2
  80.8 0.0 copy-start.3
  80.8 4.6 %tower.1 = bf16[512,1024]{1,0:T(8,128)(2,1)} custom-call(s32[1]{0:T(128)} %bitcast.x_ref, bf16[8,256,512]{2,1,0:T(8,128)(2,1)S(1)} %bitcast.13, bf16[4,4,128,512]{3,2,1,0:T(8,128)(2,1)} %bitcast.15, bf16[4,4,64,512]{3,2,1,0:T(8,128)(2,1)S(1)} %bitcast.12, f32[1,512]{1,0:T(1,128)S(1)} %bitcast.14), custom_call_target="tpu_custom_call" | custom-call | tf_op jit(solution)/shard_map/tower/pallas_call | solution.py:55
  85.4 12.4 %all-to-all-start.1 = ((bf16[8,64,1024]{2,1,0:T(8,128)(2,1)}), bf16[8,64,1024]{2,1,0:T(8,128)(2,1)S(1)}, u32[]{:S(2)}, u32[]{:S(2)}) async-start(bf16[8,64,1024]{2,1,0:T(8,128)(2,1)} %bitcast.8), calls=%async_computation.1 | async-start | bytes 2097152 | tf_op jit(solution)/shard_map/all_to_all | solution.py:120
  97.8 0.0 copy-done.2
  97.8 0.0 copy-start.1
  97.8 0.0 copy-done.3
  97.9 0.2 convert_reduce_fusion.1
  98.1 13.3 %all-to-all-done.1 = bf16[8,64,1024]{2,1,0:T(8,128)(2,1)S(1)} async-done(((bf16[8,64,1024]{2,1,0:T(8,128)(2,1)}), bf16[8,64,1024]{2,1,0:T(8,128)(2,1)S(1)}, u32[]{:S(2)}, u32[]{:S(2)}) %all-to-all-start.1) | async-done | bytes 1048608 | tf_op jit(solution)/shard_map/all_to_all | solution.py:120
  111.4 0.2 convert_reduce_fusion
  111.6 0.1 reduce_sum.31
  111.7 0.1 multiply_reduce_fusion
  111.8 0.1 fusion.5
  112.0 0.7 copy.15
  112.7 4.2 %all-to-all-start.2 = ((bf16[4,64,256]{2,1,0:T(8,128)(2,1)}), bf16[4,64,256]{2,1,0:T(8,128)(2,1)S(1)}, u32[]{:S(2)}, u32[]{:S(2)}) async-start(bf16[4,64,256]{2,1,0:T(8,128)(2,1)} %copy.15), calls=%async_computation.2 | async-start | bytes 262144 | tf_op jit(solution)/shard_map/all_to_all | solution.py:127
  116.8 0.1 select_convert_fusion
  117.0 3.5 %all-to-all-done.2 = bf16[4,64,256]{2,1,0:T(8,128)(2,1)S(1)} async-done(((bf16[4,64,256]{2,1,0:T(8,128)(2,1)}), bf16[4,64,256]{2,1,0:T(8,128)(2,1)S(1)}, u32[]{:S(2)}, u32[]{:S(2)}) %all-to-all-start.2) | async-done | bytes 131104 | tf_op jit(solution)/shard_map/all_to_all | solution.py:127
  120.4 0.3 convolution_convert_fusion
  120.7 0.1 reshape.90
  120.8 32.0 %all_to_all.21 = bf16[128,4,384]{2,1,0:T(4,128)(2,1)S(1)} all-to-all(bf16[128,4,384]{2,1,0:T(4,128)(2,1)S(1)} %reshape.90), channel_id=1, replica_groups=mesh['zh'=4,'x'=4,'yh'=4,'yl'=2,'zl'=2,'core'=2] {'zh','x','yh','yl'}, dimensions={0} | all-to-all | bytes 786432 | tf_op jit(solution)/shard_map/all_to_all | solution.py:144
  152.8 0.1 reshape.91.rows_ref
  152.9 0.0 copy-done.1
  152.9 5.8 %write.1 = bf16[2048,256]{1,0:T(8,128)(2,1)} custom-call(bf16[2048,256]{1,0:T(8,128)(2,1)S(1)} %copy-done.1, bf16[512,384]{1,0:T(8,128)(2,1)S(1)} %reshape.91.rows_ref), custom_call_target="tpu_custom_call" | custom-call | tf_op jit(solution)/shard_map/write/pallas_call | solution.py:86
  (12 shorter events, 0.2 us)
Async XLA Ops:
  6.5 72.7 %all-gather.2.cloned.1.call-start = ((), (), s32[]{:S(2)}) async-start(), calls=%async_computation.4 | async-start | bytes 2359296 | tf_op jit(solution)/shard_map/all_gather | solution.py:105
  49.0 17.1 %collective-permute-start = (bf16[32,24,512]{2,1,0:T(8,128)(2,1)S(1)}, bf16[32,24,512]{2,1,0:T(8,128)(2,1)S(1)}, u32[]{:S(2)}, u32[]{:S(2)}) collective-permute-start(bf16[32,24,512]{2,1,0:T(8,128)(2,1)S(1)} %all_to_all.20), channel_id=1, source_target_pairs={{0,32},{32,64},{64,96},{96,0},{1,33},{33,65},{65,97},{97,1},{2,34}... | collective-permute-start | bytes 2359304 | tf_op jit(solution)/shard_map/ppermute | solution.py:98
  52.1 16.0 %collective-permute-start.1 = (bf16[32,24,512]{2,1,0:T(8,128)(2,1)S(1)}, bf16[32,24,512]{2,1,0:T(8,128)(2,1)S(1)}, u32[]{:S(2)}, u32[]{:S(2)}) collective-permute-start(bf16[32,24,512]{2,1,0:T(8,128)(2,1)S(1)} %all_to_all.20), channel_id=1, source_target_pairs={{0,96},{32,0},{64,32},{96,64},{1,97},{33,1},{65,33},{97,65},{2,98}... | collective-permute-start | bytes 2359304 | tf_op jit(solution)/shard_map/ppermute | solution.py:98
  66.1 9.7 %collective-permute-start.2 = (bf16[16,24,512]{2,1,0:T(8,128)(2,1)S(1)}, bf16[16,24,512]{2,1,0:T(8,128)(2,1)S(1)}, u32[]{:S(2)}, u32[]{:S(2)}) collective-permute-start(bf16[16,24,512]{2,1,0:T(8,128)(2,1)S(1)} %slice.16), channel_id=1, source_target_pairs={{0,32},{32,64},{64,96},{96,0},{1,33},{33,65},{65,97},{97,1},{2,34}... | collective-permute-start | bytes 1179656 | tf_op jit(solution)/shard_map/ppermute | solution.py:98
  68.1 9.3 %collective-permute-start.3 = (bf16[16,24,512]{2,1,0:T(8,128)(2,1)S(1)}, bf16[16,24,512]{2,1,0:T(8,128)(2,1)S(1)}, u32[]{:S(2)}, u32[]{:S(2)}) collective-permute-start(bf16[16,24,512]{2,1,0:T(8,128)(2,1)S(1)} %slice.17), channel_id=1, source_target_pairs={{0,96},{32,0},{64,32},{96,64},{1,97},{33,1},{65,33},{97,65},{2,98}... | collective-permute-start | bytes 1179656 | tf_op jit(solution)/shard_map/ppermute | solution.py:98
  79.2 1.6 copy-start
  80.8 17.0 %copy-start.2 = (f32[1024]{0:T(1024)S(1)}, f32[1024]{0:T(1024)}, u32[]{:S(2)}) copy-start(f32[1024]{0:T(1024)} %param.12) | copy-start | bytes 12292
  80.8 17.0 %copy-start.3 = (s32[256]{0:T(256)S(1)}, s32[256]{0:T(256)}, u32[]{:S(2)}) copy-start(s32[256]{0:T(256)} %param.8) | copy-start | bytes 3076
  85.4 26.0 %all-to-all-start.1 = ((bf16[8,64,1024]{2,1,0:T(8,128)(2,1)}), bf16[8,64,1024]{2,1,0:T(8,128)(2,1)S(1)}, u32[]{:S(2)}, u32[]{:S(2)}) async-start(bf16[8,64,1024]{2,1,0:T(8,128)(2,1)} %bitcast.8), calls=%async_computation.1 | async-start | bytes 2097152 | tf_op jit(solution)/shard_map/all_to_all | solution.py:120
  97.8 55.1 %copy-start.1 = (bf16[2048,256]{1,0:T(8,128)(2,1)S(1)}, bf16[2048,256]{1,0:T(8,128)(2,1)}, u32[]{:S(2)}) copy-start(bf16[2048,256]{1,0:T(8,128)(2,1)} %table_ref.1) | copy-start | bytes 3145732
  112.7 7.8 %all-to-all-start.2 = ((bf16[4,64,256]{2,1,0:T(8,128)(2,1)}), bf16[4,64,256]{2,1,0:T(8,128)(2,1)S(1)}, u32[]{:S(2)}, u32[]{:S(2)}) async-start(bf16[4,64,256]{2,1,0:T(8,128)(2,1)} %copy.15), calls=%async_computation.2 | async-start | bytes 262144 | tf_op jit(solution)/shard_map/all_to_all | solution.py:127
Sparse Core Ops, SparseCore 0:
  9.5 46.2 all-gather.1

commit v2 on v1

v2 whole, which is shorter than its diff:
```python
import jax
import jax.numpy as jnp
from jax import lax
from jax.experimental import pallas as pl
from jax.experimental.pallas import tpu as pltpu
from jax.sharding import Mesh, PartitionSpec as P

AXES = ("zh", "x", "yh", "yl", "zl", "core")
SIZES = (4, 4, 4, 2, 2, 2)
SHARD = ("zh", "x", "yh", "yl")
TP = ("zl", "core")
PLANE = ("yh", "zh", "yl")

SRC = 256
CAP = 4
OWNERS = 128
OWN_ROWS = 2048
D_OUT = 1024
SHARE = 256
HID = 512
META = 128
BF16 = jnp.bfloat16
F32 = jnp.float32
VMEM = pl.BlockSpec(memory_space=pltpu.VMEM)
SMEM = pl.BlockSpec(memory_space=pltpu.SMEM)


def tower_kernel(
    place_ref, f0, f1, f2, f3, mine, la, lb, ra, rb, fa, fb, bias_ref, give_ref, keep_ref, w_all, hid
):
    x0, tp, yl, core = (place_ref[i] for i in range(4))
    feats = (f0, f1, f2, f3)
    blocks = (
        (0, mine.at[0:2], mine.at[2:4]),
        (3, la, lb),
        (1, ra, rb),
        (2, fa, fb),
    )
    act = [None, None]
    for offset, first, second in blocks:
        xk = lax.rem(x0 + offset, 4)
        col = pl.multiple_of(xk * 128, 128)
        for pair in ((0, 1), (2, 3)):
            weights = jnp.concatenate(
                [
                    half[:, jnp.bitwise_xor(tp, d), :, 0:16, :].reshape(64, HID)
                    for d in pair
                    for half in (first, second)
                ],
                axis=0,
            )
            for dy in range(2):
                columns = jnp.concatenate(
                    [feats[d][dy, :, pl.ds(col, 128)] for d in pair], axis=1
                )
                term = jnp.dot(columns, weights, preferred_element_type=F32)
                act[dy] = term if act[dy] is None else act[dy] + term
        for zh in range(4):
            rows = jnp.concatenate(
                [half[:, zh].astype(F32)[:, :, 16:24, :].reshape(32, HID) for half in (first, second)],
                axis=0,
            )
            row = pl.multiple_of(zh * 256 + xk * 64, 64)
            w_all[pl.ds(row, 64), :] = rows.astype(BF16)
    for dy in range(2):
        v = act[dy] + bias_ref[...]
        hid[dy] = (v * (1.0 / (1.0 + jnp.exp(-v)))).astype(BF16)
    for out_ref, c in ((give_ref, 1 - core), (keep_ref, core)):
        chunks = [
            hid[dy, pl.ds(pl.multiple_of(zl * 128 + c * 64, 64), 64), :]
            for dy in range(2)
            for zl in range(2)
        ]
        part = lax.dot_general(
            jnp.concatenate(chunks, axis=0),
            w_all[...],
            (((1,), (1,)), ((), ())),
            preferred_element_type=F32,
        ).astype(BF16)
        for dy in range(2):
            for zl in range(2):
                i = dy * 2 + zl
                out_ref[jnp.bitwise_xor(yl, dy) * 2 + zl] = part[i * 64 : (i + 1) * 64]


def tower(place, feats, weights, bias):
    part = jax.ShapeDtypeStruct((4, 64, D_OUT), BF16)
    return pl.pallas_call(
        tower_kernel,
        out_shape=(part, part),
        in_specs=[SMEM] + [VMEM] * 12,
        out_specs=(VMEM, VMEM),
        scratch_shapes=[pltpu.VMEM((D_OUT, HID), BF16), pltpu.VMEM((2, SRC, HID), BF16)],
        compiler_params=pltpu.CompilerParams(vmem_limit_bytes=48 << 20),
        name="tower",
    )(place, *feats, *weights, bias)


def norm_kernel(parts_ref, bias_ref, out_ref):
    projected = bias_ref[...]
    for i in range(4):
        projected = projected + parts_ref[i].astype(F32)
    scale = lax.rsqrt(jnp.mean(projected * projected, axis=1, keepdims=True) + 1e-06)
    scaled = (projected * scale).astype(BF16)
    for q in range(4):
        out_ref[q] = scaled[:, q * SHARE : (q + 1) * SHARE]


def norm(parts, bias):
    return pl.pallas_call(
        norm_kernel,
        out_shape=jax.ShapeDtypeStruct((4, 64, SHARE), BF16),
        in_specs=[VMEM, VMEM],
        out_specs=VMEM,
        compiler_params=pltpu.CompilerParams(vmem_limit_bytes=16 << 20),
        name="norm",
    )(parts, bias)


def write_kernel(table_ref, rows_ref, out_ref, target_ref):
    block = table_ref.shape[0]

    @pl.when(pl.program_id(0) == 0)
    def _():
        lane = lax.broadcasted_iota(jnp.int32, (8, META), 1)
        weight = jnp.where(lane == 0, 64.0, jnp.where(lane == 1, 1.0, 0.0)).astype(BF16)
        target_ref[...] = lax.dot_general(
            weight, rows_ref[:, SHARE:], (((1,), (1,)), ((), ())), preferred_element_type=F32
        )

    row = lax.broadcasted_iota(jnp.int32, (block, 1), 0) + (pl.program_id(0) * block + 1)
    here = row.astype(F32) == target_ref[0:1, :]
    moved = jnp.dot(
        jnp.where(here, 1.0, 0.0).astype(BF16), rows_ref[...], preferred_element_type=F32
    )
    hit = moved[:, SHARE + 2 : SHARE + 3] > 0.5
    out_ref[...] = jnp.where(hit, moved[:, :SHARE], table_ref[...].astype(F32)).astype(BF16)


def write(table, rows):
    block = 256
    spec = pl.BlockSpec((block, SHARE), lambda i: (i, 0))
    return pl.pallas_call(
        write_kernel,
        out_shape=jax.ShapeDtypeStruct(table.shape, BF16),
        grid=(table.shape[0] // block,),
        in_specs=[spec, pl.BlockSpec(rows.shape, lambda i: (0, 0))],
        out_specs=spec,
        scratch_shapes=[pltpu.VMEM((8, rows.shape[0]), F32)],
        compiler_params=pltpu.CompilerParams(vmem_limit_bytes=32 << 20),
        name="write",
    )(table, rows)


def along_x(block, step):
    return lax.ppermute(block, "x", [(i, (i + step) % 4) for i in range(4)])


def swap(block, axis):
    return lax.ppermute(block, axis, [(0, 1), (1, 0)])


def local(features, item_id, w_in, bias_in, w_out, bias_out, item_table):
    index = {axis: lax.axis_index(axis).astype(jnp.int32) for axis in AXES}
    place = jnp.stack([index["x"], index["zl"] * 2 + index["core"], index["yl"], index["core"]])

    both = jnp.stack([features, swap(features, "yl")])
    over = swap(both, "zl")
    feats = (both, swap(both, "core"), over, swap(over, "core"))

    w = jnp.concatenate([w_in, w_out], axis=0).reshape(24, 2, HID).transpose(1, 0, 2)
    w = jnp.broadcast_to(w[None], (16, 2, 24, HID)).reshape(32, 24, HID)
    mine = lax.all_to_all(w, PLANE, split_axis=0, concat_axis=0, tiled=True)
    la, rb = along_x(mine[:16], 1), along_x(mine[16:], -1)
    lb, ra = along_x(mine[16:], 1), along_x(mine[:16], -1)
    fa, fb = along_x(la, 1), along_x(rb, -1)
    halves = [each.reshape(2, 4, 2, 24, HID) for each in (la, lb, ra, rb, fa, fb)]
    weights = [mine.reshape(4, 4, 2, 24, HID)] + halves
    bias = lax.dynamic_slice_in_dim(bias_in, index["yl"] * HID, HID).reshape(1, HID)

    give, keep = tower(place, feats, weights, bias)
    chip = (keep.astype(F32) + swap(give, "core").astype(F32)).astype(BF16)
    parts = lax.all_to_all(chip, ("yl", "zl"), split_axis=0, concat_axis=0, tiled=True)
    columns = norm(parts, bias_out.reshape(1, D_OUT))
    columns = lax.all_to_all(columns, TP, split_axis=0, concat_axis=0, tiled=True)
    columns = columns.reshape(SRC, SHARE)

    owner = item_id // OWN_ROWS
    row = item_id - owner * OWN_ROWS + 1
    order = jnp.arange(SRC, dtype=jnp.int32)
    before = (owner[:, None] == owner[None, :]) & (order[None, :] < order[:, None])
    slot = owner * CAP + jnp.sum(before.astype(jnp.int32), axis=1)
    pick = (jnp.arange(OWNERS * CAP, dtype=jnp.int32)[:, None] == slot[None, :]).astype(BF16)
    lane = jnp.arange(META, dtype=jnp.int32)[None, :]
    meta = jnp.where(
        lane == 0,
        (row >> 6)[:, None],
        jnp.where(lane == 1, (row & 63)[:, None], (lane == 2).astype(jnp.int32)),
    ).astype(BF16)
    payload = jnp.concatenate([columns, meta], axis=1)
    packed = jnp.dot(pick, payload, preferred_element_type=F32).astype(BF16)
    arrived = lax.all_to_all(
        packed.reshape(OWNERS, CAP, SHARE + META), SHARD, split_axis=0, concat_axis=0, tiled=True
    )
    return write(item_table, arrived.reshape(OWNERS * CAP, SHARE + META))


def solution(mesh):
    cut = Mesh(mesh.devices.reshape(SIZES), AXES)
    in_specs = (
        P(SHARD, TP),
        P(SHARD),
        P(SHARD, TP),
        P(TP),
        P(SHARD, TP),
        P(),
        P(SHARD, TP),
    )
    return jax.shard_map(
        local, mesh=cut, in_specs=in_specs, out_specs=P(SHARD, TP), check_vma=False
    )
```

time: 167 us -> 152 us (0.910)
  blocking collectives: 72.7 us -> 32 us
  starting transfers between devices: 29.5 us -> 60.7 us
  between operations: 13.6 us -> 0.29 us
  waiting for transfers between devices: 32 us -> 42.7 us
  local copies, waits for them, and re-layouts: 5.42 us -> 3.75 us
    all_to_all x1 -> x0, blocking collectives: 40.8 us -> none  [local(): mine = lax.all_to_all(w, PLANE, split_axis=0, concat_axis=0, tiled=True)]
    ppermute x0 -> x5, waiting for transfers between devices: none -> 22.1 us  [swap(): return lax.ppermute(block, axis, [(0, 1), (1, 0)])]
    ppermute x0 -> x5, starting transfers between devices: none -> 16.6 us  [swap(): return lax.ppermute(block, axis, [(0, 1), (1, 0)])]
    all_to_all x1 -> x2, starting transfers between devices: 12.4 us -> 20.1 us  [the longest x1 16.6 us: local(): mine = lax.all_to_all(w, PLANE, split_axis=0, concat_axis=0, tiled=True)]
    all_to_all x1 -> x2, waiting for transfers between devices: 13.3 us -> 6.83 us  [the longest x1 6.83 us: local(): lax.all_to_all(chip, ('yl', 'zl'), split_axis=0, concat_axis=0, tiled=True)]
    ppermute x4 -> x6, starting transfers between devices: 13 us -> 19.5 us  [along_x(): return lax.ppermute(block, 'x', [(i, (i + step) % 4) for i in range(4)])]
    ppermute x4 -> x6, waiting for transfers between devices: 14.4 us -> 10.3 us  [along_x(): return lax.ppermute(block, 'x', [(i, (i + step) % 4) for i in range(4)])]
    pallas_call x1 -> x2, Pallas kernels: 4.6 us -> 4.45 us  [the longest x1 3.62 us: tower(): pl.pallas_call(tower_kernel, out_shape=(part, part), in_specs=[SMEM] + [V...]
  transfers between devices with their start and end apart: 7 -> 14, of which waited for: 5 -> 8; matrix products, arithmetic and copies ran while one was open for 2% -> 1% of each run, Pallas kernels for 0% -> 0%
where the time goes in v2:
time: 152 us; the launch traced here: 151 us
  starting transfers between devices  60.7 us (40%)
  waiting for transfers between devices  42.7 us (28%)
  blocking collectives  32 us (21%)
  Pallas kernels  9.03 us (6%)
  local copies, waits for them, and re-layouts  3.75 us (2%)
  other arithmetic  2.24 us (1%)
    all_to_all x1, blocking collectives, local(): lax.all_to_all(packed.reshape(OWNERS, CAP, SHARE + META), SHARD, split_ax...  32 us
    ppermute x5, waiting for transfers between devices, swap(): return lax.ppermute(block, axis, [(0, 1), (1, 0)])  22.1 us
    ppermute x6, starting transfers between devices, along_x(): return lax.ppermute(block, 'x', [(i, (i + step) % 4) for i in range(4)])  19.5 us
    all_to_all x1, starting transfers between devices, local(): mine = lax.all_to_all(w, PLANE, split_axis=0, concat_axis=0, tiled=True)  16.6 us
    ppermute x5, starting transfers between devices, swap(): return lax.ppermute(block, axis, [(0, 1), (1, 0)])  16.6 us
    ppermute x6, waiting for transfers between devices, along_x(): return lax.ppermute(block, 'x', [(i, (i + step) % 4) for i in range(4)])  10.3 us
    all_to_all x1, waiting for transfers between devices, local(): lax.all_to_all(chip, ('yl', 'zl'), split_axis=0, concat_axis=0, tiled=True)  6.83 us
    pallas_call x1, Pallas kernels, write(): pl.pallas_call(write_kernel, out_shape=jax.ShapeDtypeStruct(table.shape,...  4.58 us
  transfers between devices with their start and end apart: 14, of which 8 were waited for; matrix products, arithmetic and copies ran while one was open for 1% of the time, Pallas kernels for 0%

profile of v2, /device:TPU:1, one launch (start us, length us, event | category | flops | bytes accessed | tf_op | source)
XLA Modules:
  0.0 151.0 jit_solution(4582410390703668436)
XLA Ops:
  0.0 0.8 pad_maximum_fusion.1
  0.8 1.0 broadcast_in_dim.36
  1.8 0.0 copy-start.3
  1.8 16.6 %all-to-all-start = ((bf16[32,24,512]{2,1,0:T(8,128)(2,1)}), bf16[32,24,512]{2,1,0:T(8,128)(2,1)S(1)}, u32[]{:S(2)}, u32[]{:S(2)}) async-start(bf16[32,24,512]{2,1,0:T(8,128)(2,1)} %bitcast.7), calls=%async_computation | async-start | bytes 1572864 | tf_op jit(solution)/shard_map/all_to_all | solution.py:173
  18.4 0.0 copy-done.3
  18.4 3.1 %collective-permute-start = (bf16[256,512]{1,0:T(8,128)(2,1)S(1)}, bf16[256,512]{1,0:T(8,128)(2,1)S(1)}, u32[]{:S(2)}, u32[]{:S(2)}) collective-permute-start(bf16[256,512]{1,0:T(8,128)(2,1)S(1)} %copy-done.3), channel_id=1, source_target_pairs={{0,4},{4,0},{1,5},{5,1},{2,6},{6,2},{3,7},{7,3},{8,12},{12,8},{9,1... | collective-permute-start | bytes 786440 | tf_op jit(solution)/shard_map/ppermute | solution.py:160
  21.6 20.6 %collective-permute-done = bf16[256,512]{1,0:T(8,128)(2,1)S(1)} collective-permute-done((bf16[256,512]{1,0:T(8,128)(2,1)S(1)}, bf16[256,512]{1,0:T(8,128)(2,1)S(1)}, u32[]{:S(2)}, u32[]{:S(2)}) %collective-permute-start) | collective-permute-done | bytes 262176 | tf_op jit(solution)/shard_map/ppermute | solution.py:160
  42.2 0.1 pad_maximum_fusion.f0
  42.2 3.1 %collective-permute-start.2 = (bf16[2,256,512]{2,1,0:T(8,128)(2,1)S(1)}, bf16[2,256,512]{2,1,0:T(8,128)(2,1)S(1)}, u32[]{:S(2)}, u32[]{:S(2)}) collective-permute-start(bf16[2,256,512]{2,1,0:T(8,128)(2,1)S(1)} %pad_maximum_fusion.f0), channel_id=1, source_target_pairs={{0,2},{2,0},{1,3},{3,1},{4,6},{6,4},{5,7},{7,5},{8,10},{10,8},{9,1... | collective-permute-start | bytes 1572872 | tf_op jit(solution)/shard_map/ppermute | solution.py:160
  45.3 3.9 %collective-permute-start.1 = (bf16[2,256,512]{2,1,0:T(8,128)(2,1)S(1)}, bf16[2,256,512]{2,1,0:T(8,128)(2,1)S(1)}, u32[]{:S(2)}, u32[]{:S(2)}) collective-permute-start(bf16[2,256,512]{2,1,0:T(8,128)(2,1)S(1)} %pad_maximum_fusion.f0), channel_id=1, source_target_pairs={{0,1},{1,0},{2,3},{3,2},{4,5},{5,4},{6,7},{7,6},{8,9},{9,8},{10,11... | collective-permute-start | bytes 1572872 | tf_op jit(solution)/shard_map/ppermute | solution.py:160
  49.2 0.0 all-to-all-done
  49.2 0.0 copy-start.2
  49.3 1.0 fusion.6
  50.2 0.1 copy-done.2
  50.4 3.1 %collective-permute-start.4 = (bf16[16,24,512]{2,1,0:T(8,128)(2,1)}, bf16[16,24,512]{2,1,0:T(8,128)(2,1)S(1)}, u32[]{:S(2)}, u32[]{:S(2)}) collective-permute-start(bf16[16,24,512]{2,1,0:T(8,128)(2,1)} %get-tuple-element.12), channel_id=1, source_target_pairs={{0,32},{32,64},{64,96},{96,0},{1,33},{33,65},{65,97},{97,1},{2,34}... | collective-permute-start | bytes 1179656 | tf_op jit(solution)/shard_map/ppermute | solution.py:156
  53.5 3.4 %collective-permute-start.7 = (bf16[16,24,512]{2,1,0:T(8,128)(2,1)}, bf16[16,24,512]{2,1,0:T(8,128)(2,1)S(1)}, u32[]{:S(2)}, u32[]{:S(2)}) collective-permute-start(bf16[16,24,512]{2,1,0:T(8,128)(2,1)} %get-tuple-element.11), channel_id=1, source_target_pairs={{0,96},{32,0},{64,32},{96,64},{1,97},{33,1},{65,33},{97,65},{2,98}... | collective-permute-start | bytes 1179656 | tf_op jit(solution)/shard_map/ppermute | solution.py:156
  56.9 0.0 collective-permute-done.2.f2
  56.9 3.5 %collective-permute-start.3 = (bf16[2,256,512]{2,1,0:T(8,128)(2,1)S(1)}, bf16[2,256,512]{2,1,0:T(8,128)(2,1)S(1)}, u32[]{:S(2)}, u32[]{:S(2)}) collective-permute-start(bf16[2,256,512]{2,1,0:T(8,128)(2,1)S(1)} %collective-permute-done.2.f2), channel_id=1, source_target_pairs={{0,1},{1,0},{2,3},{3,2},{4,5},{5,4},{6,7},{7,6},{8,9},{9,8},{10,11... | collective-permute-start | bytes 1572872 | tf_op jit(solution)/shard_map/ppermute | solution.py:160
  60.3 3.1 %collective-permute-start.5 = (bf16[16,24,512]{2,1,0:T(8,128)(2,1)}, bf16[16,24,512]{2,1,0:T(8,128)(2,1)S(1)}, u32[]{:S(2)}, u32[]{:S(2)}) collective-permute-start(bf16[16,24,512]{2,1,0:T(8,128)(2,1)} %get-tuple-element.11), channel_id=1, source_target_pairs={{0,32},{32,64},{64,96},{96,0},{1,33},{33,65},{65,97},{97,1},{2,34}... | collective-permute-start | bytes 1179656 | tf_op jit(solution)/shard_map/ppermute | solution.py:156
  63.5 0.0 collective-permute-done.1.f1
  63.5 3.4 %collective-permute-start.6 = (bf16[16,24,512]{2,1,0:T(8,128)(2,1)}, bf16[16,24,512]{2,1,0:T(8,128)(2,1)}, u32[]{:S(2)}, u32[]{:S(2)}) collective-permute-start(bf16[16,24,512]{2,1,0:T(8,128)(2,1)} %get-tuple-element.12), channel_id=1, source_target_pairs={{0,96},{32,0},{64,32},{96,64},{1,97},{33,1},{65,33},{97,65},{2,98}... | collective-permute-start | bytes 1179656 | tf_op jit(solution)/shard_map/ppermute | solution.py:156
  66.9 0.0 collective-permute-done.4
  66.9 1.9 %collective-permute-start.8 = (bf16[16,24,512]{2,1,0:T(8,128)(2,1)S(1)}, bf16[16,24,512]{2,1,0:T(8,128)(2,1)}, u32[]{:S(2)}, u32[]{:S(2)}) collective-permute-start(bf16[16,24,512]{2,1,0:T(8,128)(2,1)S(1)} %collective-permute-done.4), channel_id=1, source_target_pairs={{0,32},{32,64},{64,96},{96,0},{1,33},{33,65},{65,97},{97,1},{2,34}... | collective-permute-start | bytes 1179656 | tf_op jit(solution)/shard_map/ppermute | solution.py:156
  68.8 0.0 collective-permute-done.7
  68.8 4.6 %collective-permute-start.9 = (bf16[16,24,512]{2,1,0:T(8,128)(2,1)S(1)}, bf16[16,24,512]{2,1,0:T(8,128)(2,1)}, u32[]{:S(2)}, u32[]{:S(2)}) collective-permute-start(bf16[16,24,512]{2,1,0:T(8,128)(2,1)S(1)} %collective-permute-done.7), channel_id=1, source_target_pairs={{0,96},{32,0},{64,32},{96,64},{1,97},{33,1},{65,33},{97,65},{2,98}... | collective-permute-start | bytes 1179656 | tf_op jit(solution)/shard_map/ppermute | solution.py:156
  73.4 0.0 copy-start.5
  73.4 0.7 copy-done.5
  74.1 0.1 dynamic_slice.3
  74.2 0.1 pad_add_fusion.place_ref
  74.2 0.0 collective-permute-done.3.f3
  74.3 0.1 collective-permute-done.5
  74.4 1.7 %collective-permute-done.6 = bf16[16,24,512]{2,1,0:T(8,128)(2,1)} collective-permute-done((bf16[16,24,512]{2,1,0:T(8,128)(2,1)}, bf16[16,24,512]{2,1,0:T(8,128)(2,1)}, u32[]{:S(2)}, u32[]{:S(2)}) %collective-permute-start.6) | collective-permute-done | bytes 393248 | tf_op jit(solution)/shard_map/ppermute | solution.py:156
  76.1 6.8 %collective-permute-done.8 = bf16[16,24,512]{2,1,0:T(8,128)(2,1)} collective-permute-done((bf16[16,24,512]{2,1,0:T(8,128)(2,1)S(1)}, bf16[16,24,512]{2,1,0:T(8,128)(2,1)}, u32[]{:S(2)}, u32[]{:S(2)}) %collective-permute-start.8) | collective-permute-done | bytes 393248 | tf_op jit(solution)/shard_map/ppermute | solution.py:156
  82.9 1.6 %collective-permute-done.9 = bf16[16,24,512]{2,1,0:T(8,128)(2,1)} collective-permute-done((bf16[16,24,512]{2,1,0:T(8,128)(2,1)S(1)}, bf16[16,24,512]{2,1,0:T(8,128)(2,1)}, u32[]{:S(2)}, u32[]{:S(2)}) %collective-permute-start.9) | collective-permute-done | bytes 393248 | tf_op jit(solution)/shard_map/ppermute | solution.py:156
  84.5 3.6 %tower.1 = (bf16[4,64,1024]{2,1,0:T(8,128)(2,1)S(1)}, bf16[4,64,1024]{2,1,0:T(8,128)(2,1)S(1)}) custom-call(s32[4]{0:T(128)S(1)} %pad_add_fusion.place_ref, bf16[2,256,512]{2,1,0:T(8,128)(2,1)S(1)} %pad_maximum_fusion.f0, bf16[2,256,512]{2,1,0:T(8,128)(2,1)S(1)} %collective-permute-done.1.f1, bf16[2,256,512]{2,1,0:T(8,128)(2,1)S(1)} %collective-permute-done.2.f2, ...), custom_call_target="tpu_custom_call" | custom-call | tf_op jit(solution)/shard_map/tower/pallas_call | solution.py:88
  88.2 3.0 %collective-permute-start.10 = (bf16[4,64,1024]{2,1,0:T(8,128)(2,1)S(1)}, bf16[4,64,1024]{2,1,0:T(8,128)(2,1)S(1)}, u32[]{:S(2)}, u32[]{:S(2)}) collective-permute-start(bf16[4,64,1024]{2,1,0:T(8,128)(2,1)S(1)} %get-tuple-element.8), channel_id=1, source_target_pairs={{0,1},{1,0},{2,3},{3,2},{4,5},{5,4},{6,7},{7,6},{8,9},{9,8},{10,11... | collective-permute-start | bytes 1572872 | tf_op jit(solution)/shard_map/ppermute | solution.py:160
  91.2 1.5 %collective-permute-done.10 = bf16[4,64,1024]{2,1,0:T(8,128)(2,1)S(1)} collective-permute-done((bf16[4,64,1024]{2,1,0:T(8,128)(2,1)S(1)}, bf16[4,64,1024]{2,1,0:T(8,128)(2,1)S(1)}, u32[]{:S(2)}, u32[]{:S(2)}) %collective-permute-start.10) | collective-permute-done | bytes 524320 | tf_op jit(solution)/shard_map/ppermute | solution.py:160
  92.7 1.0 add_convert_fusion
  93.7 3.5 %all-to-all-start.1 = ((bf16[4,64,1024]{2,1,0:T(8,128)(2,1)}), bf16[4,64,1024]{2,1,0:T(8,128)(2,1)S(1)}, u32[]{:S(2)}, u32[]{:S(2)}) async-start(bf16[4,64,1024]{2,1,0:T(8,128)(2,1)} %add_convert_fusion), calls=%async_computation.1 | async-start | bytes 1048576 | tf_op jit(solution)/shard_map/all_to_all | solution.py:183
  97.2 0.0 copy-start.4
  97.2 0.7 copy-done.4
  97.9 0.2 convert_reduce_fusion
  98.1 0.0 copy-start.1
  98.1 6.8 %all-to-all-done.1.parts_ref = bf16[4,64,1024]{2,1,0:T(8,128)(2,1)S(1)} async-done(((bf16[4,64,1024]{2,1,0:T(8,128)(2,1)}), bf16[4,64,1024]{2,1,0:T(8,128)(2,1)S(1)}, u32[]{:S(2)}, u32[]{:S(2)}) %all-to-all-start.1) | async-done | bytes 524320 | tf_op jit(solution)/shard_map/all_to_all | solution.py:183
  104.9 0.0 copy-done.1
  104.9 0.8 norm.1
  105.8 4.5 %all-to-all-start.2 = ((bf16[4,64,256]{2,1,0:T(8,128)(2,1)}), bf16[4,64,256]{2,1,0:T(8,128)(2,1)S(1)}, u32[]{:S(2)}, u32[]{:S(2)}) async-start(bf16[4,64,256]{2,1,0:T(8,128)(2,1)} %norm.1), calls=%async_computation.2 | async-start | bytes 262144 | tf_op jit(solution)/shard_map/all_to_all | solution.py:185
  110.2 0.1 select_convert_fusion
  110.4 3.5 %all-to-all-done.2 = bf16[4,64,256]{2,1,0:T(8,128)(2,1)S(1)} async-done(((bf16[4,64,256]{2,1,0:T(8,128)(2,1)}), bf16[4,64,256]{2,1,0:T(8,128)(2,1)S(1)}, u32[]{:S(2)}, u32[]{:S(2)}) %all-to-all-start.2) | async-done | bytes 131104 | tf_op jit(solution)/shard_map/all_to_all | solution.py:185
  113.8 0.3 convolution_convert_fusion
  114.2 0.0 copy-start
  114.2 0.1 reshape.77
  114.3 32.0 %all_to_all.20 = bf16[128,4,384]{2,1,0:T(4,128)(2,1)S(1)} all-to-all(bf16[128,4,384]{2,1,0:T(4,128)(2,1)S(1)} %reshape.77), channel_id=1, replica_groups=mesh['zh'=4,'x'=4,'yh'=4,'yl'=2,'zl'=2,'core'=2] {'zh','x','yh','yl'}, dimensions={0} | all-to-all | bytes 786432 | tf_op jit(solution)/shard_map/all_to_all | solution.py:202
  146.3 0.1 reshape.78.rows_ref
  146.4 0.0 copy-done
  146.4 4.6 %write.1 = bf16[2048,256]{1,0:T(8,128)(2,1)} custom-call(bf16[2048,256]{1,0:T(8,128)(2,1)S(1)} %copy-done, bf16[512,384]{1,0:T(8,128)(2,1)S(1)} %reshape.78.rows_ref), custom_call_target="tpu_custom_call" | custom-call | tf_op jit(solution)/shard_map/write/pallas_call | solution.py:143
  (6 shorter events, 0.1 us)
Async XLA Ops:
  1.8 16.6 %copy-start.3 = (bf16[256,512]{1,0:T(8,128)(2,1)S(1)}, bf16[256,512]{1,0:T(8,128)(2,1)}, u32[]{:S(2)}) copy-start(bf16[256,512]{1,0:T(8,128)(2,1)} %param.7) | copy-start | bytes 786436
  1.8 47.4 %all-to-all-start = ((bf16[32,24,512]{2,1,0:T(8,128)(2,1)}), bf16[32,24,512]{2,1,0:T(8,128)(2,1)S(1)}, u32[]{:S(2)}, u32[]{:S(2)}) async-start(bf16[32,24,512]{2,1,0:T(8,128)(2,1)} %bitcast.7), calls=%async_computation | async-start | bytes 1572864 | tf_op jit(solution)/shard_map/all_to_all | solution.py:173
  18.4 23.7 %collective-permute-start = (bf16[256,512]{1,0:T(8,128)(2,1)S(1)}, bf16[256,512]{1,0:T(8,128)(2,1)S(1)}, u32[]{:S(2)}, u32[]{:S(2)}) collective-permute-start(bf16[256,512]{1,0:T(8,128)(2,1)S(1)} %copy-done.3), channel_id=1, source_target_pairs={{0,4},{4,0},{1,5},{5,1},{2,6},{6,2},{3,7},{7,3},{8,12},{12,8},{9,1... | collective-permute-start | bytes 786440 | tf_op jit(solution)/shard_map/ppermute | solution.py:160
  42.2 14.7 %collective-permute-start.2 = (bf16[2,256,512]{2,1,0:T(8,128)(2,1)S(1)}, bf16[2,256,512]{2,1,0:T(8,128)(2,1)S(1)}, u32[]{:S(2)}, u32[]{:S(2)}) collective-permute-start(bf16[2,256,512]{2,1,0:T(8,128)(2,1)S(1)} %pad_maximum_fusion.f0), channel_id=1, source_target_pairs={{0,2},{2,0},{1,3},{3,1},{4,6},{6,4},{5,7},{7,5},{8,10},{10,8},{9,1... | collective-permute-start | bytes 1572872 | tf_op jit(solution)/shard_map/ppermute | solution.py:160
  45.3 18.2 %collective-permute-start.1 = (bf16[2,256,512]{2,1,0:T(8,128)(2,1)S(1)}, bf16[2,256,512]{2,1,0:T(8,128)(2,1)S(1)}, u32[]{:S(2)}, u32[]{:S(2)}) collective-permute-start(bf16[2,256,512]{2,1,0:T(8,128)(2,1)S(1)} %pad_maximum_fusion.f0), channel_id=1, source_target_pairs={{0,1},{1,0},{2,3},{3,2},{4,5},{5,4},{6,7},{7,6},{8,9},{9,8},{10,11... | collective-permute-start | bytes 1572872 | tf_op jit(solution)/shard_map/ppermute | solution.py:160
  49.2 1.1 copy-start.2
  50.4 16.5 %collective-permute-start.4 = (bf16[16,24,512]{2,1,0:T(8,128)(2,1)}, bf16[16,24,512]{2,1,0:T(8,128)(2,1)S(1)}, u32[]{:S(2)}, u32[]{:S(2)}) collective-permute-start(bf16[16,24,512]{2,1,0:T(8,128)(2,1)} %get-tuple-element.12), channel_id=1, source_target_pairs={{0,32},{32,64},{64,96},{96,0},{1,33},{33,65},{65,97},{97,1},{2,34}... | collective-permute-start | bytes 1179656 | tf_op jit(solution)/shard_map/ppermute | solution.py:156
  53.5 15.3 %collective-permute-start.7 = (bf16[16,24,512]{2,1,0:T(8,128)(2,1)}, bf16[16,24,512]{2,1,0:T(8,128)(2,1)S(1)}, u32[]{:S(2)}, u32[]{:S(2)}) collective-permute-start(bf16[16,24,512]{2,1,0:T(8,128)(2,1)} %get-tuple-element.11), channel_id=1, source_target_pairs={{0,96},{32,0},{64,32},{96,64},{1,97},{33,1},{65,33},{97,65},{2,98}... | collective-permute-start | bytes 1179656 | tf_op jit(solution)/shard_map/ppermute | solution.py:156
  56.9 17.4 %collective-permute-start.3 = (bf16[2,256,512]{2,1,0:T(8,128)(2,1)S(1)}, bf16[2,256,512]{2,1,0:T(8,128)(2,1)S(1)}, u32[]{:S(2)}, u32[]{:S(2)}) collective-permute-start(bf16[2,256,512]{2,1,0:T(8,128)(2,1)S(1)} %collective-permute-done.2.f2), channel_id=1, source_target_pairs={{0,1},{1,0},{2,3},{3,2},{4,5},{5,4},{6,7},{7,6},{8,9},{9,8},{10,11... | collective-permute-start | bytes 1572872 | tf_op jit(solution)/shard_map/ppermute | solution.py:160
  60.3 14.0 %collective-permute-start.5 = (bf16[16,24,512]{2,1,0:T(8,128)(2,1)}, bf16[16,24,512]{2,1,0:T(8,128)(2,1)S(1)}, u32[]{:S(2)}, u32[]{:S(2)}) collective-permute-start(bf16[16,24,512]{2,1,0:T(8,128)(2,1)} %get-tuple-element.11), channel_id=1, source_target_pairs={{0,32},{32,64},{64,96},{96,0},{1,33},{33,65},{65,97},{97,1},{2,34}... | collective-permute-start | bytes 1179656 | tf_op jit(solution)/shard_map/ppermute | solution.py:156
  63.5 12.6 %collective-permute-start.6 = (bf16[16,24,512]{2,1,0:T(8,128)(2,1)}, bf16[16,24,512]{2,1,0:T(8,128)(2,1)}, u32[]{:S(2)}, u32[]{:S(2)}) collective-permute-start(bf16[16,24,512]{2,1,0:T(8,128)(2,1)} %get-tuple-element.12), channel_id=1, source_target_pairs={{0,96},{32,0},{64,32},{96,64},{1,97},{33,1},{65,33},{97,65},{2,98}... | collective-permute-start | bytes 1179656 | tf_op jit(solution)/shard_map/ppermute | solution.py:156
  66.9 16.1 %collective-permute-start.8 = (bf16[16,24,512]{2,1,0:T(8,128)(2,1)S(1)}, bf16[16,24,512]{2,1,0:T(8,128)(2,1)}, u32[]{:S(2)}, u32[]{:S(2)}) collective-permute-start(bf16[16,24,512]{2,1,0:T(8,128)(2,1)S(1)} %collective-permute-done.4), channel_id=1, source_target_pairs={{0,32},{32,64},{64,96},{96,0},{1,33},{33,65},{65,97},{97,1},{2,34}... | collective-permute-start | bytes 1179656 | tf_op jit(solution)/shard_map/ppermute | solution.py:156
  68.8 15.7 %collective-permute-start.9 = (bf16[16,24,512]{2,1,0:T(8,128)(2,1)S(1)}, bf16[16,24,512]{2,1,0:T(8,128)(2,1)}, u32[]{:S(2)}, u32[]{:S(2)}) collective-permute-start(bf16[16,24,512]{2,1,0:T(8,128)(2,1)S(1)} %collective-permute-done.7), channel_id=1, source_target_pairs={{0,96},{32,0},{64,32},{96,64},{1,97},{33,1},{65,33},{97,65},{2,98}... | collective-permute-start | bytes 1179656 | tf_op jit(solution)/shard_map/ppermute | solution.py:156
  73.4 0.7 copy-start.5
  88.2 4.5 %collective-permute-start.10 = (bf16[4,64,1024]{2,1,0:T(8,128)(2,1)S(1)}, bf16[4,64,1024]{2,1,0:T(8,128)(2,1)S(1)}, u32[]{:S(2)}, u32[]{:S(2)}) collective-permute-start(bf16[4,64,1024]{2,1,0:T(8,128)(2,1)S(1)} %get-tuple-element.8), channel_id=1, source_target_pairs={{0,1},{1,0},{2,3},{3,2},{4,5},{5,4},{6,7},{7,6},{8,9},{9,8},{10,11... | collective-permute-start | bytes 1572872 | tf_op jit(solution)/shard_map/ppermute | solution.py:160
  93.7 11.2 %all-to-all-start.1 = ((bf16[4,64,1024]{2,1,0:T(8,128)(2,1)}), bf16[4,64,1024]{2,1,0:T(8,128)(2,1)S(1)}, u32[]{:S(2)}, u32[]{:S(2)}) async-start(bf16[4,64,1024]{2,1,0:T(8,128)(2,1)} %add_convert_fusion), calls=%async_computation.1 | async-start | bytes 1048576 | tf_op jit(solution)/shard_map/all_to_all | solution.py:183
  97.2 0.7 copy-start.4
  98.1 6.9 %copy-start.1 = (f32[1024]{0:T(1024)S(1)}, f32[1024]{0:T(1024)}, u32[]{:S(2)}) copy-start(f32[1024]{0:T(1024)} %param.12) | copy-start | bytes 12292
  105.8 8.1 %all-to-all-start.2 = ((bf16[4,64,256]{2,1,0:T(8,128)(2,1)}), bf16[4,64,256]{2,1,0:T(8,128)(2,1)S(1)}, u32[]{:S(2)}, u32[]{:S(2)}) async-start(bf16[4,64,256]{2,1,0:T(8,128)(2,1)} %norm.1), calls=%async_computation.2 | async-start | bytes 262144 | tf_op jit(solution)/shard_map/all_to_all | solution.py:185
  114.2 32.2 %copy-start = (bf16[2048,256]{1,0:T(8,128)(2,1)S(1)}, bf16[2048,256]{1,0:T(8,128)(2,1)}, u32[]{:S(2)}) copy-start(bf16[2048,256]{1,0:T(8,128)(2,1)} %table_ref.1) | copy-start | bytes 3145732

commit v3 on v2

--- a/solution.py
+++ b/solution.py
@@ -25,11 +25,31 @@
 SMEM = pl.BlockSpec(memory_space=pltpu.SMEM)
 
 
+def pieces_kernel(w_in_ref, w_out_ref, out_ref):
+    for yl in range(2):
+        cut = pl.ds(yl * HID, HID)
+        rows = jnp.concatenate([w_in_ref[:, cut].astype(F32), w_out_ref[:, cut].astype(F32)], axis=0)
+        for i in range(16):
+            out_ref[i * 2 + yl] = rows.astype(BF16)
+
+
+def pieces(w_in, w_out):
+    return pl.pallas_call(
+        pieces_kernel,
+        out_shape=jax.ShapeDtypeStruct((32, 24, HID), BF16),
+        in_specs=[VMEM, VMEM],
+        out_specs=VMEM,
+        cost_estimate=pl.CostEstimate(flops=0, bytes_accessed=64 << 20, transcendentals=0),
+        compiler_params=pltpu.CompilerParams(vmem_limit_bytes=16 << 20),
+        name="pieces",
+    )(w_in, w_out)
+
+
 def tower_kernel(
-    place_ref, f0, f1, f2, f3, mine, la, lb, ra, rb, fa, fb, bias_ref, give_ref, keep_ref, w_all, hid
+    place_ref, near, far, mine, la, lb, ra, rb, fa, fb, bias_ref, give_ref, keep_ref, w_all, hid
 ):
     x0, tp, yl, core = (place_ref[i] for i in range(4))
-    feats = (f0, f1, f2, f3)
+    feats = (near, far)
     blocks = (
         (0, mine.at[0:2], mine.at[2:4]),
         (3, la, lb),
@@ -40,18 +60,18 @@
     for offset, first, second in blocks:
         xk = lax.rem(x0 + offset, 4)
         col = pl.multiple_of(xk * 128, 128)
-        for pair in ((0, 1), (2, 3)):
+        for dz in range(2):
             weights = jnp.concatenate(
                 [
-                    half[:, jnp.bitwise_xor(tp, d), :, 0:16, :].reshape(64, HID)
-                    for d in pair
+                    half[:, jnp.bitwise_xor(tp, dz * 2 + dc), :, 0:16, :].reshape(64, HID)
+                    for dc in range(2)
                     for half in (first, second)
                 ],
                 axis=0,
             )
             for dy in range(2):
                 columns = jnp.concatenate(
-                    [feats[d][dy, :, pl.ds(col, 128)] for d in pair], axis=1
+                    [feats[dz][dy, dc, :, pl.ds(col, 128)] for dc in range(2)], axis=1
                 )
                 term = jnp.dot(columns, weights, preferred_element_type=F32)
                 act[dy] = term if act[dy] is None else act[dy] + term
@@ -88,7 +108,7 @@
     return pl.pallas_call(
         tower_kernel,
         out_shape=(part, part),
-        in_specs=[SMEM] + [VMEM] * 12,
+        in_specs=[SMEM] + [VMEM] * 10,
         out_specs=(VMEM, VMEM),
         scratch_shapes=[pltpu.VMEM((D_OUT, HID), BF16), pltpu.VMEM((2, SRC, HID), BF16)],
         compiler_params=pltpu.CompilerParams(vmem_limit_bytes=48 << 20),
@@ -129,16 +149,14 @@
         )
 
     row = lax.broadcasted_iota(jnp.int32, (block, 1), 0) + (pl.program_id(0) * block + 1)
-    here = row.astype(F32) == target_ref[0:1, :]
-    moved = jnp.dot(
-        jnp.where(here, 1.0, 0.0).astype(BF16), rows_ref[...], preferred_element_type=F32
-    )
-    hit = moved[:, SHARE + 2 : SHARE + 3] > 0.5
-    out_ref[...] = jnp.where(hit, moved[:, :SHARE], table_ref[...].astype(F32)).astype(BF16)
+    here = jnp.where(row.astype(F32) == target_ref[0:1, :], 1.0, 0.0)
+    moved = jnp.dot(here.astype(BF16), rows_ref[:, :SHARE], preferred_element_type=F32)
+    hit = jnp.max(here, axis=1, keepdims=True) > 0.5
+    out_ref[...] = jnp.where(hit, moved, table_ref[...].astype(F32)).astype(BF16)
 
 
 def write(table, rows):
-    block = 256
+    block = 512
     spec = pl.BlockSpec((block, SHARE), lambda i: (i, 0))
     return pl.pallas_call(
         write_kernel,
@@ -164,16 +182,17 @@
     index = {axis: lax.axis_index(axis).astype(jnp.int32) for axis in AXES}
     place = jnp.stack([index["x"], index["zl"] * 2 + index["core"], index["yl"], index["core"]])
 
-    both = jnp.stack([features, swap(features, "yl")])
-    over = swap(both, "zl")
-    feats = (both, swap(both, "core"), over, swap(over, "core"))
-
-    w = jnp.concatenate([w_in, w_out], axis=0).reshape(24, 2, HID).transpose(1, 0, 2)
-    w = jnp.broadcast_to(w[None], (16, 2, 24, HID)).reshape(32, 24, HID)
+    w = pieces(w_in, w_out)
     mine = lax.all_to_all(w, PLANE, split_axis=0, concat_axis=0, tiled=True)
+    pair = jnp.stack([features, swap(features, "core")])
+    mine, near = lax.optimization_barrier((mine, swap(pair, "yl")))
     la, rb = along_x(mine[:16], 1), along_x(mine[16:], -1)
     lb, ra = along_x(mine[16:], 1), along_x(mine[:16], -1)
     fa, fb = along_x(la, 1), along_x(rb, -1)
+
+    near = jnp.stack([pair, near])
+    feats = (near, swap(near, "zl"))
+
     halves = [each.reshape(2, 4, 2, 24, HID) for each in (la, lb, ra, rb, fa, fb)]
     weights = [mine.reshape(4, 4, 2, 24, HID)] + halves
     bias = lax.dynamic_slice_in_dim(bias_in, index["yl"] * HID, HID).reshape(1, HID)
@@ -195,7 +214,7 @@
     meta = jnp.where(
         lane == 0,
         (row >> 6)[:, None],
-        jnp.where(lane == 1, (row & 63)[:, None], (lane == 2).astype(jnp.int32)),
+        jnp.where(lane == 1, (row & 63)[:, None], 0),
     ).astype(BF16)
     payload = jnp.concatenate([columns, meta], axis=1)
     packed = jnp.dot(pick, payload, preferred_element_type=F32).astype(BF16)

time: 152 us -> 151 us (level)
  waiting for transfers between devices: 42.7 us -> 45 us
  starting transfers between devices: 60.7 us -> 58.5 us
    ppermute x5 -> x4, waiting for transfers between devices: 22.1 us -> 24.5 us  [swap(): return lax.ppermute(block, axis, [(0, 1), (1, 0)])]
    ppermute x5 -> x4, starting transfers between devices: 16.6 us -> 14.4 us  [swap(): return lax.ppermute(block, axis, [(0, 1), (1, 0)])]
    pallas_call x1, Pallas kernels: 4.58 us -> 2.74 us  [write(): pl.pallas_call(write_kernel, out_shape=jax.ShapeDtypeStruct(table.shape,...]
  transfers between devices with their start and end apart: 14 -> 13, of which waited for: 8 -> 9; matrix products, arithmetic and copies ran while one was open for 1% -> 1% of each run, Pallas kernels for 0% -> 0%
where the time goes in v3:
time: 151 us; the launch traced here: 150 us
  starting transfers between devices  58.5 us (39%)
  waiting for transfers between devices  45 us (30%)
  blocking collectives  32 us (21%)
  Pallas kernels  8.11 us (5%)
  local copies, waits for them, and re-layouts  4.03 us (3%)
  other arithmetic  1.57 us (1%)
    all_to_all x1, blocking collectives, local(): lax.all_to_all(packed.reshape(OWNERS, CAP, SHARE + META), SHARD, split_ax...  32 us
    ppermute x4, waiting for transfers between devices, swap(): return lax.ppermute(block, axis, [(0, 1), (1, 0)])  24.5 us
    ppermute x6, starting transfers between devices, along_x(): return lax.ppermute(block, 'x', [(i, (i + step) % 4) for i in range(4)])  19.5 us
    all_to_all x1, starting transfers between devices, local(): mine = lax.all_to_all(w, PLANE, split_axis=0, concat_axis=0, tiled=True)  16.6 us
    ppermute x4, starting transfers between devices, swap(): return lax.ppermute(block, axis, [(0, 1), (1, 0)])  14.4 us
    ppermute x6, waiting for transfers between devices, along_x(): return lax.ppermute(block, 'x', [(i, (i + step) % 4) for i in range(4)])  10.2 us
    all_to_all x1, waiting for transfers between devices, local(): lax.all_to_all(chip, ('yl', 'zl'), split_axis=0, concat_axis=0, tiled=True)  6.84 us
    all_to_all x1, starting transfers between devices, local(): lax.all_to_all(columns, TP, split_axis=0, concat_axis=0, tiled=True)  4.49 us
  transfers between devices with their start and end apart: 13, of which 9 were waited for; matrix products, arithmetic and copies ran while one was open for 1% of the time, Pallas kernels for 0%

profile of v3, /device:TPU:1, one launch (start us, length us, event | category | flops | bytes accessed | tf_op | source)
XLA Modules:
  0.0 149.7 jit_solution(11327219054334337689)
XLA Ops:
  0.0 0.0 copy-start.1
  0.0 0.8 copy-done.1
  0.8 0.0 copy-start.2
  0.8 0.7 copy-done.2
  1.5 1.0 pieces.1
  2.4 0.0 copy-start.4
  2.4 16.6 %all-to-all-start = ((bf16[32,24,512]{2,1,0:T(8,128)(2,1)}), bf16[32,24,512]{2,1,0:T(8,128)(2,1)S(1)}, u32[]{:S(2)}, u32[]{:S(2)}) async-start(bf16[32,24,512]{2,1,0:T(8,128)(2,1)} %pieces.1), calls=%async_computation | async-start | bytes 1572864 | tf_op jit(solution)/shard_map/all_to_all | solution.py:186
  19.1 0.0 copy-done.4
  19.1 2.9 %collective-permute-start = (bf16[256,512]{1,0:T(8,128)(2,1)S(1)}, bf16[256,512]{1,0:T(8,128)(2,1)S(1)}, u32[]{:S(2)}, u32[]{:S(2)}) collective-permute-start(bf16[256,512]{1,0:T(8,128)(2,1)S(1)} %copy-done.4), channel_id=1, source_target_pairs={{0,1},{1,0},{2,3},{3,2},{4,5},{5,4},{6,7},{7,6},{8,9},{9,8},{10,11... | collective-permute-start | bytes 786440 | tf_op jit(solution)/shard_map/ppermute | solution.py:178
  22.0 1.1 collective-permute-done
  23.1 0.1 fusion.6
  23.2 3.4 %collective-permute-start.1 = (bf16[2,256,512]{2,1,0:T(8,128)(2,1)S(1)}, bf16[2,256,512]{2,1,0:T(8,128)(2,1)S(1)}, u32[]{:S(2)}, u32[]{:S(2)}) collective-permute-start(bf16[2,256,512]{2,1,0:T(8,128)(2,1)S(1)} %get-tuple-element.18), channel_id=1, source_target_pairs={{0,4},{4,0},{1,5},{5,1},{2,6},{6,2},{3,7},{7,3},{8,12},{12,8},{9,1... | collective-permute-start | bytes 1572872 | tf_op jit(solution)/shard_map/ppermute | solution.py:178
  26.6 21.8 %collective-permute-done.1 = bf16[2,256,512]{2,1,0:T(8,128)(2,1)S(1)} collective-permute-done((bf16[2,256,512]{2,1,0:T(8,128)(2,1)S(1)}, bf16[2,256,512]{2,1,0:T(8,128)(2,1)S(1)}, u32[]{:S(2)}, u32[]{:S(2)}) %collective-permute-start.1) | collective-permute-done | bytes 524320 | tf_op jit(solution)/shard_map/ppermute | solution.py:178
  48.4 0.0 all-to-all-done
  48.4 0.1 pad_maximum_fusion.near
  48.5 3.1 %collective-permute-start.2 = (bf16[2,2,256,512]{3,2,1,0:T(8,128)(2,1)S(1)}, bf16[2,2,256,512]{3,2,1,0:T(8,128)(2,1)}, u32[]{:S(2)}, u32[]{:S(2)}) collective-permute-start(bf16[2,2,256,512]{3,2,1,0:T(8,128)(2,1)S(1)} %pad_maximum_fusion.near), channel_id=1, source_target_pairs={{0,2},{2,0},{1,3},{3,1},{4,6},{6,4},{5,7},{7,5},{8,10},{10,8},{9,1... | collective-permute-start | bytes 3145736 | tf_op jit(solution)/shard_map/ppermute | solution.py:178
  51.6 0.9 fusion.7
  52.6 3.1 %collective-permute-start.3 = (bf16[16,24,512]{2,1,0:T(8,128)(2,1)}, bf16[16,24,512]{2,1,0:T(8,128)(2,1)S(1)}, u32[]{:S(2)}, u32[]{:S(2)}) collective-permute-start(bf16[16,24,512]{2,1,0:T(8,128)(2,1)} %get-tuple-element.16), channel_id=1, source_target_pairs={{0,32},{32,64},{64,96},{96,0},{1,33},{33,65},{65,97},{97,1},{2,34}... | collective-permute-start | bytes 1179656 | tf_op jit(solution)/shard_map/ppermute | solution.py:174
  55.7 3.4 %collective-permute-start.6 = (bf16[16,24,512]{2,1,0:T(8,128)(2,1)}, bf16[16,24,512]{2,1,0:T(8,128)(2,1)S(1)}, u32[]{:S(2)}, u32[]{:S(2)}) collective-permute-start(bf16[16,24,512]{2,1,0:T(8,128)(2,1)} %get-tuple-element.15), channel_id=1, source_target_pairs={{0,96},{32,0},{64,32},{96,64},{1,97},{33,1},{65,33},{97,65},{2,98}... | collective-permute-start | bytes 1179656 | tf_op jit(solution)/shard_map/ppermute | solution.py:174
  59.1 1.9 %collective-permute-start.4 = (bf16[16,24,512]{2,1,0:T(8,128)(2,1)}, bf16[16,24,512]{2,1,0:T(8,128)(2,1)S(1)}, u32[]{:S(2)}, u32[]{:S(2)}) collective-permute-start(bf16[16,24,512]{2,1,0:T(8,128)(2,1)} %get-tuple-element.15), channel_id=1, source_target_pairs={{0,32},{32,64},{64,96},{96,0},{1,33},{33,65},{65,97},{97,1},{2,34}... | collective-permute-start | bytes 1179656 | tf_op jit(solution)/shard_map/ppermute | solution.py:174
  61.0 4.6 %collective-permute-start.5 = (bf16[16,24,512]{2,1,0:T(8,128)(2,1)}, bf16[16,24,512]{2,1,0:T(8,128)(2,1)S(1)}, u32[]{:S(2)}, u32[]{:S(2)}) collective-permute-start(bf16[16,24,512]{2,1,0:T(8,128)(2,1)} %get-tuple-element.16), channel_id=1, source_target_pairs={{0,96},{32,0},{64,32},{96,64},{1,97},{33,1},{65,33},{97,65},{2,98}... | collective-permute-start | bytes 1179656 | tf_op jit(solution)/shard_map/ppermute | solution.py:174
  65.6 0.0 collective-permute-done.3
  65.6 1.9 %collective-permute-start.7 = (bf16[16,24,512]{2,1,0:T(8,128)(2,1)S(1)}, bf16[16,24,512]{2,1,0:T(8,128)(2,1)}, u32[]{:S(2)}, u32[]{:S(2)}) collective-permute-start(bf16[16,24,512]{2,1,0:T(8,128)(2,1)S(1)} %collective-permute-done.3), channel_id=1, source_target_pairs={{0,32},{32,64},{64,96},{96,0},{1,33},{33,65},{65,97},{97,1},{2,34}... | collective-permute-start | bytes 1179656 | tf_op jit(solution)/shard_map/ppermute | solution.py:174
  67.5 0.0 collective-permute-done.6
  67.5 4.6 %collective-permute-start.8 = (bf16[16,24,512]{2,1,0:T(8,128)(2,1)S(1)}, bf16[16,24,512]{2,1,0:T(8,128)(2,1)}, u32[]{:S(2)}, u32[]{:S(2)}) collective-permute-start(bf16[16,24,512]{2,1,0:T(8,128)(2,1)S(1)} %collective-permute-done.6), channel_id=1, source_target_pairs={{0,96},{32,0},{64,32},{96,64},{1,97},{33,1},{65,33},{97,65},{2,98}... | collective-permute-start | bytes 1179656 | tf_op jit(solution)/shard_map/ppermute | solution.py:174
  72.1 0.0 copy-start.6
  72.1 0.7 copy-done.6
  72.8 0.1 dynamic_slice.3
  72.9 0.1 pad_add_fusion.place_ref
  72.9 0.6 collective-permute-done.4
  73.6 1.3 collective-permute-done.5
  74.9 7.2 %collective-permute-done.7 = bf16[16,24,512]{2,1,0:T(8,128)(2,1)} collective-permute-done((bf16[16,24,512]{2,1,0:T(8,128)(2,1)S(1)}, bf16[16,24,512]{2,1,0:T(8,128)(2,1)}, u32[]{:S(2)}, u32[]{:S(2)}) %collective-permute-start.7) | collective-permute-done | bytes 393248 | tf_op jit(solution)/shard_map/ppermute | solution.py:174
  82.1 1.1 collective-permute-done.8
  83.2 0.0 collective-permute-done.2.far
  83.2 3.6 %tower.1 = (bf16[4,64,1024]{2,1,0:T(8,128)(2,1)S(1)}, bf16[4,64,1024]{2,1,0:T(8,128)(2,1)S(1)}) custom-call(s32[4]{0:T(128)S(1)} %pad_add_fusion.place_ref, bf16[2,2,256,512]{3,2,1,0:T(8,128)(2,1)S(1)} %pad_maximum_fusion.near, bf16[2,2,256,512]{3,2,1,0:T(8,128)(2,1)} %collective-permute-done.2.far, bf16[4,4,2,24,512]{4,3,2,1,0:T(8,128)(2,1)S(1)} %bitcast.19, ...), custom_call_target="tpu_custom_call" | custom-call | tf_op jit(solution)/shard_map/tower/pallas_call | solution.py:108
  86.8 5.0 %collective-permute-start.9 = (bf16[4,64,1024]{2,1,0:T(8,128)(2,1)S(1)}, bf16[4,64,1024]{2,1,0:T(8,128)(2,1)S(1)}, u32[]{:S(2)}, u32[]{:S(2)}) collective-permute-start(bf16[4,64,1024]{2,1,0:T(8,128)(2,1)S(1)} %get-tuple-element.12), channel_id=1, source_target_pairs={{0,1},{1,0},{2,3},{3,2},{4,5},{5,4},{6,7},{7,6},{8,9},{9,8},{10,11... | collective-permute-start | bytes 1572872 | tf_op jit(solution)/shard_map/ppermute | solution.py:178
  91.8 1.5 %collective-permute-done.9 = bf16[4,64,1024]{2,1,0:T(8,128)(2,1)S(1)} collective-permute-done((bf16[4,64,1024]{2,1,0:T(8,128)(2,1)S(1)}, bf16[4,64,1024]{2,1,0:T(8,128)(2,1)S(1)}, u32[]{:S(2)}, u32[]{:S(2)}) %collective-permute-start.9) | collective-permute-done | bytes 524320 | tf_op jit(solution)/shard_map/ppermute | solution.py:178
  93.3 1.0 add_convert_fusion
  94.3 3.5 %all-to-all-start.1 = ((bf16[4,64,1024]{2,1,0:T(8,128)(2,1)}), bf16[4,64,1024]{2,1,0:T(8,128)(2,1)S(1)}, u32[]{:S(2)}, u32[]{:S(2)}) async-start(bf16[4,64,1024]{2,1,0:T(8,128)(2,1)} %add_convert_fusion), calls=%async_computation.1 | async-start | bytes 1048576 | tf_op jit(solution)/shard_map/all_to_all | solution.py:202
  97.8 0.0 copy-start.5
  97.8 0.7 copy-done.5
  98.5 0.2 convert_reduce_fusion
  98.6 0.0 copy-start.3
  98.7 6.8 %all-to-all-done.1.parts_ref = bf16[4,64,1024]{2,1,0:T(8,128)(2,1)S(1)} async-done(((bf16[4,64,1024]{2,1,0:T(8,128)(2,1)}), bf16[4,64,1024]{2,1,0:T(8,128)(2,1)S(1)}, u32[]{:S(2)}, u32[]{:S(2)}) %all-to-all-start.1) | async-done | bytes 524320 | tf_op jit(solution)/shard_map/all_to_all | solution.py:202
  105.5 0.0 copy-done.3
  105.5 0.8 norm.1
  106.3 4.5 %all-to-all-start.2 = ((bf16[4,64,256]{2,1,0:T(8,128)(2,1)}), bf16[4,64,256]{2,1,0:T(8,128)(2,1)S(1)}, u32[]{:S(2)}, u32[]{:S(2)}) async-start(bf16[4,64,256]{2,1,0:T(8,128)(2,1)} %norm.1), calls=%async_computation.2 | async-start | bytes 262144 | tf_op jit(solution)/shard_map/all_to_all | solution.py:204
  110.8 0.1 select_convert_fusion
  111.0 3.5 %all-to-all-done.2 = bf16[4,64,256]{2,1,0:T(8,128)(2,1)S(1)} async-done(((bf16[4,64,256]{2,1,0:T(8,128)(2,1)}), bf16[4,64,256]{2,1,0:T(8,128)(2,1)S(1)}, u32[]{:S(2)}, u32[]{:S(2)}) %all-to-all-start.2) | async-done | bytes 131104 | tf_op jit(solution)/shard_map/all_to_all | solution.py:204
  114.4 0.3 convolution_convert_fusion
  114.7 0.0 copy-start
  114.8 0.1 reshape.61
  114.9 32.0 %all_to_all.20 = bf16[128,4,384]{2,1,0:T(4,128)(2,1)S(1)} all-to-all(bf16[128,4,384]{2,1,0:T(4,128)(2,1)S(1)} %reshape.61), channel_id=1, replica_groups=mesh['zh'=4,'x'=4,'yh'=4,'yl'=2,'zl'=2,'core'=2] {'zh','x','yh','yl'}, dimensions={0} | all-to-all | bytes 786432 | tf_op jit(solution)/shard_map/all_to_all | solution.py:221
  146.8 0.1 reshape.62.rows_ref
  146.9 0.0 copy-done
  147.0 2.7 %write.1 = bf16[2048,256]{1,0:T(8,128)(2,1)} custom-call(bf16[2048,256]{1,0:T(8,128)(2,1)S(1)} %copy-done, bf16[512,384]{1,0:T(8,128)(2,1)S(1)} %reshape.62.rows_ref), custom_call_target="tpu_custom_call" | custom-call | tf_op jit(solution)/shard_map/write/pallas_call | solution.py:161
  (3 shorter events, 0.0 us)
Async XLA Ops:
  0.0 0.8 copy-start.1
  0.8 0.7 copy-start.2
  2.4 16.6 %copy-start.4 = (bf16[256,512]{1,0:T(8,128)(2,1)S(1)}, bf16[256,512]{1,0:T(8,128)(2,1)}, u32[]{:S(2)}) copy-start(bf16[256,512]{1,0:T(8,128)(2,1)} %param.7) | copy-start | bytes 786436
  2.4 46.0 %all-to-all-start = ((bf16[32,24,512]{2,1,0:T(8,128)(2,1)}), bf16[32,24,512]{2,1,0:T(8,128)(2,1)S(1)}, u32[]{:S(2)}, u32[]{:S(2)}) async-start(bf16[32,24,512]{2,1,0:T(8,128)(2,1)} %pieces.1), calls=%async_computation | async-start | bytes 1572864 | tf_op jit(solution)/shard_map/all_to_all | solution.py:186
  19.1 4.0 %collective-permute-start = (bf16[256,512]{1,0:T(8,128)(2,1)S(1)}, bf16[256,512]{1,0:T(8,128)(2,1)S(1)}, u32[]{:S(2)}, u32[]{:S(2)}) collective-permute-start(bf16[256,512]{1,0:T(8,128)(2,1)S(1)} %copy-done.4), channel_id=1, source_target_pairs={{0,1},{1,0},{2,3},{3,2},{4,5},{5,4},{6,7},{7,6},{8,9},{9,8},{10,11... | collective-permute-start | bytes 786440 | tf_op jit(solution)/shard_map/ppermute | solution.py:178
  23.2 25.2 %collective-permute-start.1 = (bf16[2,256,512]{2,1,0:T(8,128)(2,1)S(1)}, bf16[2,256,512]{2,1,0:T(8,128)(2,1)S(1)}, u32[]{:S(2)}, u32[]{:S(2)}) collective-permute-start(bf16[2,256,512]{2,1,0:T(8,128)(2,1)S(1)} %get-tuple-element.18), channel_id=1, source_target_pairs={{0,4},{4,0},{1,5},{5,1},{2,6},{6,2},{3,7},{7,3},{8,12},{12,8},{9,1... | collective-permute-start | bytes 1572872 | tf_op jit(solution)/shard_map/ppermute | solution.py:178
  48.5 34.7 %collective-permute-start.2 = (bf16[2,2,256,512]{3,2,1,0:T(8,128)(2,1)S(1)}, bf16[2,2,256,512]{3,2,1,0:T(8,128)(2,1)}, u32[]{:S(2)}, u32[]{:S(2)}) collective-permute-start(bf16[2,2,256,512]{3,2,1,0:T(8,128)(2,1)S(1)} %pad_maximum_fusion.near), channel_id=1, source_target_pairs={{0,2},{2,0},{1,3},{3,1},{4,6},{6,4},{5,7},{7,5},{8,10},{10,8},{9,1... | collective-permute-start | bytes 3145736 | tf_op jit(solution)/shard_map/ppermute | solution.py:178
  52.6 13.0 %collective-permute-start.3 = (bf16[16,24,512]{2,1,0:T(8,128)(2,1)}, bf16[16,24,512]{2,1,0:T(8,128)(2,1)S(1)}, u32[]{:S(2)}, u32[]{:S(2)}) collective-permute-start(bf16[16,24,512]{2,1,0:T(8,128)(2,1)} %get-tuple-element.16), channel_id=1, source_target_pairs={{0,32},{32,64},{64,96},{96,0},{1,33},{33,65},{65,97},{97,1},{2,34}... | collective-permute-start | bytes 1179656 | tf_op jit(solution)/shard_map/ppermute | solution.py:174
  55.7 11.8 %collective-permute-start.6 = (bf16[16,24,512]{2,1,0:T(8,128)(2,1)}, bf16[16,24,512]{2,1,0:T(8,128)(2,1)S(1)}, u32[]{:S(2)}, u32[]{:S(2)}) collective-permute-start(bf16[16,24,512]{2,1,0:T(8,128)(2,1)} %get-tuple-element.15), channel_id=1, source_target_pairs={{0,96},{32,0},{64,32},{96,64},{1,97},{33,1},{65,33},{97,65},{2,98}... | collective-permute-start | bytes 1179656 | tf_op jit(solution)/shard_map/ppermute | solution.py:174
  59.1 14.5 %collective-permute-start.4 = (bf16[16,24,512]{2,1,0:T(8,128)(2,1)}, bf16[16,24,512]{2,1,0:T(8,128)(2,1)S(1)}, u32[]{:S(2)}, u32[]{:S(2)}) collective-permute-start(bf16[16,24,512]{2,1,0:T(8,128)(2,1)} %get-tuple-element.15), channel_id=1, source_target_pairs={{0,32},{32,64},{64,96},{96,0},{1,33},{33,65},{65,97},{97,1},{2,34}... | collective-permute-start | bytes 1179656 | tf_op jit(solution)/shard_map/ppermute | solution.py:174
  61.0 13.9 %collective-permute-start.5 = (bf16[16,24,512]{2,1,0:T(8,128)(2,1)}, bf16[16,24,512]{2,1,0:T(8,128)(2,1)S(1)}, u32[]{:S(2)}, u32[]{:S(2)}) collective-permute-start(bf16[16,24,512]{2,1,0:T(8,128)(2,1)} %get-tuple-element.16), channel_id=1, source_target_pairs={{0,96},{32,0},{64,32},{96,64},{1,97},{33,1},{65,33},{97,65},{2,98}... | collective-permute-start | bytes 1179656 | tf_op jit(solution)/shard_map/ppermute | solution.py:174
  65.6 16.5 %collective-permute-start.7 = (bf16[16,24,512]{2,1,0:T(8,128)(2,1)S(1)}, bf16[16,24,512]{2,1,0:T(8,128)(2,1)}, u32[]{:S(2)}, u32[]{:S(2)}) collective-permute-start(bf16[16,24,512]{2,1,0:T(8,128)(2,1)S(1)} %collective-permute-done.3), channel_id=1, source_target_pairs={{0,32},{32,64},{64,96},{96,0},{1,33},{33,65},{65,97},{97,1},{2,34}... | collective-permute-start | bytes 1179656 | tf_op jit(solution)/shard_map/ppermute | solution.py:174
  67.5 15.7 %collective-permute-start.8 = (bf16[16,24,512]{2,1,0:T(8,128)(2,1)S(1)}, bf16[16,24,512]{2,1,0:T(8,128)(2,1)}, u32[]{:S(2)}, u32[]{:S(2)}) collective-permute-start(bf16[16,24,512]{2,1,0:T(8,128)(2,1)S(1)} %collective-permute-done.6), channel_id=1, source_target_pairs={{0,96},{32,0},{64,32},{96,64},{1,97},{33,1},{65,33},{97,65},{2,98}... | collective-permute-start | bytes 1179656 | tf_op jit(solution)/shard_map/ppermute | solution.py:174
  72.1 0.7 copy-start.6
  86.8 6.5 %collective-permute-start.9 = (bf16[4,64,1024]{2,1,0:T(8,128)(2,1)S(1)}, bf16[4,64,1024]{2,1,0:T(8,128)(2,1)S(1)}, u32[]{:S(2)}, u32[]{:S(2)}) collective-permute-start(bf16[4,64,1024]{2,1,0:T(8,128)(2,1)S(1)} %get-tuple-element.12), channel_id=1, source_target_pairs={{0,1},{1,0},{2,3},{3,2},{4,5},{5,4},{6,7},{7,6},{8,9},{9,8},{10,11... | collective-permute-start | bytes 1572872 | tf_op jit(solution)/shard_map/ppermute | solution.py:178
  94.3 11.2 %all-to-all-start.1 = ((bf16[4,64,1024]{2,1,0:T(8,128)(2,1)}), bf16[4,64,1024]{2,1,0:T(8,128)(2,1)S(1)}, u32[]{:S(2)}, u32[]{:S(2)}) async-start(bf16[4,64,1024]{2,1,0:T(8,128)(2,1)} %add_convert_fusion), calls=%async_computation.1 | async-start | bytes 1048576 | tf_op jit(solution)/shard_map/all_to_all | solution.py:202
  97.8 0.7 copy-start.5
  98.6 6.9 %copy-start.3 = (f32[1024]{0:T(1024)S(1)}, f32[1024]{0:T(1024)}, u32[]{:S(2)}) copy-start(f32[1024]{0:T(1024)} %param.12) | copy-start | bytes 12292
  106.3 8.1 %all-to-all-start.2 = ((bf16[4,64,256]{2,1,0:T(8,128)(2,1)}), bf16[4,64,256]{2,1,0:T(8,128)(2,1)S(1)}, u32[]{:S(2)}, u32[]{:S(2)}) async-start(bf16[4,64,256]{2,1,0:T(8,128)(2,1)} %norm.1), calls=%async_computation.2 | async-start | bytes 262144 | tf_op jit(solution)/shard_map/all_to_all | solution.py:204
  114.7 32.2 %copy-start = (bf16[2048,256]{1,0:T(8,128)(2,1)S(1)}, bf16[2048,256]{1,0:T(8,128)(2,1)}, u32[]{:S(2)}) copy-start(bf16[2048,256]{1,0:T(8,128)(2,1)} %table_ref.1) | copy-start | bytes 3145732

commit v4 on v3

--- a/solution.py
+++ b/solution.py
@@ -46,10 +46,10 @@
 
 
 def tower_kernel(
-    place_ref, near, far, mine, la, lb, ra, rb, fa, fb, bias_ref, give_ref, keep_ref, w_all, hid
+    place_ref, f0, f1, f2, f3, mine, la, lb, ra, rb, fa, fb, bias_ref, give_ref, keep_ref, w_all, hid
 ):
     x0, tp, yl, core = (place_ref[i] for i in range(4))
-    feats = (near, far)
+    feats = ((f0, f1), (f2, f3))
     blocks = (
         (0, mine.at[0:2], mine.at[2:4]),
         (3, la, lb),
@@ -71,7 +71,7 @@
             )
             for dy in range(2):
                 columns = jnp.concatenate(
-                    [feats[dz][dy, dc, :, pl.ds(col, 128)] for dc in range(2)], axis=1
+                    [feats[dz][dy][dc, :, pl.ds(col, 128)] for dc in range(2)], axis=1
                 )
                 term = jnp.dot(columns, weights, preferred_element_type=F32)
                 act[dy] = term if act[dy] is None else act[dy] + term
@@ -108,7 +108,7 @@
     return pl.pallas_call(
         tower_kernel,
         out_shape=(part, part),
-        in_specs=[SMEM] + [VMEM] * 10,
+        in_specs=[SMEM] + [VMEM] * 12,
         out_specs=(VMEM, VMEM),
         scratch_shapes=[pltpu.VMEM((D_OUT, HID), BF16), pltpu.VMEM((2, SRC, HID), BF16)],
         compiler_params=pltpu.CompilerParams(vmem_limit_bytes=48 << 20),
@@ -185,13 +185,14 @@
     w = pieces(w_in, w_out)
     mine = lax.all_to_all(w, PLANE, split_axis=0, concat_axis=0, tiled=True)
     pair = jnp.stack([features, swap(features, "core")])
-    mine, near = lax.optimization_barrier((mine, swap(pair, "yl")))
+    mine, pair = lax.optimization_barrier((mine, pair))
+    near = swap(pair, "yl")
+    over = swap(pair, "zl")
     la, rb = along_x(mine[:16], 1), along_x(mine[16:], -1)
     lb, ra = along_x(mine[16:], 1), along_x(mine[:16], -1)
     fa, fb = along_x(la, 1), along_x(rb, -1)
 
-    near = jnp.stack([pair, near])
-    feats = (near, swap(near, "zl"))
+    feats = (pair, near, over, swap(near, "zl"))
 
     halves = [each.reshape(2, 4, 2, 24, HID) for each in (la, lb, ra, rb, fa, fb)]
     weights = [mine.reshape(4, 4, 2, 24, HID)] + halves

time: 151 us -> 145 us (0.960)
  waiting for transfers between devices: 45 us -> 38.8 us
  blocking collectives: 32 us -> 28.6 us
  starting transfers between devices: 58.5 us -> 61.7 us
    ppermute x4 -> x5, waiting for transfers between devices: 24.5 us -> 2.66 us  [swap(): return lax.ppermute(block, axis, [(0, 1), (1, 0)])]
    all_to_all x1, waiting for transfers between devices: 0.01 us -> 17.8 us  [local(): mine = lax.all_to_all(w, PLANE, split_axis=0, concat_axis=0, tiled=True)]
    all_to_all x1, blocking collectives: 32 us -> 28.6 us  [local(): lax.all_to_all(packed.reshape(OWNERS, CAP, SHARE + META), SHARD, split_ax...]
    ppermute x4 -> x5, starting transfers between devices: 14.4 us -> 17.6 us  [swap(): return lax.ppermute(block, axis, [(0, 1), (1, 0)])]
    ppermute x6, waiting for transfers between devices: 10.2 us -> 8.03 us  [along_x(): return lax.ppermute(block, 'x', [(i, (i + step) % 4) for i in range(4)])]
  transfers between devices with their start and end apart: 13 -> 14, of which waited for: 9 -> 7; matrix products, arithmetic and copies ran while one was open for 1% -> 1% of each run, Pallas kernels for 0% -> 0%
where the time goes in v4:
time: 145 us; the launch traced here: 143 us
  starting transfers between devices  61.7 us (43%)
  waiting for transfers between devices  38.8 us (27%)
  blocking collectives  28.6 us (20%)
  Pallas kernels  8.15 us (6%)
  local copies, waits for them, and re-layouts  3.89 us (3%)
  other arithmetic  1.45 us (1%)
    all_to_all x1, blocking collectives, local(): lax.all_to_all(packed.reshape(OWNERS, CAP, SHARE + META), SHARD, split_ax...  28.6 us
    ppermute x6, starting transfers between devices, along_x(): return lax.ppermute(block, 'x', [(i, (i + step) % 4) for i in range(4)])  19.5 us
    all_to_all x1, waiting for transfers between devices, local(): mine = lax.all_to_all(w, PLANE, split_axis=0, concat_axis=0, tiled=True)  17.8 us
    ppermute x5, starting transfers between devices, swap(): return lax.ppermute(block, axis, [(0, 1), (1, 0)])  17.6 us
    all_to_all x1, starting transfers between devices, local(): mine = lax.all_to_all(w, PLANE, split_axis=0, concat_axis=0, tiled=True)  16.6 us
    ppermute x6, waiting for transfers between devices, along_x(): return lax.ppermute(block, 'x', [(i, (i + step) % 4) for i in range(4)])  8.03 us
    all_to_all x1, waiting for transfers between devices, local(): lax.all_to_all(chip, ('yl', 'zl'), split_axis=0, concat_axis=0, tiled=True)  6.84 us
    all_to_all x1, starting transfers between devices, local(): lax.all_to_all(columns, TP, split_axis=0, concat_axis=0, tiled=True)  4.49 us
  transfers between devices with their start and end apart: 14, of which 7 were waited for; matrix products, arithmetic and copies ran while one was open for 1% of the time, Pallas kernels for 0%

profile of v4, /device:TPU:1, one launch (start us, length us, event | category | flops | bytes accessed | tf_op | source)
XLA Modules:
  0.0 143.2 jit_solution(698596695246497054)
XLA Ops:
  0.0 0.0 copy-start.1
  0.0 0.8 copy-done.1
  0.8 0.0 copy-start.2
  0.8 0.7 copy-done.2
  1.5 1.0 pieces.1
  2.4 0.0 copy-start.5
  2.4 16.6 %all-to-all-start = ((bf16[32,24,512]{2,1,0:T(8,128)(2,1)}), bf16[32,24,512]{2,1,0:T(8,128)(2,1)S(1)}, u32[]{:S(2)}, u32[]{:S(2)}) async-start(bf16[32,24,512]{2,1,0:T(8,128)(2,1)} %pieces.1), calls=%async_computation | async-start | bytes 1572864 | tf_op jit(solution)/shard_map/all_to_all | solution.py:186
  19.1 0.0 copy-done.5
  19.1 2.9 %collective-permute-start = (bf16[256,512]{1,0:T(8,128)(2,1)S(1)}, bf16[256,512]{1,0:T(8,128)(2,1)S(1)}, u32[]{:S(2)}, u32[]{:S(2)}) collective-permute-start(bf16[256,512]{1,0:T(8,128)(2,1)S(1)} %copy-done.5), channel_id=1, source_target_pairs={{0,1},{1,0},{2,3},{3,2},{4,5},{5,4},{6,7},{7,6},{8,9},{9,8},{10,11... | collective-permute-start | bytes 786440 | tf_op jit(solution)/shard_map/ppermute | solution.py:178
  22.0 1.1 collective-permute-done
  23.1 0.1 pad_maximum_fusion.f0
  23.2 17.8 %all-to-all-done = bf16[32,24,512]{2,1,0:T(8,128)(2,1)S(1)} async-done(((bf16[32,24,512]{2,1,0:T(8,128)(2,1)}), bf16[32,24,512]{2,1,0:T(8,128)(2,1)S(1)}, u32[]{:S(2)}, u32[]{:S(2)}) %all-to-all-start) | async-done | bytes 786464 | tf_op jit(solution)/shard_map/all_to_all | solution.py:186
  40.9 0.0 copy-start.4
  40.9 3.6 %collective-permute-start.1 = (bf16[2,256,512]{2,1,0:T(8,128)(2,1)S(1)}, bf16[2,256,512]{2,1,0:T(8,128)(2,1)S(1)}, u32[]{:S(2)}, u32[]{:S(2)}) collective-permute-start(bf16[2,256,512]{2,1,0:T(8,128)(2,1)S(1)} %pad_maximum_fusion.f0), channel_id=1, source_target_pairs={{0,4},{4,0},{1,5},{5,1},{2,6},{6,2},{3,7},{7,3},{8,12},{12,8},{9,1... | collective-permute-start | bytes 1572872 | tf_op jit(solution)/shard_map/ppermute | solution.py:178
  44.6 0.8 fusion.6
  45.4 0.0 copy-done.4
  45.4 3.1 %collective-permute-start.4 = (bf16[16,24,512]{2,1,0:T(8,128)(2,1)}, bf16[16,24,512]{2,1,0:T(8,128)(2,1)S(1)}, u32[]{:S(2)}, u32[]{:S(2)}) collective-permute-start(bf16[16,24,512]{2,1,0:T(8,128)(2,1)} %get-tuple-element.16), channel_id=1, source_target_pairs={{0,32},{32,64},{64,96},{96,0},{1,33},{33,65},{65,97},{97,1},{2,34}... | collective-permute-start | bytes 1179656 | tf_op jit(solution)/shard_map/ppermute | solution.py:174
  48.5 3.4 %collective-permute-start.7 = (bf16[16,24,512]{2,1,0:T(8,128)(2,1)S(1)}, bf16[16,24,512]{2,1,0:T(8,128)(2,1)S(1)}, u32[]{:S(2)}, u32[]{:S(2)}) collective-permute-start(bf16[16,24,512]{2,1,0:T(8,128)(2,1)S(1)} %get-tuple-element.15), channel_id=1, source_target_pairs={{0,96},{32,0},{64,32},{96,64},{1,97},{33,1},{65,33},{97,65},{2,98}... | collective-permute-start | bytes 1179656 | tf_op jit(solution)/shard_map/ppermute | solution.py:174
  51.9 1.9 %collective-permute-start.5 = (bf16[16,24,512]{2,1,0:T(8,128)(2,1)S(1)}, bf16[16,24,512]{2,1,0:T(8,128)(2,1)S(1)}, u32[]{:S(2)}, u32[]{:S(2)}) collective-permute-start(bf16[16,24,512]{2,1,0:T(8,128)(2,1)S(1)} %get-tuple-element.15), channel_id=1, source_target_pairs={{0,32},{32,64},{64,96},{96,0},{1,33},{33,65},{65,97},{97,1},{2,34}... | collective-permute-start | bytes 1179656 | tf_op jit(solution)/shard_map/ppermute | solution.py:174
  53.8 3.0 %collective-permute-start.2 = (bf16[2,256,512]{2,1,0:T(8,128)(2,1)S(1)}, bf16[2,256,512]{2,1,0:T(8,128)(2,1)S(1)}, u32[]{:S(2)}, u32[]{:S(2)}) collective-permute-start(bf16[2,256,512]{2,1,0:T(8,128)(2,1)S(1)} %pad_maximum_fusion.f0), channel_id=1, source_target_pairs={{0,2},{2,0},{1,3},{3,1},{4,6},{6,4},{5,7},{7,5},{8,10},{10,8},{9,1... | collective-permute-start | bytes 1572872 | tf_op jit(solution)/shard_map/ppermute | solution.py:178
  56.8 0.0 collective-permute-done.1.f1
  56.8 2.3 %collective-permute-start.3 = (bf16[2,256,512]{2,1,0:T(8,128)(2,1)S(1)}, bf16[2,256,512]{2,1,0:T(8,128)(2,1)S(1)}, u32[]{:S(2)}, u32[]{:S(2)}) collective-permute-start(bf16[2,256,512]{2,1,0:T(8,128)(2,1)S(1)} %collective-permute-done.1.f1), channel_id=1, source_target_pairs={{0,2},{2,0},{1,3},{3,1},{4,6},{6,4},{5,7},{7,5},{8,10},{10,8},{9,1... | collective-permute-start | bytes 1572872 | tf_op jit(solution)/shard_map/ppermute | solution.py:178
  59.1 0.0 collective-permute-done.4
  59.1 4.6 %collective-permute-start.6 = (bf16[16,24,512]{2,1,0:T(8,128)(2,1)}, bf16[16,24,512]{2,1,0:T(8,128)(2,1)}, u32[]{:S(2)}, u32[]{:S(2)}) collective-permute-start(bf16[16,24,512]{2,1,0:T(8,128)(2,1)} %get-tuple-element.16), channel_id=1, source_target_pairs={{0,96},{32,0},{64,32},{96,64},{1,97},{33,1},{65,33},{97,65},{2,98}... | collective-permute-start | bytes 1179656 | tf_op jit(solution)/shard_map/ppermute | solution.py:174
  63.7 0.0 collective-permute-done.7
  63.7 1.9 %collective-permute-start.8 = (bf16[16,24,512]{2,1,0:T(8,128)(2,1)S(1)}, bf16[16,24,512]{2,1,0:T(8,128)(2,1)}, u32[]{:S(2)}, u32[]{:S(2)}) collective-permute-start(bf16[16,24,512]{2,1,0:T(8,128)(2,1)S(1)} %collective-permute-done.4), channel_id=1, source_target_pairs={{0,32},{32,64},{64,96},{96,0},{1,33},{33,65},{65,97},{97,1},{2,34}... | collective-permute-start | bytes 1179656 | tf_op jit(solution)/shard_map/ppermute | solution.py:174
  65.6 0.0 collective-permute-done.5
  65.7 4.6 %collective-permute-start.9 = (bf16[16,24,512]{2,1,0:T(8,128)(2,1)S(1)}, bf16[16,24,512]{2,1,0:T(8,128)(2,1)}, u32[]{:S(2)}, u32[]{:S(2)}) collective-permute-start(bf16[16,24,512]{2,1,0:T(8,128)(2,1)S(1)} %collective-permute-done.7), channel_id=1, source_target_pairs={{0,96},{32,0},{64,32},{96,64},{1,97},{33,1},{65,33},{97,65},{2,98}... | collective-permute-start | bytes 1179656 | tf_op jit(solution)/shard_map/ppermute | solution.py:174
  70.2 0.0 copy-start.7
  70.3 0.7 copy-done.7
  70.9 0.1 dynamic_slice.3
  71.0 0.1 pad_add_fusion.place_ref
  71.1 0.0 collective-permute-done.6
  71.1 0.0 collective-permute-done.2.f2
  71.1 2.5 %collective-permute-done.8 = bf16[16,24,512]{2,1,0:T(8,128)(2,1)} collective-permute-done((bf16[16,24,512]{2,1,0:T(8,128)(2,1)S(1)}, bf16[16,24,512]{2,1,0:T(8,128)(2,1)}, u32[]{:S(2)}, u32[]{:S(2)}) %collective-permute-start.8) | collective-permute-done | bytes 393248 | tf_op jit(solution)/shard_map/ppermute | solution.py:174
  73.6 5.6 %collective-permute-done.9 = bf16[16,24,512]{2,1,0:T(8,128)(2,1)} collective-permute-done((bf16[16,24,512]{2,1,0:T(8,128)(2,1)S(1)}, bf16[16,24,512]{2,1,0:T(8,128)(2,1)}, u32[]{:S(2)}, u32[]{:S(2)}) %collective-permute-start.9) | collective-permute-done | bytes 393248 | tf_op jit(solution)/shard_map/ppermute | solution.py:174
  79.1 0.0 collective-permute-done.3.f3
  79.1 3.6 %tower.1 = (bf16[4,64,1024]{2,1,0:T(8,128)(2,1)S(1)}, bf16[4,64,1024]{2,1,0:T(8,128)(2,1)S(1)}) custom-call(s32[4]{0:T(128)S(1)} %pad_add_fusion.place_ref, bf16[2,256,512]{2,1,0:T(8,128)(2,1)S(1)} %pad_maximum_fusion.f0, bf16[2,256,512]{2,1,0:T(8,128)(2,1)S(1)} %collective-permute-done.1.f1, bf16[2,256,512]{2,1,0:T(8,128)(2,1)S(1)} %collective-permute-done.2.f2, ...), custom_call_target="tpu_custom_call" | custom-call | tf_op jit(solution)/shard_map/tower/pallas_call | solution.py:108
  82.7 5.8 %collective-permute-start.10 = (bf16[4,64,1024]{2,1,0:T(8,128)(2,1)S(1)}, bf16[4,64,1024]{2,1,0:T(8,128)(2,1)S(1)}, u32[]{:S(2)}, u32[]{:S(2)}) collective-permute-start(bf16[4,64,1024]{2,1,0:T(8,128)(2,1)S(1)} %get-tuple-element.12), channel_id=1, source_target_pairs={{0,1},{1,0},{2,3},{3,2},{4,5},{5,4},{6,7},{7,6},{8,9},{9,8},{10,11... | collective-permute-start | bytes 1572872 | tf_op jit(solution)/shard_map/ppermute | solution.py:178
  88.6 1.5 %collective-permute-done.10 = bf16[4,64,1024]{2,1,0:T(8,128)(2,1)S(1)} collective-permute-done((bf16[4,64,1024]{2,1,0:T(8,128)(2,1)S(1)}, bf16[4,64,1024]{2,1,0:T(8,128)(2,1)S(1)}, u32[]{:S(2)}, u32[]{:S(2)}) %collective-permute-start.10) | collective-permute-done | bytes 524320 | tf_op jit(solution)/shard_map/ppermute | solution.py:178
  90.1 1.0 add_convert_fusion
  91.1 3.5 %all-to-all-start.1 = ((bf16[4,64,1024]{2,1,0:T(8,128)(2,1)}), bf16[4,64,1024]{2,1,0:T(8,128)(2,1)S(1)}, u32[]{:S(2)}, u32[]{:S(2)}) async-start(bf16[4,64,1024]{2,1,0:T(8,128)(2,1)} %add_convert_fusion), calls=%async_computation.1 | async-start | bytes 1048576 | tf_op jit(solution)/shard_map/all_to_all | solution.py:203
  94.6 0.0 copy-start.6
  94.6 0.7 copy-done.6
  95.3 0.2 convert_reduce_fusion
  95.4 0.0 copy-start.3
  95.5 6.8 %all-to-all-done.1.parts_ref = bf16[4,64,1024]{2,1,0:T(8,128)(2,1)S(1)} async-done(((bf16[4,64,1024]{2,1,0:T(8,128)(2,1)}), bf16[4,64,1024]{2,1,0:T(8,128)(2,1)S(1)}, u32[]{:S(2)}, u32[]{:S(2)}) %all-to-all-start.1) | async-done | bytes 524320 | tf_op jit(solution)/shard_map/all_to_all | solution.py:203
  102.3 0.0 copy-done.3
  102.3 0.8 norm.1
  103.1 4.5 %all-to-all-start.2 = ((bf16[4,64,256]{2,1,0:T(8,128)(2,1)}), bf16[4,64,256]{2,1,0:T(8,128)(2,1)S(1)}, u32[]{:S(2)}, u32[]{:S(2)}) async-start(bf16[4,64,256]{2,1,0:T(8,128)(2,1)} %norm.1), calls=%async_computation.2 | async-start | bytes 262144 | tf_op jit(solution)/shard_map/all_to_all | solution.py:205
  107.6 0.1 select_convert_fusion
  107.8 3.5 %all-to-all-done.2 = bf16[4,64,256]{2,1,0:T(8,128)(2,1)S(1)} async-done(((bf16[4,64,256]{2,1,0:T(8,128)(2,1)}), bf16[4,64,256]{2,1,0:T(8,128)(2,1)S(1)}, u32[]{:S(2)}, u32[]{:S(2)}) %all-to-all-start.2) | async-done | bytes 131104 | tf_op jit(solution)/shard_map/all_to_all | solution.py:205
  111.2 0.3 convolution_convert_fusion
  111.5 0.0 copy-start
  111.6 0.1 reshape.61
  111.7 28.6 %all_to_all.20 = bf16[128,4,384]{2,1,0:T(4,128)(2,1)S(1)} all-to-all(bf16[128,4,384]{2,1,0:T(4,128)(2,1)S(1)} %reshape.61), channel_id=1, replica_groups=mesh['zh'=4,'x'=4,'yh'=4,'yl'=2,'zl'=2,'core'=2] {'zh','x','yh','yl'}, dimensions={0} | all-to-all | bytes 786432 | tf_op jit(solution)/shard_map/all_to_all | solution.py:222
  140.3 0.1 reshape.62.rows_ref
  140.4 0.0 copy-done
  140.4 2.7 %write.1 = bf16[2048,256]{1,0:T(8,128)(2,1)} custom-call(bf16[2048,256]{1,0:T(8,128)(2,1)S(1)} %copy-done, bf16[512,384]{1,0:T(8,128)(2,1)S(1)} %reshape.62.rows_ref), custom_call_target="tpu_custom_call" | custom-call | tf_op jit(solution)/shard_map/write/pallas_call | solution.py:161
  (3 shorter events, 0.0 us)
Async XLA Ops:
  0.0 0.8 copy-start.1
  0.8 0.7 copy-start.2
  2.4 16.6 %copy-start.5 = (bf16[256,512]{1,0:T(8,128)(2,1)S(1)}, bf16[256,512]{1,0:T(8,128)(2,1)}, u32[]{:S(2)}) copy-start(bf16[256,512]{1,0:T(8,128)(2,1)} %param.7) | copy-start | bytes 786436
  2.4 38.5 %all-to-all-start = ((bf16[32,24,512]{2,1,0:T(8,128)(2,1)}), bf16[32,24,512]{2,1,0:T(8,128)(2,1)S(1)}, u32[]{:S(2)}, u32[]{:S(2)}) async-start(bf16[32,24,512]{2,1,0:T(8,128)(2,1)} %pieces.1), calls=%async_computation | async-start | bytes 1572864 | tf_op jit(solution)/shard_map/all_to_all | solution.py:186
  19.1 4.0 %collective-permute-start = (bf16[256,512]{1,0:T(8,128)(2,1)S(1)}, bf16[256,512]{1,0:T(8,128)(2,1)S(1)}, u32[]{:S(2)}, u32[]{:S(2)}) collective-permute-start(bf16[256,512]{1,0:T(8,128)(2,1)S(1)} %copy-done.5), channel_id=1, source_target_pairs={{0,1},{1,0},{2,3},{3,2},{4,5},{5,4},{6,7},{7,6},{8,9},{9,8},{10,11... | collective-permute-start | bytes 786440 | tf_op jit(solution)/shard_map/ppermute | solution.py:178
  40.9 4.4 %copy-start.4 = (bf16[32,24,512]{2,1,0:T(8,128)(2,1)}, bf16[32,24,512]{2,1,0:T(8,128)(2,1)S(1)}, u32[]{:S(2)}) copy-start(bf16[32,24,512]{2,1,0:T(8,128)(2,1)S(1)} %all-to-all-done) | copy-start | bytes 2359300
  40.9 15.9 %collective-permute-start.1 = (bf16[2,256,512]{2,1,0:T(8,128)(2,1)S(1)}, bf16[2,256,512]{2,1,0:T(8,128)(2,1)S(1)}, u32[]{:S(2)}, u32[]{:S(2)}) collective-permute-start(bf16[2,256,512]{2,1,0:T(8,128)(2,1)S(1)} %pad_maximum_fusion.f0), channel_id=1, source_target_pairs={{0,4},{4,0},{1,5},{5,1},{2,6},{6,2},{3,7},{7,3},{8,12},{12,8},{9,1... | collective-permute-start | bytes 1572872 | tf_op jit(solution)/shard_map/ppermute | solution.py:178
  45.4 13.7 %collective-permute-start.4 = (bf16[16,24,512]{2,1,0:T(8,128)(2,1)}, bf16[16,24,512]{2,1,0:T(8,128)(2,1)S(1)}, u32[]{:S(2)}, u32[]{:S(2)}) collective-permute-start(bf16[16,24,512]{2,1,0:T(8,128)(2,1)} %get-tuple-element.16), channel_id=1, source_target_pairs={{0,32},{32,64},{64,96},{96,0},{1,33},{33,65},{65,97},{97,1},{2,34}... | collective-permute-start | bytes 1179656 | tf_op jit(solution)/shard_map/ppermute | solution.py:174
  48.5 15.2 %collective-permute-start.7 = (bf16[16,24,512]{2,1,0:T(8,128)(2,1)S(1)}, bf16[16,24,512]{2,1,0:T(8,128)(2,1)S(1)}, u32[]{:S(2)}, u32[]{:S(2)}) collective-permute-start(bf16[16,24,512]{2,1,0:T(8,128)(2,1)S(1)} %get-tuple-element.15), channel_id=1, source_target_pairs={{0,96},{32,0},{64,32},{96,64},{1,97},{33,1},{65,33},{97,65},{2,98}... | collective-permute-start | bytes 1179656 | tf_op jit(solution)/shard_map/ppermute | solution.py:174
  51.9 13.8 %collective-permute-start.5 = (bf16[16,24,512]{2,1,0:T(8,128)(2,1)S(1)}, bf16[16,24,512]{2,1,0:T(8,128)(2,1)S(1)}, u32[]{:S(2)}, u32[]{:S(2)}) collective-permute-start(bf16[16,24,512]{2,1,0:T(8,128)(2,1)S(1)} %get-tuple-element.15), channel_id=1, source_target_pairs={{0,32},{32,64},{64,96},{96,0},{1,33},{33,65},{65,97},{97,1},{2,34}... | collective-permute-start | bytes 1179656 | tf_op jit(solution)/shard_map/ppermute | solution.py:174
  53.8 17.3 %collective-permute-start.2 = (bf16[2,256,512]{2,1,0:T(8,128)(2,1)S(1)}, bf16[2,256,512]{2,1,0:T(8,128)(2,1)S(1)}, u32[]{:S(2)}, u32[]{:S(2)}) collective-permute-start(bf16[2,256,512]{2,1,0:T(8,128)(2,1)S(1)} %pad_maximum_fusion.f0), channel_id=1, source_target_pairs={{0,2},{2,0},{1,3},{3,1},{4,6},{6,4},{5,7},{7,5},{8,10},{10,8},{9,1... | collective-permute-start | bytes 1572872 | tf_op jit(solution)/shard_map/ppermute | solution.py:178
  56.8 22.3 %collective-permute-start.3 = (bf16[2,256,512]{2,1,0:T(8,128)(2,1)S(1)}, bf16[2,256,512]{2,1,0:T(8,128)(2,1)S(1)}, u32[]{:S(2)}, u32[]{:S(2)}) collective-permute-start(bf16[2,256,512]{2,1,0:T(8,128)(2,1)S(1)} %collective-permute-done.1.f1), channel_id=1, source_target_pairs={{0,2},{2,0},{1,3},{3,1},{4,6},{6,4},{5,7},{7,5},{8,10},{10,8},{9,1... | collective-permute-start | bytes 1572872 | tf_op jit(solution)/shard_map/ppermute | solution.py:178
  59.1 12.0 %collective-permute-start.6 = (bf16[16,24,512]{2,1,0:T(8,128)(2,1)}, bf16[16,24,512]{2,1,0:T(8,128)(2,1)}, u32[]{:S(2)}, u32[]{:S(2)}) collective-permute-start(bf16[16,24,512]{2,1,0:T(8,128)(2,1)} %get-tuple-element.16), channel_id=1, source_target_pairs={{0,96},{32,0},{64,32},{96,64},{1,97},{33,1},{65,33},{97,65},{2,98}... | collective-permute-start | bytes 1179656 | tf_op jit(solution)/shard_map/ppermute | solution.py:174
  63.7 9.8 %collective-permute-start.8 = (bf16[16,24,512]{2,1,0:T(8,128)(2,1)S(1)}, bf16[16,24,512]{2,1,0:T(8,128)(2,1)}, u32[]{:S(2)}, u32[]{:S(2)}) collective-permute-start(bf16[16,24,512]{2,1,0:T(8,128)(2,1)S(1)} %collective-permute-done.4), channel_id=1, source_target_pairs={{0,32},{32,64},{64,96},{96,0},{1,33},{33,65},{65,97},{97,1},{2,34}... | collective-permute-start | bytes 1179656 | tf_op jit(solution)/shard_map/ppermute | solution.py:174
  65.7 13.5 %collective-permute-start.9 = (bf16[16,24,512]{2,1,0:T(8,128)(2,1)S(1)}, bf16[16,24,512]{2,1,0:T(8,128)(2,1)}, u32[]{:S(2)}, u32[]{:S(2)}) collective-permute-start(bf16[16,24,512]{2,1,0:T(8,128)(2,1)S(1)} %collective-permute-done.7), channel_id=1, source_target_pairs={{0,96},{32,0},{64,32},{96,64},{1,97},{33,1},{65,33},{97,65},{2,98}... | collective-permute-start | bytes 1179656 | tf_op jit(solution)/shard_map/ppermute | solution.py:174
  70.2 0.7 copy-start.7
  82.7 7.3 %collective-permute-start.10 = (bf16[4,64,1024]{2,1,0:T(8,128)(2,1)S(1)}, bf16[4,64,1024]{2,1,0:T(8,128)(2,1)S(1)}, u32[]{:S(2)}, u32[]{:S(2)}) collective-permute-start(bf16[4,64,1024]{2,1,0:T(8,128)(2,1)S(1)} %get-tuple-element.12), channel_id=1, source_target_pairs={{0,1},{1,0},{2,3},{3,2},{4,5},{5,4},{6,7},{7,6},{8,9},{9,8},{10,11... | collective-permute-start | bytes 1572872 | tf_op jit(solution)/shard_map/ppermute | solution.py:178
  91.1 11.2 %all-to-all-start.1 = ((bf16[4,64,1024]{2,1,0:T(8,128)(2,1)}), bf16[4,64,1024]{2,1,0:T(8,128)(2,1)S(1)}, u32[]{:S(2)}, u32[]{:S(2)}) async-start(bf16[4,64,1024]{2,1,0:T(8,128)(2,1)} %add_convert_fusion), calls=%async_computation.1 | async-start | bytes 1048576 | tf_op jit(solution)/shard_map/all_to_all | solution.py:203
  94.6 0.7 copy-start.6
  95.4 6.9 %copy-start.3 = (f32[1024]{0:T(1024)S(1)}, f32[1024]{0:T(1024)}, u32[]{:S(2)}) copy-start(f32[1024]{0:T(1024)} %param.12) | copy-start | bytes 12292
  103.1 8.1 %all-to-all-start.2 = ((bf16[4,64,256]{2,1,0:T(8,128)(2,1)}), bf16[4,64,256]{2,1,0:T(8,128)(2,1)S(1)}, u32[]{:S(2)}, u32[]{:S(2)}) async-start(bf16[4,64,256]{2,1,0:T(8,128)(2,1)} %norm.1), calls=%async_computation.2 | async-start | bytes 262144 | tf_op jit(solution)/shard_map/all_to_all | solution.py:205
  111.5 28.9 %copy-start = (bf16[2048,256]{1,0:T(8,128)(2,1)S(1)}, bf16[2048,256]{1,0:T(8,128)(2,1)}, u32[]{:S(2)}) copy-start(bf16[2048,256]{1,0:T(8,128)(2,1)} %table_ref.1) | copy-start | bytes 3145732

commit v5 on v4

v5 whole, which is shorter than its diff:
```python
import jax
import jax.numpy as jnp
from jax import lax
from jax.experimental import pallas as pl
from jax.experimental.pallas import tpu as pltpu
from jax.sharding import Mesh, PartitionSpec as P

AXES = ("zh", "x", "yh", "yl", "zl", "core")
SIZES = (4, 4, 4, 2, 2, 2)
SHARD = ("zh", "x", "yh", "yl")
TP = ("zl", "core")
ROUTE = ("yl", "yh", "x", "zh")
PLANE = ("yh", "zh", "yl")

SRC = 256
CAP = 4
OWNERS = 128
OWN_ROWS = 2048
D_OUT = 1024
SHARE = 256
HID = 512
META = 128
BF16 = jnp.bfloat16
F32 = jnp.float32
VMEM = pl.BlockSpec(memory_space=pltpu.VMEM)
SMEM = pl.BlockSpec(memory_space=pltpu.SMEM)


def add_block(x0, tp, offset, first, second, feats, act, w_all):
    xk = lax.rem(x0 + offset, 4)
    col = pl.multiple_of(xk * 128, 128)
    act = list(act)
    for dz in range(2):
        weights = jnp.concatenate(
            [
                half[:, jnp.bitwise_xor(tp, dz * 2 + dc), :, 0:16, :].reshape(64, HID)
                for dc in range(2)
                for half in (first, second)
            ],
            axis=0,
        )
        for dy in range(2):
            columns = jnp.concatenate(
                [feats[dz][dy][dc, :, pl.ds(col, 128)] for dc in range(2)], axis=1
            )
            term = jnp.dot(columns, weights, preferred_element_type=F32)
            act[dy] = term if act[dy] is None else act[dy] + term
    for zh in range(4):
        rows = jnp.concatenate(
            [half[:, zh].astype(F32)[:, :, 16:24, :].reshape(32, HID) for half in (first, second)],
            axis=0,
        )
        row = pl.multiple_of(zh * 256 + xk * 64, 64)
        w_all[pl.ds(row, 64), :] = rows.astype(BF16)
    return act


def early_kernel(place_ref, f0, f1, f2, f3, mine, la, lb, ra, rb, act_ref, w_all):
    x0, tp = place_ref[0], place_ref[1]
    feats = ((f0, f1), (f2, f3))
    act = [None, None]
    for offset, first, second in ((0, mine.at[0:2], mine.at[2:4]), (3, la, lb), (1, ra, rb)):
        act = add_block(x0, tp, offset, first, second, feats, act, w_all)
    for dy in range(2):
        act_ref[dy] = act[dy]


def late_kernel(
    place_ref, f0, f1, f2, f3, fa, fb, bias_ref, act_ref, old_ref, give_ref, kept_ref, w_all, hid
):
    x0, tp, yl, core = (place_ref[i] for i in range(4))
    feats = ((f0, f1), (f2, f3))
    act = add_block(x0, tp, 2, fa, fb, feats, [act_ref[0], act_ref[1]], w_all)
    for dy in range(2):
        v = act[dy] + bias_ref[...]
        hid[dy] = (v * (1.0 / (1.0 + jnp.exp(-v)))).astype(BF16)

    def chunks(c):
        return [
            hid[dy, pl.ds(pl.multiple_of(zl * 128 + c * 64, 64), 64), :]
            for dy in range(2)
            for zl in range(2)
        ]

    part = lax.dot_general(
        jnp.concatenate(chunks(1 - core), axis=0),
        w_all[...],
        (((1,), (1,)), ((), ())),
        preferred_element_type=F32,
    ).astype(BF16)
    for i, chunk in enumerate(chunks(core)):
        slot = (i % 2) * 2 + jnp.bitwise_xor(yl, i // 2)
        give_ref[slot] = part[i * 64 : (i + 1) * 64]
        kept_ref[pl.ds(pl.multiple_of(slot * 64, 64), 64), :] = chunk


def kept_kernel(kept_ref, w_all, out_ref):
    part = lax.dot_general(
        kept_ref[...], w_all[...], (((1,), (1,)), ((), ())), preferred_element_type=F32
    )
    out_ref[...] = part.astype(BF16).reshape(out_ref.shape)


def cost(flops, moved):
    return pl.CostEstimate(flops=flops, bytes_accessed=moved, transcendentals=0)


def tower(place, feats, weights, bias):
    params = pltpu.CompilerParams(vmem_limit_bytes=48 << 20)
    part = jax.ShapeDtypeStruct((4, 64, D_OUT), BF16)
    w_shape = jax.ShapeDtypeStruct((D_OUT, HID), BF16)
    act, w_all = pl.pallas_call(
        early_kernel,
        out_shape=(jax.ShapeDtypeStruct((2, SRC, HID), F32), w_shape),
        in_specs=[SMEM] + [VMEM] * 9,
        out_specs=(VMEM, VMEM),
        compiler_params=params,
        cost_estimate=cost(6 * SRC * 1536 * HID, 6 << 20),
        name="early",
    )(place, *feats, *weights[:5])
    give, kept, w_all = pl.pallas_call(
        late_kernel,
        out_shape=(part, jax.ShapeDtypeStruct((SRC, HID), BF16), w_shape),
        in_specs=[SMEM] + [VMEM] * 9,
        out_specs=(VMEM, VMEM, VMEM),
        scratch_shapes=[pltpu.VMEM((2, SRC, HID), BF16)],
        input_output_aliases={9: 2},
        compiler_params=params,
        cost_estimate=cost(4 * SRC * 1024 * HID, 6 << 20),
        name="late",
    )(place, *feats, *weights[5:], bias, act, w_all)
    keep = pl.pallas_call(
        kept_kernel,
        out_shape=part,
        in_specs=[VMEM, VMEM],
        out_specs=VMEM,
        compiler_params=params,
        cost_estimate=cost(2 * SRC * HID * D_OUT, 2 << 20),
        name="kept",
    )(kept, w_all)
    return give, keep


def norm_kernel(parts_ref, bias_ref, out_ref):
    projected = bias_ref[...]
    for i in range(4):
        projected = projected + parts_ref[i].astype(F32)
    scale = lax.rsqrt(jnp.mean(projected * projected, axis=1, keepdims=True) + 1e-06)
    scaled = (projected * scale).astype(BF16)
    for q in range(4):
        out_ref[q] = scaled[:, q * SHARE : (q + 1) * SHARE]


def norm(parts, bias):
    return pl.pallas_call(
        norm_kernel,
        out_shape=jax.ShapeDtypeStruct((4, 64, SHARE), BF16),
        in_specs=[VMEM, VMEM],
        out_specs=VMEM,
        compiler_params=pltpu.CompilerParams(vmem_limit_bytes=16 << 20),
        name="norm",
    )(parts, bias)


def write_kernel(table_ref, rows_ref, out_ref, target_ref):
    block = table_ref.shape[0]

    @pl.when(pl.program_id(0) == 0)
    def _():
        lane = lax.broadcasted_iota(jnp.int32, (8, META), 1)
        weight = jnp.where(lane == 0, 64.0, jnp.where(lane == 1, 1.0, 0.0)).astype(BF16)
        target_ref[...] = lax.dot_general(
            weight, rows_ref[:, SHARE:], (((1,), (1,)), ((), ())), preferred_element_type=F32
        )

    row = lax.broadcasted_iota(jnp.int32, (block, 1), 0) + (pl.program_id(0) * block + 1)
    here = jnp.where(row.astype(F32) == target_ref[0:1, :], 1.0, 0.0)
    moved = jnp.dot(here.astype(BF16), rows_ref[:, :SHARE], preferred_element_type=F32)
    hit = jnp.max(here, axis=1, keepdims=True) > 0.5
    out_ref[...] = jnp.where(hit, moved, table_ref[...].astype(F32)).astype(BF16)


def write(table, rows):
    block = 512
    spec = pl.BlockSpec((block, SHARE), lambda i: (i, 0))
    return pl.pallas_call(
        write_kernel,
        out_shape=jax.ShapeDtypeStruct(table.shape, BF16),
        grid=(table.shape[0] // block,),
        in_specs=[spec, pl.BlockSpec(rows.shape, lambda i: (0, 0))],
        out_specs=spec,
        scratch_shapes=[pltpu.VMEM((8, rows.shape[0]), F32)],
        compiler_params=pltpu.CompilerParams(vmem_limit_bytes=32 << 20),
        name="write",
    )(table, rows)


def along_x(block, step):
    return lax.ppermute(block, "x", [(i, (i + step) % 4) for i in range(4)])


def swap(block, axis):
    return lax.ppermute(block, axis, [(0, 1), (1, 0)])


def local(features, item_id, w_in, bias_in, w_out, bias_out, item_table):
    index = {axis: lax.axis_index(axis).astype(jnp.int32) for axis in AXES}
    place = jnp.stack([index["x"], index["zl"] * 2 + index["core"], index["yl"], index["core"]])

    w = jnp.concatenate([w_in, w_out], axis=0).reshape(24, 2, HID).transpose(1, 0, 2)
    w = jnp.broadcast_to(w[None], (16, 2, 24, HID)).reshape(32, 24, HID)
    mine = lax.all_to_all(w, PLANE, split_axis=0, concat_axis=0, tiled=True)
    pair = jnp.stack([features, swap(features, "core")])
    mine, pair = lax.optimization_barrier((mine, pair))
    near = swap(pair, "yl")
    la, rb = along_x(mine[:16], 1), along_x(mine[16:], -1)
    lb, ra = along_x(mine[16:], 1), along_x(mine[:16], -1)
    fa, fb = along_x(la, 1), along_x(rb, -1)

    over = swap(pair, "zl")
    feats = (pair, near, over, swap(near, "zl"))

    halves = [each.reshape(2, 4, 2, 24, HID) for each in (la, lb, ra, rb, fa, fb)]
    weights = [mine.reshape(4, 4, 2, 24, HID)] + halves
    bias = lax.dynamic_slice_in_dim(bias_in, index["yl"] * HID, HID).reshape(1, HID)

    give, keep = tower(place, feats, weights, bias)
    chip = (keep.astype(F32) + swap(give, "core").astype(F32)).astype(BF16)
    parts = lax.all_to_all(chip, ("zl", "yl"), split_axis=0, concat_axis=0, tiled=True)
    columns = norm(parts, bias_out.reshape(1, D_OUT))
    columns = lax.all_to_all(columns, TP, split_axis=0, concat_axis=0, tiled=True)
    columns = columns.reshape(SRC, SHARE)

    owner = item_id // OWN_ROWS
    row = item_id - owner * OWN_ROWS + 1
    order = jnp.arange(SRC, dtype=jnp.int32)
    before = (owner[:, None] == owner[None, :]) & (order[None, :] < order[:, None])
    place_of = (owner & 1) * 64 + ((owner >> 1) & 3) * 16 + ((owner >> 3) & 3) * 4 + (owner >> 5)
    slot = place_of * CAP + jnp.sum(before.astype(jnp.int32), axis=1)
    pick = (jnp.arange(OWNERS * CAP, dtype=jnp.int32)[:, None] == slot[None, :]).astype(BF16)
    lane = jnp.arange(META, dtype=jnp.int32)[None, :]
    meta = jnp.where(
        lane == 0,
        (row >> 6)[:, None],
        jnp.where(lane == 1, (row & 63)[:, None], 0),
    ).astype(BF16)
    payload = jnp.concatenate([columns, meta], axis=1)
    packed = jnp.dot(pick, payload, preferred_element_type=F32).astype(BF16)
    arrived = lax.all_to_all(
        packed.reshape(OWNERS, CAP, SHARE + META), ROUTE, split_axis=0, concat_axis=0, tiled=True
    )
    return write(item_table, arrived.reshape(OWNERS * CAP, SHARE + META))


def solution(mesh):
    cut = Mesh(mesh.devices.reshape(SIZES), AXES)
    in_specs = (
        P(SHARD, TP),
        P(SHARD),
        P(SHARD, TP),
        P(TP),
        P(SHARD, TP),
        P(),
        P(SHARD, TP),
    )
    return jax.shard_map(
        local, mesh=cut, in_specs=in_specs, out_specs=P(SHARD, TP), check_vma=False
    )
```

time: 145 us -> 145 us (level)
  the two profiles are of different devices: /device:TPU:1 before, /device:TPU:8 now
where the time goes in v5:
time: 145 us; the launch traced here: 144 us
  starting transfers between devices  57.5 us (40%)
  waiting for transfers between devices  39.3 us (27%)
  blocking collectives  28.9 us (20%)
  Pallas kernels  9.29 us (6%)
  local copies, waits for them, and re-layouts  6.43 us (4%)
  other arithmetic  2.24 us (2%)
    all_to_all x1, blocking collectives, local(): lax.all_to_all(packed.reshape(OWNERS, CAP, SHARE + META), ROUTE, split_ax...  28.9 us
    ppermute x6, starting transfers between devices, along_x(): return lax.ppermute(block, 'x', [(i, (i + step) % 4) for i in range(4)])  21.1 us
    all_to_all x1, waiting for transfers between devices, local(): mine = lax.all_to_all(w, PLANE, split_axis=0, concat_axis=0, tiled=True)  21.1 us
    all_to_all x1, starting transfers between devices, local(): mine = lax.all_to_all(w, PLANE, split_axis=0, concat_axis=0, tiled=True)  16.3 us
    ppermute x5, starting transfers between devices, swap(): return lax.ppermute(block, axis, [(0, 1), (1, 0)])  11.6 us
    all_to_all x1, waiting for transfers between devices, local(): lax.all_to_all(chip, ('zl', 'yl'), split_axis=0, concat_axis=0, tiled=True)  7.1 us
    ppermute x5, waiting for transfers between devices, swap(): return lax.ppermute(block, axis, [(0, 1), (1, 0)])  6.62 us
    all_to_all x1, starting transfers between devices, local(): lax.all_to_all(chip, ('zl', 'yl'), split_axis=0, concat_axis=0, tiled=True)  5.17 us
  transfers between devices with their start and end apart: 14, of which 6 were waited for; matrix products, arithmetic and copies ran while one was open for 1% of the time, Pallas kernels for 3%

profile of v5, /device:TPU:8, one launch (start us, length us, event | category | flops | bytes accessed | tf_op | source)
XLA Modules:
  0.0 144.2 jit_solution(6074015461902935923)
XLA Ops:
  0.0 0.8 pad_maximum_fusion.1
  0.8 1.0 broadcast_in_dim.32
  1.8 0.0 copy-start.5
  1.8 16.3 %all-to-all-start = ((bf16[32,24,512]{2,1,0:T(8,128)(2,1)}), bf16[32,24,512]{2,1,0:T(8,128)(2,1)S(1)}, u32[]{:S(2)}, u32[]{:S(2)}) async-start(bf16[32,24,512]{2,1,0:T(8,128)(2,1)} %bitcast.5), calls=%async_computation | async-start | bytes 1572864 | tf_op jit(solution)/shard_map/all_to_all | solution.py:212
  18.1 0.0 copy-done.5
  18.1 1.9 %collective-permute-start = (bf16[256,512]{1,0:T(8,128)(2,1)S(1)}, bf16[256,512]{1,0:T(8,128)(2,1)S(1)}, u32[]{:S(2)}, u32[]{:S(2)}) collective-permute-start(bf16[256,512]{1,0:T(8,128)(2,1)S(1)} %copy-done.5), channel_id=1, source_target_pairs={{0,1},{1,0},{2,3},{3,2},{4,5},{5,4},{6,7},{7,6},{8,9},{9,8},{10,11... | collective-permute-start | bytes 786440 | tf_op jit(solution)/shard_map/ppermute | solution.py:203
  20.0 1.5 %collective-permute-done = bf16[256,512]{1,0:T(8,128)(2,1)S(1)} collective-permute-done((bf16[256,512]{1,0:T(8,128)(2,1)S(1)}, bf16[256,512]{1,0:T(8,128)(2,1)S(1)}, u32[]{:S(2)}, u32[]{:S(2)}) %collective-permute-start) | collective-permute-done | bytes 262176 | tf_op jit(solution)/shard_map/ppermute | solution.py:203
  21.5 0.1 pad_maximum_fusion.f0
  21.6 21.1 %all-to-all-done = bf16[32,24,512]{2,1,0:T(8,128)(2,1)S(1)} async-done(((bf16[32,24,512]{2,1,0:T(8,128)(2,1)}), bf16[32,24,512]{2,1,0:T(8,128)(2,1)S(1)}, u32[]{:S(2)}, u32[]{:S(2)}) %all-to-all-start) | async-done | bytes 786464 | tf_op jit(solution)/shard_map/all_to_all | solution.py:212
  42.7 1.9 %collective-permute-start.1 = (bf16[2,256,512]{2,1,0:T(8,128)(2,1)S(1)}, bf16[2,256,512]{2,1,0:T(8,128)(2,1)S(1)}, u32[]{:S(2)}, u32[]{:S(2)}) collective-permute-start(bf16[2,256,512]{2,1,0:T(8,128)(2,1)S(1)} %pad_maximum_fusion.f0), channel_id=1, source_target_pairs={{0,4},{4,0},{1,5},{5,1},{2,6},{6,2},{3,7},{7,3},{8,12},{12,8},{9,1... | collective-permute-start | bytes 1572872 | tf_op jit(solution)/shard_map/ppermute | solution.py:203
  44.6 0.8 fusion.6
  45.4 3.4 %collective-permute-start.4 = (bf16[16,24,512]{2,1,0:T(8,128)(2,1)}, bf16[16,24,512]{2,1,0:T(8,128)(2,1)}, u32[]{:S(2)}, u32[]{:S(2)}) collective-permute-start(bf16[16,24,512]{2,1,0:T(8,128)(2,1)} %get-tuple-element.22), channel_id=1, source_target_pairs={{0,32},{32,64},{64,96},{96,0},{1,33},{33,65},{65,97},{97,1},{2,34}... | collective-permute-start | bytes 1179656 | tf_op jit(solution)/shard_map/ppermute | solution.py:199
  48.8 3.7 %collective-permute-start.6 = (bf16[16,24,512]{2,1,0:T(8,128)(2,1)S(1)}, bf16[16,24,512]{2,1,0:T(8,128)(2,1)}, u32[]{:S(2)}, u32[]{:S(2)}) collective-permute-start(bf16[16,24,512]{2,1,0:T(8,128)(2,1)S(1)} %get-tuple-element.21), channel_id=1, source_target_pairs={{0,96},{32,0},{64,32},{96,64},{1,97},{33,1},{65,33},{97,65},{2,98}... | collective-permute-start | bytes 1179656 | tf_op jit(solution)/shard_map/ppermute | solution.py:199
  52.5 2.2 %collective-permute-start.8 = (bf16[16,24,512]{2,1,0:T(8,128)(2,1)S(1)}, bf16[16,24,512]{2,1,0:T(8,128)(2,1)S(1)}, u32[]{:S(2)}, u32[]{:S(2)}) collective-permute-start(bf16[16,24,512]{2,1,0:T(8,128)(2,1)S(1)} %get-tuple-element.21), channel_id=1, source_target_pairs={{0,32},{32,64},{64,96},{96,0},{1,33},{33,65},{65,97},{97,1},{2,34}... | collective-permute-start | bytes 1179656 | tf_op jit(solution)/shard_map/ppermute | solution.py:199
  54.7 3.4 %collective-permute-start.2 = (bf16[2,256,512]{2,1,0:T(8,128)(2,1)S(1)}, bf16[2,256,512]{2,1,0:T(8,128)(2,1)S(1)}, u32[]{:S(2)}, u32[]{:S(2)}) collective-permute-start(bf16[2,256,512]{2,1,0:T(8,128)(2,1)S(1)} %pad_maximum_fusion.f0), channel_id=1, source_target_pairs={{0,2},{2,0},{1,3},{3,1},{4,6},{6,4},{5,7},{7,5},{8,10},{10,8},{9,1... | collective-permute-start | bytes 1572872 | tf_op jit(solution)/shard_map/ppermute | solution.py:203
  58.0 0.0 collective-permute-done.1.f1
  58.1 2.5 %collective-permute-start.3 = (bf16[2,256,512]{2,1,0:T(8,128)(2,1)S(1)}, bf16[2,256,512]{2,1,0:T(8,128)(2,1)S(1)}, u32[]{:S(2)}, u32[]{:S(2)}) collective-permute-start(bf16[2,256,512]{2,1,0:T(8,128)(2,1)S(1)} %collective-permute-done.1.f1), channel_id=1, source_target_pairs={{0,2},{2,0},{1,3},{3,1},{4,6},{6,4},{5,7},{7,5},{8,10},{10,8},{9,1... | collective-permute-start | bytes 1572872 | tf_op jit(solution)/shard_map/ppermute | solution.py:203
  60.5 0.0 collective-permute-done.4
  60.5 4.9 %collective-permute-start.9 = (bf16[16,24,512]{2,1,0:T(8,128)(2,1)}, bf16[16,24,512]{2,1,0:T(8,128)(2,1)}, u32[]{:S(2)}, u32[]{:S(2)}) collective-permute-start(bf16[16,24,512]{2,1,0:T(8,128)(2,1)} %get-tuple-element.22), channel_id=1, source_target_pairs={{0,96},{32,0},{64,32},{96,64},{1,97},{33,1},{65,33},{97,65},{2,98}... | collective-permute-start | bytes 1179656 | tf_op jit(solution)/shard_map/ppermute | solution.py:199
  65.4 0.0 collective-permute-done.6
  65.4 1.9 %collective-permute-start.5 = (bf16[16,24,512]{2,1,0:T(8,128)(2,1)}, bf16[16,24,512]{2,1,0:T(8,128)(2,1)S(1)}, u32[]{:S(2)}, u32[]{:S(2)}) collective-permute-start(bf16[16,24,512]{2,1,0:T(8,128)(2,1)} %collective-permute-done.4), channel_id=1, source_target_pairs={{0,32},{32,64},{64,96},{96,0},{1,33},{33,65},{65,97},{97,1},{2,34}... | collective-permute-start | bytes 1179656 | tf_op jit(solution)/shard_map/ppermute | solution.py:199
  67.3 0.0 collective-permute-done.8
  67.4 0.0 copy-start.3
  67.4 0.8 copy-done.3
  68.1 5.1 %collective-permute-start.7 = (bf16[16,24,512]{2,1,0:T(8,128)(2,1)}, bf16[16,24,512]{2,1,0:T(8,128)(2,1)}, u32[]{:S(2)}, u32[]{:S(2)}) collective-permute-start(bf16[16,24,512]{2,1,0:T(8,128)(2,1)} %collective-permute-done.6), channel_id=1, source_target_pairs={{0,96},{32,0},{64,32},{96,64},{1,97},{33,1},{65,33},{97,65},{2,98}... | collective-permute-start | bytes 1179656 | tf_op jit(solution)/shard_map/ppermute | solution.py:199
  73.3 0.0 copy-start.7
  73.3 0.7 copy-done.7
  74.0 0.1 dynamic_slice.3
  74.0 0.1 pad_add_fusion.place_ref
  74.1 0.0 collective-permute-done.9
  74.1 0.0 collective-permute-done.2.f2
  74.1 3.7 %collective-permute-done.3.f3 = bf16[2,256,512]{2,1,0:T(8,128)(2,1)S(1)} collective-permute-done((bf16[2,256,512]{2,1,0:T(8,128)(2,1)S(1)}, bf16[2,256,512]{2,1,0:T(8,128)(2,1)S(1)}, u32[]{:S(2)}, u32[]{:S(2)}) %collective-permute-start.3) | collective-permute-done | bytes 524320 | tf_op jit(solution)/shard_map/ppermute | solution.py:203
  77.8 0.0 copy-start.4
  77.8 1.0 copy-done.4
  78.8 3.2 %early.1 = (f32[2,256,512]{2,1,0:T(8,128)S(1)}, bf16[1024,512]{1,0:T(8,128)(2,1)}) custom-call(s32[4]{0:T(128)S(1)} %pad_add_fusion.place_ref, bf16[2,256,512]{2,1,0:T(8,128)(2,1)S(1)} %pad_maximum_fusion.f0, bf16[2,256,512]{2,1,0:T(8,128)(2,1)S(1)} %collective-permute-done.1.f1, bf16[2,256,512]{2,1,0:T(8,128)(2,1)S(1)} %collective-permute-done.2.f2, ...), custom_call_target="tpu_custom_call" | custom-call | flops 1207959552 | bytes 6291456 | tf_op jit(solution)/shard_map/early/pallas_call | solution.py:112
  82.0 0.0 collective-permute-done.5
  82.0 0.0 collective-permute-done.7
  82.0 0.0 copy-start
  82.0 1.2 copy-done
  83.3 2.1 %late.1 = (bf16[4,64,1024]{2,1,0:T(8,128)(2,1)S(1)}, bf16[256,512]{1,0:T(8,128)(2,1)S(1)}, bf16[1024,512]{1,0:T(8,128)(2,1)S(1)}) custom-call(s32[4]{0:T(128)S(1)} %pad_add_fusion.place_ref, bf16[2,256,512]{2,1,0:T(8,128)(2,1)S(1)} %pad_maximum_fusion.f0, bf16[2,256,512]{2,1,0:T(8,128)(2,1)S(1)} %collective-permute-done.1.f1, ...), custom_call_target="tpu_custom_call", output_to_operand_aliasing={{2}: (9, {})} | custom-call | flops 536870912 | bytes 6291456 | tf_op jit(solution)/shard_map/late/pallas_call | solution.py:121
  85.3 1.9 %collective-permute-start.10 = (bf16[4,64,1024]{2,1,0:T(8,128)(2,1)S(1)}, bf16[4,64,1024]{2,1,0:T(8,128)(2,1)S(1)}, u32[]{:S(2)}, u32[]{:S(2)}) collective-permute-start(bf16[4,64,1024]{2,1,0:T(8,128)(2,1)S(1)} %get-tuple-element.18), channel_id=1, source_target_pairs={{0,1},{1,0},{2,3},{3,2},{4,5},{5,4},{6,7},{7,6},{8,9},{9,8},{10,11... | collective-permute-start | bytes 1572872 | tf_op jit(solution)/shard_map/ppermute | solution.py:203
  87.3 0.5 kept.1
  87.7 1.4 collective-permute-done.10
  89.1 1.0 add_convert_fusion
  90.1 5.2 %all-to-all-start.1 = ((bf16[4,64,1024]{2,1,0:T(8,128)(2,1)}), bf16[4,64,1024]{2,1,0:T(8,128)(2,1)S(1)}, u32[]{:S(2)}, u32[]{:S(2)}) async-start(bf16[4,64,1024]{2,1,0:T(8,128)(2,1)} %add_convert_fusion), calls=%async_computation.1 | async-start | bytes 1048576 | tf_op jit(solution)/shard_map/all_to_all | solution.py:229
  95.3 0.0 copy-start.6
  95.3 0.7 copy-done.6
  96.0 0.2 convert_reduce_fusion
  96.2 0.0 copy-start.2
  96.2 7.1 %all-to-all-done.1.parts_ref = bf16[4,64,1024]{2,1,0:T(8,128)(2,1)S(1)} async-done(((bf16[4,64,1024]{2,1,0:T(8,128)(2,1)}), bf16[4,64,1024]{2,1,0:T(8,128)(2,1)S(1)}, u32[]{:S(2)}, u32[]{:S(2)}) %all-to-all-start.1) | async-done | bytes 524320 | tf_op jit(solution)/shard_map/all_to_all | solution.py:229
  103.3 0.0 copy-done.2
  103.3 0.8 norm.1
  104.1 3.3 %all-to-all-start.2 = ((bf16[4,64,256]{2,1,0:T(8,128)(2,1)}), bf16[4,64,256]{2,1,0:T(8,128)(2,1)S(1)}, u32[]{:S(2)}, u32[]{:S(2)}) async-start(bf16[4,64,256]{2,1,0:T(8,128)(2,1)} %norm.1), calls=%async_computation.2 | async-start | bytes 262144 | tf_op jit(solution)/shard_map/all_to_all | solution.py:231
  107.5 0.1 select_convert_fusion
  107.6 4.5 %all-to-all-done.2 = bf16[4,64,256]{2,1,0:T(8,128)(2,1)S(1)} async-done(((bf16[4,64,256]{2,1,0:T(8,128)(2,1)}), bf16[4,64,256]{2,1,0:T(8,128)(2,1)S(1)}, u32[]{:S(2)}, u32[]{:S(2)}) %all-to-all-start.2) | async-done | bytes 131104 | tf_op jit(solution)/shard_map/all_to_all | solution.py:231
  112.1 0.3 convolution_convert_fusion
  112.4 0.0 copy-start.1
  112.4 0.1 reshape.70
  112.5 28.9 %all_to_all.20 = bf16[128,4,384]{2,1,0:T(4,128)(2,1)S(1)} all-to-all(bf16[128,4,384]{2,1,0:T(4,128)(2,1)S(1)} %reshape.70), channel_id=1, replica_groups=mesh['zh'=4,'x'=4,'yh'=4,'yl'=2,'zl'=2,'core'=2] {'yl','yh','x','zh'}, dimensions={0} | all-to-all | bytes 786432 | tf_op jit(solution)/shard_map/all_to_all | solution.py:249
  141.4 0.1 reshape.71.rows_ref
  141.5 0.0 copy-done.1
  141.5 2.7 %write.1 = bf16[2048,256]{1,0:T(8,128)(2,1)} custom-call(bf16[2048,256]{1,0:T(8,128)(2,1)S(1)} %copy-done.1, bf16[512,384]{1,0:T(8,128)(2,1)S(1)} %reshape.71.rows_ref), custom_call_target="tpu_custom_call" | custom-call | tf_op jit(solution)/shard_map/write/pallas_call | solution.py:186
  (5 shorter events, 0.1 us)
Async XLA Ops:
  1.8 16.3 %copy-start.5 = (bf16[256,512]{1,0:T(8,128)(2,1)S(1)}, bf16[256,512]{1,0:T(8,128)(2,1)}, u32[]{:S(2)}) copy-start(bf16[256,512]{1,0:T(8,128)(2,1)} %param.7) | copy-start | bytes 786436
  1.8 40.9 %all-to-all-start = ((bf16[32,24,512]{2,1,0:T(8,128)(2,1)}), bf16[32,24,512]{2,1,0:T(8,128)(2,1)S(1)}, u32[]{:S(2)}, u32[]{:S(2)}) async-start(bf16[32,24,512]{2,1,0:T(8,128)(2,1)} %bitcast.5), calls=%async_computation | async-start | bytes 1572864 | tf_op jit(solution)/shard_map/all_to_all | solution.py:212
  18.1 3.4 %collective-permute-start = (bf16[256,512]{1,0:T(8,128)(2,1)S(1)}, bf16[256,512]{1,0:T(8,128)(2,1)S(1)}, u32[]{:S(2)}, u32[]{:S(2)}) collective-permute-start(bf16[256,512]{1,0:T(8,128)(2,1)S(1)} %copy-done.5), channel_id=1, source_target_pairs={{0,1},{1,0},{2,3},{3,2},{4,5},{5,4},{6,7},{7,6},{8,9},{9,8},{10,11... | collective-permute-start | bytes 786440 | tf_op jit(solution)/shard_map/ppermute | solution.py:203
  42.7 15.4 %collective-permute-start.1 = (bf16[2,256,512]{2,1,0:T(8,128)(2,1)S(1)}, bf16[2,256,512]{2,1,0:T(8,128)(2,1)S(1)}, u32[]{:S(2)}, u32[]{:S(2)}) collective-permute-start(bf16[2,256,512]{2,1,0:T(8,128)(2,1)S(1)} %pad_maximum_fusion.f0), channel_id=1, source_target_pairs={{0,4},{4,0},{1,5},{5,1},{2,6},{6,2},{3,7},{7,3},{8,12},{12,8},{9,1... | collective-permute-start | bytes 1572872 | tf_op jit(solution)/shard_map/ppermute | solution.py:203
  45.4 15.1 %collective-permute-start.4 = (bf16[16,24,512]{2,1,0:T(8,128)(2,1)}, bf16[16,24,512]{2,1,0:T(8,128)(2,1)}, u32[]{:S(2)}, u32[]{:S(2)}) collective-permute-start(bf16[16,24,512]{2,1,0:T(8,128)(2,1)} %get-tuple-element.22), channel_id=1, source_target_pairs={{0,32},{32,64},{64,96},{96,0},{1,33},{33,65},{65,97},{97,1},{2,34}... | collective-permute-start | bytes 1179656 | tf_op jit(solution)/shard_map/ppermute | solution.py:199
  48.8 16.6 %collective-permute-start.6 = (bf16[16,24,512]{2,1,0:T(8,128)(2,1)S(1)}, bf16[16,24,512]{2,1,0:T(8,128)(2,1)}, u32[]{:S(2)}, u32[]{:S(2)}) collective-permute-start(bf16[16,24,512]{2,1,0:T(8,128)(2,1)S(1)} %get-tuple-element.21), channel_id=1, source_target_pairs={{0,96},{32,0},{64,32},{96,64},{1,97},{33,1},{65,33},{97,65},{2,98}... | collective-permute-start | bytes 1179656 | tf_op jit(solution)/shard_map/ppermute | solution.py:199
  52.5 14.9 %collective-permute-start.8 = (bf16[16,24,512]{2,1,0:T(8,128)(2,1)S(1)}, bf16[16,24,512]{2,1,0:T(8,128)(2,1)S(1)}, u32[]{:S(2)}, u32[]{:S(2)}) collective-permute-start(bf16[16,24,512]{2,1,0:T(8,128)(2,1)S(1)} %get-tuple-element.21), channel_id=1, source_target_pairs={{0,32},{32,64},{64,96},{96,0},{1,33},{33,65},{65,97},{97,1},{2,34}... | collective-permute-start | bytes 1179656 | tf_op jit(solution)/shard_map/ppermute | solution.py:199
  54.7 19.5 %collective-permute-start.2 = (bf16[2,256,512]{2,1,0:T(8,128)(2,1)S(1)}, bf16[2,256,512]{2,1,0:T(8,128)(2,1)S(1)}, u32[]{:S(2)}, u32[]{:S(2)}) collective-permute-start(bf16[2,256,512]{2,1,0:T(8,128)(2,1)S(1)} %pad_maximum_fusion.f0), channel_id=1, source_target_pairs={{0,2},{2,0},{1,3},{3,1},{4,6},{6,4},{5,7},{7,5},{8,10},{10,8},{9,1... | collective-permute-start | bytes 1572872 | tf_op jit(solution)/shard_map/ppermute | solution.py:203
  58.1 19.8 %collective-permute-start.3 = (bf16[2,256,512]{2,1,0:T(8,128)(2,1)S(1)}, bf16[2,256,512]{2,1,0:T(8,128)(2,1)S(1)}, u32[]{:S(2)}, u32[]{:S(2)}) collective-permute-start(bf16[2,256,512]{2,1,0:T(8,128)(2,1)S(1)} %collective-permute-done.1.f1), channel_id=1, source_target_pairs={{0,2},{2,0},{1,3},{3,1},{4,6},{6,4},{5,7},{7,5},{8,10},{10,8},{9,1... | collective-permute-start | bytes 1572872 | tf_op jit(solution)/shard_map/ppermute | solution.py:203
  60.5 13.6 %collective-permute-start.9 = (bf16[16,24,512]{2,1,0:T(8,128)(2,1)}, bf16[16,24,512]{2,1,0:T(8,128)(2,1)}, u32[]{:S(2)}, u32[]{:S(2)}) collective-permute-start(bf16[16,24,512]{2,1,0:T(8,128)(2,1)} %get-tuple-element.22), channel_id=1, source_target_pairs={{0,96},{32,0},{64,32},{96,64},{1,97},{33,1},{65,33},{97,65},{2,98}... | collective-permute-start | bytes 1179656 | tf_op jit(solution)/shard_map/ppermute | solution.py:199
  65.4 16.6 %collective-permute-start.5 = (bf16[16,24,512]{2,1,0:T(8,128)(2,1)}, bf16[16,24,512]{2,1,0:T(8,128)(2,1)S(1)}, u32[]{:S(2)}, u32[]{:S(2)}) collective-permute-start(bf16[16,24,512]{2,1,0:T(8,128)(2,1)} %collective-permute-done.4), channel_id=1, source_target_pairs={{0,32},{32,64},{64,96},{96,0},{1,33},{33,65},{65,97},{97,1},{2,34}... | collective-permute-start | bytes 1179656 | tf_op jit(solution)/shard_map/ppermute | solution.py:199
  67.4 0.8 copy-start.3
  68.1 13.9 %collective-permute-start.7 = (bf16[16,24,512]{2,1,0:T(8,128)(2,1)}, bf16[16,24,512]{2,1,0:T(8,128)(2,1)}, u32[]{:S(2)}, u32[]{:S(2)}) collective-permute-start(bf16[16,24,512]{2,1,0:T(8,128)(2,1)} %collective-permute-done.6), channel_id=1, source_target_pairs={{0,96},{32,0},{64,32},{96,64},{1,97},{33,1},{65,33},{97,65},{2,98}... | collective-permute-start | bytes 1179656 | tf_op jit(solution)/shard_map/ppermute | solution.py:199
  73.3 0.7 copy-start.7
  77.8 1.0 copy-start.4
  82.0 1.2 copy-start
  85.3 3.8 %collective-permute-start.10 = (bf16[4,64,1024]{2,1,0:T(8,128)(2,1)S(1)}, bf16[4,64,1024]{2,1,0:T(8,128)(2,1)S(1)}, u32[]{:S(2)}, u32[]{:S(2)}) collective-permute-start(bf16[4,64,1024]{2,1,0:T(8,128)(2,1)S(1)} %get-tuple-element.18), channel_id=1, source_target_pairs={{0,1},{1,0},{2,3},{3,2},{4,5},{5,4},{6,7},{7,6},{8,9},{9,8},{10,11... | collective-permute-start | bytes 1572872 | tf_op jit(solution)/shard_map/ppermute | solution.py:203
  90.1 13.2 %all-to-all-start.1 = ((bf16[4,64,1024]{2,1,0:T(8,128)(2,1)}), bf16[4,64,1024]{2,1,0:T(8,128)(2,1)S(1)}, u32[]{:S(2)}, u32[]{:S(2)}) async-start(bf16[4,64,1024]{2,1,0:T(8,128)(2,1)} %add_convert_fusion), calls=%async_computation.1 | async-start | bytes 1048576 | tf_op jit(solution)/shard_map/all_to_all | solution.py:229
  95.3 0.7 copy-start.6
  96.2 7.1 %copy-start.2 = (f32[1024]{0:T(1024)S(1)}, f32[1024]{0:T(1024)}, u32[]{:S(2)}) copy-start(f32[1024]{0:T(1024)} %param.12) | copy-start | bytes 12292
  104.1 7.9 %all-to-all-start.2 = ((bf16[4,64,256]{2,1,0:T(8,128)(2,1)}), bf16[4,64,256]{2,1,0:T(8,128)(2,1)S(1)}, u32[]{:S(2)}, u32[]{:S(2)}) async-start(bf16[4,64,256]{2,1,0:T(8,128)(2,1)} %norm.1), calls=%async_computation.2 | async-start | bytes 262144 | tf_op jit(solution)/shard_map/all_to_all | solution.py:231
  112.4 29.1 %copy-start.1 = (bf16[2048,256]{1,0:T(8,128)(2,1)S(1)}, bf16[2048,256]{1,0:T(8,128)(2,1)}, u32[]{:S(2)}) copy-start(bf16[2048,256]{1,0:T(8,128)(2,1)} %table_ref.1) | copy-start | bytes 3145732

commit v6 on v5

--- a/solution.py
+++ b/solution.py
@@ -55,22 +55,20 @@
     return act
 
 
-def early_kernel(place_ref, f0, f1, f2, f3, mine, la, lb, ra, rb, act_ref, w_all):
-    x0, tp = place_ref[0], place_ref[1]
-    feats = ((f0, f1), (f2, f3))
-    act = [None, None]
-    for offset, first, second in ((0, mine.at[0:2], mine.at[2:4]), (3, la, lb), (1, ra, rb)):
-        act = add_block(x0, tp, offset, first, second, feats, act, w_all)
-    for dy in range(2):
-        act_ref[dy] = act[dy]
-
-
-def late_kernel(
-    place_ref, f0, f1, f2, f3, fa, fb, bias_ref, act_ref, old_ref, give_ref, kept_ref, w_all, hid
+def tower_kernel(
+    place_ref, f0, f1, f2, f3, mine, left, ra, rb, fa, fb, bias_ref, give_ref, kept_ref, w_all, hid
 ):
     x0, tp, yl, core = (place_ref[i] for i in range(4))
     feats = ((f0, f1), (f2, f3))
-    act = add_block(x0, tp, 2, fa, fb, feats, [act_ref[0], act_ref[1]], w_all)
+    act = [None, None]
+    blocks = (
+        (0, mine.at[0:2], mine.at[2:4]),
+        (3, left.at[0:2], left.at[2:4]),
+        (1, ra, rb),
+        (2, fa, fb),
+    )
+    for offset, first, second in blocks:
+        act = add_block(x0, tp, offset, first, second, feats, act, w_all)
     for dy in range(2):
         v = act[dy] + bias_ref[...]
         hid[dy] = (v * (1.0 / (1.0 + jnp.exp(-v)))).astype(BF16)
@@ -109,26 +107,15 @@
     params = pltpu.CompilerParams(vmem_limit_bytes=48 << 20)
     part = jax.ShapeDtypeStruct((4, 64, D_OUT), BF16)
     w_shape = jax.ShapeDtypeStruct((D_OUT, HID), BF16)
-    act, w_all = pl.pallas_call(
-        early_kernel,
-        out_shape=(jax.ShapeDtypeStruct((2, SRC, HID), F32), w_shape),
-        in_specs=[SMEM] + [VMEM] * 9,
-        out_specs=(VMEM, VMEM),
-        compiler_params=params,
-        cost_estimate=cost(6 * SRC * 1536 * HID, 6 << 20),
-        name="early",
-    )(place, *feats, *weights[:5])
     give, kept, w_all = pl.pallas_call(
-        late_kernel,
+        tower_kernel,
         out_shape=(part, jax.ShapeDtypeStruct((SRC, HID), BF16), w_shape),
-        in_specs=[SMEM] + [VMEM] * 9,
+        in_specs=[SMEM] + [VMEM] * 11,
         out_specs=(VMEM, VMEM, VMEM),
         scratch_shapes=[pltpu.VMEM((2, SRC, HID), BF16)],
-        input_output_aliases={9: 2},
         compiler_params=params,
-        cost_estimate=cost(4 * SRC * 1024 * HID, 6 << 20),
-        name="late",
-    )(place, *feats, *weights[5:], bias, act, w_all)
+        name="tower",
+    )(place, *feats, *weights, bias)
     keep = pl.pallas_call(
         kept_kernel,
         out_shape=part,
@@ -213,15 +200,14 @@
     pair = jnp.stack([features, swap(features, "core")])
     mine, pair = lax.optimization_barrier((mine, pair))
     near = swap(pair, "yl")
-    la, rb = along_x(mine[:16], 1), along_x(mine[16:], -1)
-    lb, ra = along_x(mine[16:], 1), along_x(mine[:16], -1)
-    fa, fb = along_x(la, 1), along_x(rb, -1)
+    left = along_x(mine, 1)
+    rb, ra = along_x(mine[16:], -1), along_x(mine[:16], -1)
+    fa, fb = along_x(left[:16], 1), along_x(rb, -1)
 
     over = swap(pair, "zl")
     feats = (pair, near, over, swap(near, "zl"))
 
-    halves = [each.reshape(2, 4, 2, 24, HID) for each in (la, lb, ra, rb, fa, fb)]
-    weights = [mine.reshape(4, 4, 2, 24, HID)] + halves
+    weights = [each.reshape(-1, 4, 2, 24, HID) for each in (mine, left, ra, rb, fa, fb)]
     bias = lax.dynamic_slice_in_dim(bias_in, index["yl"] * HID, HID).reshape(1, HID)
 
     give, keep = tower(place, feats, weights, bias)

time: 145 us -> 146 us (level)
  the two profiles are of different devices: /device:TPU:8 before, /device:TPU:1 now
where the time goes in v6:
time: 146 us; the launch traced here: 143 us
  starting transfers between devices  60.3 us (41%)
  waiting for transfers between devices  37.9 us (26%)
  blocking collectives  28.7 us (20%)
  Pallas kernels  8.13 us (6%)
  local copies, waits for them, and re-layouts  5.43 us (4%)
  other arithmetic  2.24 us (2%)
    all_to_all x1, blocking collectives, local(): lax.all_to_all(packed.reshape(OWNERS, CAP, SHARE + META), ROUTE, split_ax...  28.7 us
    ppermute x5, starting transfers between devices, swap(): return lax.ppermute(block, axis, [(0, 1), (1, 0)])  20.8 us
    all_to_all x1, waiting for transfers between devices, local(): mine = lax.all_to_all(w, PLANE, split_axis=0, concat_axis=0, tiled=True)  17.8 us
    all_to_all x1, starting transfers between devices, local(): mine = lax.all_to_all(w, PLANE, split_axis=0, concat_axis=0, tiled=True)  16.6 us
    ppermute x5, starting transfers between devices, along_x(): return lax.ppermute(block, 'x', [(i, (i + step) % 4) for i in range(4)])  15.1 us
    all_to_all x1, waiting for transfers between devices, local(): lax.all_to_all(chip, ('zl', 'yl'), split_axis=0, concat_axis=0, tiled=True)  7.09 us
    ppermute x5, waiting for transfers between devices, along_x(): return lax.ppermute(block, 'x', [(i, (i + step) % 4) for i in range(4)])  7.08 us
    all_to_all x1, starting transfers between devices, local(): lax.all_to_all(columns, TP, split_axis=0, concat_axis=0, tiled=True)  4.26 us
  transfers between devices with their start and end apart: 13, of which 7 were waited for; matrix products, arithmetic and copies ran while one was open for 1% of the time, Pallas kernels for 0%

profile of v6, /device:TPU:1, one launch (start us, length us, event | category | flops | bytes accessed | tf_op | source)
XLA Modules:
  0.0 143.2 jit_solution(17884245180183578239)
XLA Ops:
  0.0 0.8 pad_maximum_fusion.1
  0.8 1.0 broadcast_in_dim.32
  1.8 0.0 copy-start.3
  1.8 16.6 %all-to-all-start = ((bf16[32,24,512]{2,1,0:T(8,128)(2,1)}), bf16[32,24,512]{2,1,0:T(8,128)(2,1)S(1)}, u32[]{:S(2)}, u32[]{:S(2)}) async-start(bf16[32,24,512]{2,1,0:T(8,128)(2,1)} %bitcast.5), calls=%async_computation | async-start | bytes 1572864 | tf_op jit(solution)/shard_map/all_to_all | solution.py:199
  18.4 0.0 copy-done.3
  18.4 2.9 %collective-permute-start = (bf16[256,512]{1,0:T(8,128)(2,1)S(1)}, bf16[256,512]{1,0:T(8,128)(2,1)S(1)}, u32[]{:S(2)}, u32[]{:S(2)}) collective-permute-start(bf16[256,512]{1,0:T(8,128)(2,1)S(1)} %copy-done.3), channel_id=1, source_target_pairs={{0,1},{1,0},{2,3},{3,2},{4,5},{5,4},{6,7},{7,6},{8,9},{9,8},{10,11... | collective-permute-start | bytes 786440 | tf_op jit(solution)/shard_map/ppermute | solution.py:190
  21.3 1.1 collective-permute-done
  22.5 0.1 pad_maximum_fusion.f0
  22.5 17.8 %all-to-all-done = bf16[32,24,512]{2,1,0:T(8,128)(2,1)S(1)} async-done(((bf16[32,24,512]{2,1,0:T(8,128)(2,1)}), bf16[32,24,512]{2,1,0:T(8,128)(2,1)S(1)}, u32[]{:S(2)}, u32[]{:S(2)}) %all-to-all-start) | async-done | bytes 786464 | tf_op jit(solution)/shard_map/all_to_all | solution.py:199
  40.3 3.1 %collective-permute-start.4 = (bf16[32,24,512]{2,1,0:T(8,128)(2,1)S(1)}, bf16[32,24,512]{2,1,0:T(8,128)(2,1)S(1)}, u32[]{:S(2)}, u32[]{:S(2)}) collective-permute-start(bf16[32,24,512]{2,1,0:T(8,128)(2,1)S(1)} %all-to-all-done), channel_id=1, source_target_pairs={{0,32},{32,64},{64,96},{96,0},{1,33},{33,65},{65,97},{97,1},{2,34}... | collective-permute-start | bytes 2359304 | tf_op jit(solution)/shard_map/ppermute | solution.py:186
  43.4 3.6 %collective-permute-start.1 = (bf16[2,256,512]{2,1,0:T(8,128)(2,1)S(1)}, bf16[2,256,512]{2,1,0:T(8,128)(2,1)S(1)}, u32[]{:S(2)}, u32[]{:S(2)}) collective-permute-start(bf16[2,256,512]{2,1,0:T(8,128)(2,1)S(1)} %pad_maximum_fusion.f0), channel_id=1, source_target_pairs={{0,4},{4,0},{1,5},{5,1},{2,6},{6,2},{3,7},{7,3},{8,12},{12,8},{9,1... | collective-permute-start | bytes 1572872 | tf_op jit(solution)/shard_map/ppermute | solution.py:190
  47.1 0.8 fusion.6
  47.9 3.4 %collective-permute-start.6 = (bf16[16,24,512]{2,1,0:T(8,128)(2,1)S(1)}, bf16[16,24,512]{2,1,0:T(8,128)(2,1)S(1)}, u32[]{:S(2)}, u32[]{:S(2)}) collective-permute-start(bf16[16,24,512]{2,1,0:T(8,128)(2,1)S(1)} %get-tuple-element.17), channel_id=1, source_target_pairs={{0,96},{32,0},{64,32},{96,64},{1,97},{33,1},{65,33},{97,65},{2,98}... | collective-permute-start | bytes 1179656 | tf_op jit(solution)/shard_map/ppermute | solution.py:186
  51.2 3.0 %collective-permute-start.2 = (bf16[2,256,512]{2,1,0:T(8,128)(2,1)S(1)}, bf16[2,256,512]{2,1,0:T(8,128)(2,1)S(1)}, u32[]{:S(2)}, u32[]{:S(2)}) collective-permute-start(bf16[2,256,512]{2,1,0:T(8,128)(2,1)S(1)} %pad_maximum_fusion.f0), channel_id=1, source_target_pairs={{0,2},{2,0},{1,3},{3,1},{4,6},{6,4},{5,7},{7,5},{8,10},{10,8},{9,1... | collective-permute-start | bytes 1572872 | tf_op jit(solution)/shard_map/ppermute | solution.py:190
  54.3 1.3 collective-permute-done.1.f1
  55.5 2.9 %collective-permute-start.3 = (bf16[2,256,512]{2,1,0:T(8,128)(2,1)S(1)}, bf16[2,256,512]{2,1,0:T(8,128)(2,1)}, u32[]{:S(2)}, u32[]{:S(2)}) collective-permute-start(bf16[2,256,512]{2,1,0:T(8,128)(2,1)S(1)} %collective-permute-done.1.f1), channel_id=1, source_target_pairs={{0,2},{2,0},{1,3},{3,1},{4,6},{6,4},{5,7},{7,5},{8,10},{10,8},{9,1... | collective-permute-start | bytes 1572872 | tf_op jit(solution)/shard_map/ppermute | solution.py:190
  58.5 3.4 %collective-permute-start.5 = (bf16[16,24,512]{2,1,0:T(8,128)(2,1)}, bf16[16,24,512]{2,1,0:T(8,128)(2,1)}, u32[]{:S(2)}, u32[]{:S(2)}) collective-permute-start(bf16[16,24,512]{2,1,0:T(8,128)(2,1)} %get-tuple-element.18), channel_id=1, source_target_pairs={{0,96},{32,0},{64,32},{96,64},{1,97},{33,1},{65,33},{97,65},{2,98}... | collective-permute-start | bytes 1179656 | tf_op jit(solution)/shard_map/ppermute | solution.py:186
  61.9 0.0 collective-permute-done.6
  61.9 3.2 %collective-permute-start.8 = (bf16[16,24,512]{2,1,0:T(8,128)(2,1)S(1)}, bf16[16,24,512]{2,1,0:T(8,128)(2,1)}, u32[]{:S(2)}, u32[]{:S(2)}) collective-permute-start(bf16[16,24,512]{2,1,0:T(8,128)(2,1)S(1)} %collective-permute-done.6), channel_id=1, source_target_pairs={{0,96},{32,0},{64,32},{96,64},{1,97},{33,1},{65,33},{97,65},{2,98}... | collective-permute-start | bytes 1179656 | tf_op jit(solution)/shard_map/ppermute | solution.py:186
  65.1 0.0 collective-permute-done.4
  65.1 0.8 slice.12
  65.9 2.1 %collective-permute-start.7 = (bf16[16,24,512]{2,1,0:T(8,128)(2,1)}, bf16[16,24,512]{2,1,0:T(8,128)(2,1)}, u32[]{:S(2)}, u32[]{:S(2)}) collective-permute-start(bf16[16,24,512]{2,1,0:T(8,128)(2,1)} %slice.12), channel_id=1, source_target_pairs={{0,32},{32,64},{64,96},{96,0},{1,33},{33,65},{65,97},{97,1},{2,34}... | collective-permute-start | bytes 1179656 | tf_op jit(solution)/shard_map/ppermute | solution.py:186
  68.0 0.0 copy-start.5
  68.0 0.7 copy-done.5
  68.7 0.1 dynamic_slice.3
  68.7 0.1 pad_add_fusion.place_ref
  68.8 0.0 collective-permute-done.5
  68.8 0.0 collective-permute-done.2.f2
  68.8 6.2 %collective-permute-done.8 = bf16[16,24,512]{2,1,0:T(8,128)(2,1)} collective-permute-done((bf16[16,24,512]{2,1,0:T(8,128)(2,1)S(1)}, bf16[16,24,512]{2,1,0:T(8,128)(2,1)}, u32[]{:S(2)}, u32[]{:S(2)}) %collective-permute-start.8) | collective-permute-done | bytes 393248 | tf_op jit(solution)/shard_map/ppermute | solution.py:186
  75.0 0.0 collective-permute-done.3.f3
  75.0 0.9 collective-permute-done.7
  75.9 4.1 %tower.1 = (bf16[4,64,1024]{2,1,0:T(8,128)(2,1)S(1)}, bf16[256,512]{1,0:T(8,128)(2,1)S(1)}, bf16[1024,512]{1,0:T(8,128)(2,1)}) custom-call(s32[4]{0:T(128)S(1)} %pad_add_fusion.place_ref, bf16[2,256,512]{2,1,0:T(8,128)(2,1)S(1)} %pad_maximum_fusion.f0, bf16[2,256,512]{2,1,0:T(8,128)(2,1)S(1)} %collective-permute-done.1.f1, ...), custom_call_target="tpu_custom_call" | custom-call | tf_op jit(solution)/shard_map/tower/pallas_call | solution.py:110
  80.0 8.3 %collective-permute-start.9 = (bf16[4,64,1024]{2,1,0:T(8,128)(2,1)S(1)}, bf16[4,64,1024]{2,1,0:T(8,128)(2,1)S(1)}, u32[]{:S(2)}, u32[]{:S(2)}) collective-permute-start(bf16[4,64,1024]{2,1,0:T(8,128)(2,1)S(1)} %get-tuple-element.14), channel_id=1, source_target_pairs={{0,1},{1,0},{2,3},{3,2},{4,5},{5,4},{6,7},{7,6},{8,9},{9,8},{10,11... | collective-permute-start | bytes 1572872 | tf_op jit(solution)/shard_map/ppermute | solution.py:190
  88.3 0.0 copy-start
  88.4 1.2 copy-done
  89.6 0.5 kept.1
  90.0 0.0 collective-permute-done.9
  90.1 1.0 add_convert_fusion
  91.0 3.5 %all-to-all-start.1 = ((bf16[4,64,1024]{2,1,0:T(8,128)(2,1)}), bf16[4,64,1024]{2,1,0:T(8,128)(2,1)S(1)}, u32[]{:S(2)}, u32[]{:S(2)}) async-start(bf16[4,64,1024]{2,1,0:T(8,128)(2,1)} %add_convert_fusion), calls=%async_computation.1 | async-start | bytes 1048576 | tf_op jit(solution)/shard_map/all_to_all | solution.py:215
  94.5 0.0 copy-start.4
  94.6 0.7 copy-done.4
  95.2 0.2 convert_reduce_fusion
  95.4 0.0 copy-start.2
  95.4 7.1 %all-to-all-done.1.parts_ref = bf16[4,64,1024]{2,1,0:T(8,128)(2,1)S(1)} async-done(((bf16[4,64,1024]{2,1,0:T(8,128)(2,1)}), bf16[4,64,1024]{2,1,0:T(8,128)(2,1)S(1)}, u32[]{:S(2)}, u32[]{:S(2)}) %all-to-all-start.1) | async-done | bytes 524320 | tf_op jit(solution)/shard_map/all_to_all | solution.py:215
  102.5 0.0 copy-done.2
  102.5 0.8 norm.1
  103.3 4.3 %all-to-all-start.2 = ((bf16[4,64,256]{2,1,0:T(8,128)(2,1)}), bf16[4,64,256]{2,1,0:T(8,128)(2,1)S(1)}, u32[]{:S(2)}, u32[]{:S(2)}) async-start(bf16[4,64,256]{2,1,0:T(8,128)(2,1)} %norm.1), calls=%async_computation.2 | async-start | bytes 262144 | tf_op jit(solution)/shard_map/all_to_all | solution.py:217
  107.6 0.1 select_convert_fusion
  107.7 3.5 %all-to-all-done.2 = bf16[4,64,256]{2,1,0:T(8,128)(2,1)S(1)} async-done(((bf16[4,64,256]{2,1,0:T(8,128)(2,1)}), bf16[4,64,256]{2,1,0:T(8,128)(2,1)S(1)}, u32[]{:S(2)}, u32[]{:S(2)}) %all-to-all-start.2) | async-done | bytes 131104 | tf_op jit(solution)/shard_map/all_to_all | solution.py:217
  111.2 0.3 convolution_convert_fusion
  111.5 0.0 copy-start.1
  111.5 0.1 reshape.66
  111.6 28.7 %all_to_all.20 = bf16[128,4,384]{2,1,0:T(4,128)(2,1)S(1)} all-to-all(bf16[128,4,384]{2,1,0:T(4,128)(2,1)S(1)} %reshape.66), channel_id=1, replica_groups=mesh['zh'=4,'x'=4,'yh'=4,'yl'=2,'zl'=2,'core'=2] {'yl','yh','x','zh'}, dimensions={0} | all-to-all | bytes 786432 | tf_op jit(solution)/shard_map/all_to_all | solution.py:235
  140.4 0.1 reshape.67.rows_ref
  140.5 0.0 copy-done.1
  140.5 2.7 %write.1 = bf16[2048,256]{1,0:T(8,128)(2,1)} custom-call(bf16[2048,256]{1,0:T(8,128)(2,1)S(1)} %copy-done.1, bf16[512,384]{1,0:T(8,128)(2,1)S(1)} %reshape.67.rows_ref), custom_call_target="tpu_custom_call" | custom-call | tf_op jit(solution)/shard_map/write/pallas_call | solution.py:173
  (5 shorter events, 0.1 us)
Async XLA Ops:
  1.8 16.6 %copy-start.3 = (bf16[256,512]{1,0:T(8,128)(2,1)S(1)}, bf16[256,512]{1,0:T(8,128)(2,1)}, u32[]{:S(2)}) copy-start(bf16[256,512]{1,0:T(8,128)(2,1)} %param.7) | copy-start | bytes 786436
  1.8 38.5 %all-to-all-start = ((bf16[32,24,512]{2,1,0:T(8,128)(2,1)}), bf16[32,24,512]{2,1,0:T(8,128)(2,1)S(1)}, u32[]{:S(2)}, u32[]{:S(2)}) async-start(bf16[32,24,512]{2,1,0:T(8,128)(2,1)} %bitcast.5), calls=%async_computation | async-start | bytes 1572864 | tf_op jit(solution)/shard_map/all_to_all | solution.py:199
  18.4 4.0 %collective-permute-start = (bf16[256,512]{1,0:T(8,128)(2,1)S(1)}, bf16[256,512]{1,0:T(8,128)(2,1)S(1)}, u32[]{:S(2)}, u32[]{:S(2)}) collective-permute-start(bf16[256,512]{1,0:T(8,128)(2,1)S(1)} %copy-done.3), channel_id=1, source_target_pairs={{0,1},{1,0},{2,3},{3,2},{4,5},{5,4},{6,7},{7,6},{8,9},{9,8},{10,11... | collective-permute-start | bytes 786440 | tf_op jit(solution)/shard_map/ppermute | solution.py:190
  40.3 24.8 %collective-permute-start.4 = (bf16[32,24,512]{2,1,0:T(8,128)(2,1)S(1)}, bf16[32,24,512]{2,1,0:T(8,128)(2,1)S(1)}, u32[]{:S(2)}, u32[]{:S(2)}) collective-permute-start(bf16[32,24,512]{2,1,0:T(8,128)(2,1)S(1)} %all-to-all-done), channel_id=1, source_target_pairs={{0,32},{32,64},{64,96},{96,0},{1,33},{33,65},{65,97},{97,1},{2,34}... | collective-permute-start | bytes 2359304 | tf_op jit(solution)/shard_map/ppermute | solution.py:186
  43.4 12.1 %collective-permute-start.1 = (bf16[2,256,512]{2,1,0:T(8,128)(2,1)S(1)}, bf16[2,256,512]{2,1,0:T(8,128)(2,1)S(1)}, u32[]{:S(2)}, u32[]{:S(2)}) collective-permute-start(bf16[2,256,512]{2,1,0:T(8,128)(2,1)S(1)} %pad_maximum_fusion.f0), channel_id=1, source_target_pairs={{0,4},{4,0},{1,5},{5,1},{2,6},{6,2},{3,7},{7,3},{8,12},{12,8},{9,1... | collective-permute-start | bytes 1572872 | tf_op jit(solution)/shard_map/ppermute | solution.py:190
  47.9 14.0 %collective-permute-start.6 = (bf16[16,24,512]{2,1,0:T(8,128)(2,1)S(1)}, bf16[16,24,512]{2,1,0:T(8,128)(2,1)S(1)}, u32[]{:S(2)}, u32[]{:S(2)}) collective-permute-start(bf16[16,24,512]{2,1,0:T(8,128)(2,1)S(1)} %get-tuple-element.17), channel_id=1, source_target_pairs={{0,96},{32,0},{64,32},{96,64},{1,97},{33,1},{65,33},{97,65},{2,98}... | collective-permute-start | bytes 1179656 | tf_op jit(solution)/shard_map/ppermute | solution.py:186
  51.2 17.6 %collective-permute-start.2 = (bf16[2,256,512]{2,1,0:T(8,128)(2,1)S(1)}, bf16[2,256,512]{2,1,0:T(8,128)(2,1)S(1)}, u32[]{:S(2)}, u32[]{:S(2)}) collective-permute-start(bf16[2,256,512]{2,1,0:T(8,128)(2,1)S(1)} %pad_maximum_fusion.f0), channel_id=1, source_target_pairs={{0,2},{2,0},{1,3},{3,1},{4,6},{6,4},{5,7},{7,5},{8,10},{10,8},{9,1... | collective-permute-start | bytes 1572872 | tf_op jit(solution)/shard_map/ppermute | solution.py:190
  55.5 19.5 %collective-permute-start.3 = (bf16[2,256,512]{2,1,0:T(8,128)(2,1)S(1)}, bf16[2,256,512]{2,1,0:T(8,128)(2,1)}, u32[]{:S(2)}, u32[]{:S(2)}) collective-permute-start(bf16[2,256,512]{2,1,0:T(8,128)(2,1)S(1)} %collective-permute-done.1.f1), channel_id=1, source_target_pairs={{0,2},{2,0},{1,3},{3,1},{4,6},{6,4},{5,7},{7,5},{8,10},{10,8},{9,1... | collective-permute-start | bytes 1572872 | tf_op jit(solution)/shard_map/ppermute | solution.py:190
  58.5 10.3 %collective-permute-start.5 = (bf16[16,24,512]{2,1,0:T(8,128)(2,1)}, bf16[16,24,512]{2,1,0:T(8,128)(2,1)}, u32[]{:S(2)}, u32[]{:S(2)}) collective-permute-start(bf16[16,24,512]{2,1,0:T(8,128)(2,1)} %get-tuple-element.18), channel_id=1, source_target_pairs={{0,96},{32,0},{64,32},{96,64},{1,97},{33,1},{65,33},{97,65},{2,98}... | collective-permute-start | bytes 1179656 | tf_op jit(solution)/shard_map/ppermute | solution.py:186
  61.9 13.1 %collective-permute-start.8 = (bf16[16,24,512]{2,1,0:T(8,128)(2,1)S(1)}, bf16[16,24,512]{2,1,0:T(8,128)(2,1)}, u32[]{:S(2)}, u32[]{:S(2)}) collective-permute-start(bf16[16,24,512]{2,1,0:T(8,128)(2,1)S(1)} %collective-permute-done.6), channel_id=1, source_target_pairs={{0,96},{32,0},{64,32},{96,64},{1,97},{33,1},{65,33},{97,65},{2,98}... | collective-permute-start | bytes 1179656 | tf_op jit(solution)/shard_map/ppermute | solution.py:186
  65.9 10.0 %collective-permute-start.7 = (bf16[16,24,512]{2,1,0:T(8,128)(2,1)}, bf16[16,24,512]{2,1,0:T(8,128)(2,1)}, u32[]{:S(2)}, u32[]{:S(2)}) collective-permute-start(bf16[16,24,512]{2,1,0:T(8,128)(2,1)} %slice.12), channel_id=1, source_target_pairs={{0,32},{32,64},{64,96},{96,0},{1,33},{33,65},{65,97},{97,1},{2,34}... | collective-permute-start | bytes 1179656 | tf_op jit(solution)/shard_map/ppermute | solution.py:186
  68.0 0.7 copy-start.5
  80.0 10.1 %collective-permute-start.9 = (bf16[4,64,1024]{2,1,0:T(8,128)(2,1)S(1)}, bf16[4,64,1024]{2,1,0:T(8,128)(2,1)S(1)}, u32[]{:S(2)}, u32[]{:S(2)}) collective-permute-start(bf16[4,64,1024]{2,1,0:T(8,128)(2,1)S(1)} %get-tuple-element.14), channel_id=1, source_target_pairs={{0,1},{1,0},{2,3},{3,2},{4,5},{5,4},{6,7},{7,6},{8,9},{9,8},{10,11... | collective-permute-start | bytes 1572872 | tf_op jit(solution)/shard_map/ppermute | solution.py:190
  88.3 1.2 copy-start
  91.0 11.5 %all-to-all-start.1 = ((bf16[4,64,1024]{2,1,0:T(8,128)(2,1)}), bf16[4,64,1024]{2,1,0:T(8,128)(2,1)S(1)}, u32[]{:S(2)}, u32[]{:S(2)}) async-start(bf16[4,64,1024]{2,1,0:T(8,128)(2,1)} %add_convert_fusion), calls=%async_computation.1 | async-start | bytes 1048576 | tf_op jit(solution)/shard_map/all_to_all | solution.py:215
  94.5 0.7 copy-start.4
  95.4 7.1 %copy-start.2 = (f32[1024]{0:T(1024)S(1)}, f32[1024]{0:T(1024)}, u32[]{:S(2)}) copy-start(f32[1024]{0:T(1024)} %param.12) | copy-start | bytes 12292
  103.3 7.9 %all-to-all-start.2 = ((bf16[4,64,256]{2,1,0:T(8,128)(2,1)}), bf16[4,64,256]{2,1,0:T(8,128)(2,1)S(1)}, u32[]{:S(2)}, u32[]{:S(2)}) async-start(bf16[4,64,256]{2,1,0:T(8,128)(2,1)} %norm.1), calls=%async_computation.2 | async-start | bytes 262144 | tf_op jit(solution)/shard_map/all_to_all | solution.py:217
  111.5 28.9 %copy-start.1 = (bf16[2048,256]{1,0:T(8,128)(2,1)S(1)}, bf16[2048,256]{1,0:T(8,128)(2,1)}, u32[]{:S(2)}) copy-start(bf16[2048,256]{1,0:T(8,128)(2,1)} %table_ref.1) | copy-start | bytes 3145732

commit v7 on v6

--- a/solution.py
+++ b/solution.py
@@ -56,76 +56,45 @@
 
 
 def tower_kernel(
-    place_ref, f0, f1, f2, f3, mine, left, ra, rb, fa, fb, bias_ref, give_ref, kept_ref, w_all, hid
+    place_ref, f0, f1, f2, f3, mine, la, lb, ra, rb, fa, fb, bias_ref, give_ref, keep_ref, w_all, hid
 ):
     x0, tp, yl, core = (place_ref[i] for i in range(4))
     feats = ((f0, f1), (f2, f3))
     act = [None, None]
-    blocks = (
-        (0, mine.at[0:2], mine.at[2:4]),
-        (3, left.at[0:2], left.at[2:4]),
-        (1, ra, rb),
-        (2, fa, fb),
-    )
+    blocks = ((0, mine.at[0:2], mine.at[2:4]), (3, la, lb), (1, ra, rb), (2, fa, fb))
     for offset, first, second in blocks:
         act = add_block(x0, tp, offset, first, second, feats, act, w_all)
     for dy in range(2):
         v = act[dy] + bias_ref[...]
         hid[dy] = (v * (1.0 / (1.0 + jnp.exp(-v)))).astype(BF16)
 
-    def chunks(c):
-        return [
+    for out_ref, c in ((give_ref, 1 - core), (keep_ref, core)):
+        chunks = [
             hid[dy, pl.ds(pl.multiple_of(zl * 128 + c * 64, 64), 64), :]
             for dy in range(2)
             for zl in range(2)
         ]
-
-    part = lax.dot_general(
-        jnp.concatenate(chunks(1 - core), axis=0),
-        w_all[...],
-        (((1,), (1,)), ((), ())),
-        preferred_element_type=F32,
-    ).astype(BF16)
-    for i, chunk in enumerate(chunks(core)):
-        slot = (i % 2) * 2 + jnp.bitwise_xor(yl, i // 2)
-        give_ref[slot] = part[i * 64 : (i + 1) * 64]
-        kept_ref[pl.ds(pl.multiple_of(slot * 64, 64), 64), :] = chunk
-
-
-def kept_kernel(kept_ref, w_all, out_ref):
-    part = lax.dot_general(
-        kept_ref[...], w_all[...], (((1,), (1,)), ((), ())), preferred_element_type=F32
-    )
-    out_ref[...] = part.astype(BF16).reshape(out_ref.shape)
-
-
-def cost(flops, moved):
-    return pl.CostEstimate(flops=flops, bytes_accessed=moved, transcendentals=0)
+        part = lax.dot_general(
+            jnp.concatenate(chunks, axis=0),
+            w_all[...],
+            (((1,), (1,)), ((), ())),
+            preferred_element_type=F32,
+        ).astype(BF16)
+        for i in range(4):
+            out_ref[(i % 2) * 2 + jnp.bitwise_xor(yl, i // 2)] = part[i * 64 : (i + 1) * 64]
 
 
 def tower(place, feats, weights, bias):
-    params = pltpu.CompilerParams(vmem_limit_bytes=48 << 20)
     part = jax.ShapeDtypeStruct((4, 64, D_OUT), BF16)
-    w_shape = jax.ShapeDtypeStruct((D_OUT, HID), BF16)
-    give, kept, w_all = pl.pallas_call(
+    return pl.pallas_call(
         tower_kernel,
-        out_shape=(part, jax.ShapeDtypeStruct((SRC, HID), BF16), w_shape),
-        in_specs=[SMEM] + [VMEM] * 11,
-        out_specs=(VMEM, VMEM, VMEM),
-        scratch_shapes=[pltpu.VMEM((2, SRC, HID), BF16)],
-        compiler_params=params,
+        out_shape=(part, part),
+        in_specs=[SMEM] + [VMEM] * 12,
+        out_specs=(VMEM, VMEM),
+        scratch_shapes=[pltpu.VMEM((D_OUT, HID), BF16), pltpu.VMEM((2, SRC, HID), BF16)],
+        compiler_params=pltpu.CompilerParams(vmem_limit_bytes=48 << 20),
         name="tower",
     )(place, *feats, *weights, bias)
-    keep = pl.pallas_call(
-        kept_kernel,
-        out_shape=part,
-        in_specs=[VMEM, VMEM],
-        out_specs=VMEM,
-        compiler_params=params,
-        cost_estimate=cost(2 * SRC * HID * D_OUT, 2 << 20),
-        name="kept",
-    )(kept, w_all)
-    return give, keep
 
 
 def norm_kernel(parts_ref, bias_ref, out_ref):
@@ -202,12 +171,13 @@
     near = swap(pair, "yl")
     left = along_x(mine, 1)
     rb, ra = along_x(mine[16:], -1), along_x(mine[:16], -1)
-    fa, fb = along_x(left[:16], 1), along_x(rb, -1)
+    la, lb = left[:16], left[16:]
+    fa, fb = along_x(la, 1), along_x(rb, -1)
 
     over = swap(pair, "zl")
     feats = (pair, near, over, swap(near, "zl"))
 
-    weights = [each.reshape(-1, 4, 2, 24, HID) for each in (mine, left, ra, rb, fa, fb)]
+    weights = [each.reshape(-1, 4, 2, 24, HID) for each in (mine, la, lb, ra, rb, fa, fb)]
     bias = lax.dynamic_slice_in_dim(bias_in, index["yl"] * HID, HID).reshape(1, HID)
 
     give, keep = tower(place, feats, weights, bias)

time: 146 us -> 141 us (0.966)
  blocking collectives: 28.7 us -> 22.9 us
  starting transfers between devices: 60.3 us -> 63.1 us
  local copies, waits for them, and re-layouts: 5.43 us -> 3.48 us
    all_to_all x1, blocking collectives: 28.7 us -> 22.9 us  [local(): lax.all_to_all(packed.reshape(OWNERS, CAP, SHARE + META), ROUTE, split_ax...]
    ppermute x5, starting transfers between devices: 20.8 us -> 23.4 us  [swap(): return lax.ppermute(block, axis, [(0, 1), (1, 0)])]
    pallas_call x2 -> x1, Pallas kernels: 4.56 us -> 3.62 us  [tower(): pl.pallas_call(tower_kernel, out_shape=(part, part), in_specs=[SMEM] + [V...]
  transfers between devices with their start and end apart: 13 -> 13, of which waited for: 7 -> 6; matrix products, arithmetic and copies ran while one was open for 1% -> 1% of each run, Pallas kernels for 0% -> 0%
where the time goes in v7:
time: 141 us; the launch traced here: 138 us
  starting transfers between devices  63.1 us (45%)
  waiting for transfers between devices  38.9 us (28%)
  blocking collectives  22.9 us (16%)
  Pallas kernels  7.2 us (5%)
  local copies, waits for them, and re-layouts  3.48 us (2%)
  other arithmetic  2.24 us (2%)
    ppermute x5, starting transfers between devices, swap(): return lax.ppermute(block, axis, [(0, 1), (1, 0)])  23.4 us
    all_to_all x1, blocking collectives, local(): lax.all_to_all(packed.reshape(OWNERS, CAP, SHARE + META), ROUTE, split_ax...  22.9 us
    all_to_all x1, waiting for transfers between devices, local(): mine = lax.all_to_all(w, PLANE, split_axis=0, concat_axis=0, tiled=True)  17.8 us
    all_to_all x1, starting transfers between devices, local(): mine = lax.all_to_all(w, PLANE, split_axis=0, concat_axis=0, tiled=True)  16.6 us
    ppermute x5, starting transfers between devices, along_x(): return lax.ppermute(block, 'x', [(i, (i + step) % 4) for i in range(4)])  15.1 us
    ppermute x5, waiting for transfers between devices, along_x(): return lax.ppermute(block, 'x', [(i, (i + step) % 4) for i in range(4)])  8.14 us
    all_to_all x1, waiting for transfers between devices, local(): lax.all_to_all(chip, ('zl', 'yl'), split_axis=0, concat_axis=0, tiled=True)  6.84 us
    all_to_all x1, starting transfers between devices, local(): lax.all_to_all(columns, TP, split_axis=0, concat_axis=0, tiled=True)  4.49 us
  transfers between devices with their start and end apart: 13, of which 6 were waited for; matrix products, arithmetic and copies ran while one was open for 1% of the time, Pallas kernels for 0%

profile of v7, /device:TPU:1, one launch (start us, length us, event | category | flops | bytes accessed | tf_op | source)
XLA Modules:
  0.0 138.3 jit_solution(11443517285828335997)
XLA Ops:
  0.0 0.8 pad_maximum_fusion.1
  0.8 1.0 broadcast_in_dim.32
  1.8 0.0 copy-start.3
  1.8 16.6 %all-to-all-start = ((bf16[32,24,512]{2,1,0:T(8,128)(2,1)}), bf16[32,24,512]{2,1,0:T(8,128)(2,1)S(1)}, u32[]{:S(2)}, u32[]{:S(2)}) async-start(bf16[32,24,512]{2,1,0:T(8,128)(2,1)} %bitcast.5), calls=%async_computation | async-start | bytes 1572864 | tf_op jit(solution)/shard_map/all_to_all | solution.py:168
  18.4 0.0 copy-done.3
  18.4 2.9 %collective-permute-start = (bf16[256,512]{1,0:T(8,128)(2,1)S(1)}, bf16[256,512]{1,0:T(8,128)(2,1)S(1)}, u32[]{:S(2)}, u32[]{:S(2)}) collective-permute-start(bf16[256,512]{1,0:T(8,128)(2,1)S(1)} %copy-done.3), channel_id=1, source_target_pairs={{0,1},{1,0},{2,3},{3,2},{4,5},{5,4},{6,7},{7,6},{8,9},{9,8},{10,11... | collective-permute-start | bytes 786440 | tf_op jit(solution)/shard_map/ppermute | solution.py:159
  21.3 1.1 collective-permute-done
  22.5 0.1 pad_maximum_fusion.f0
  22.5 17.8 %all-to-all-done = bf16[32,24,512]{2,1,0:T(8,128)(2,1)S(1)} async-done(((bf16[32,24,512]{2,1,0:T(8,128)(2,1)}), bf16[32,24,512]{2,1,0:T(8,128)(2,1)S(1)}, u32[]{:S(2)}, u32[]{:S(2)}) %all-to-all-start) | async-done | bytes 786464 | tf_op jit(solution)/shard_map/all_to_all | solution.py:168
  40.3 0.0 copy-start.2
  40.3 3.1 %collective-permute-start.4 = (bf16[32,24,512]{2,1,0:T(8,128)(2,1)S(1)}, bf16[32,24,512]{2,1,0:T(8,128)(2,1)S(1)}, u32[]{:S(2)}, u32[]{:S(2)}) collective-permute-start(bf16[32,24,512]{2,1,0:T(8,128)(2,1)S(1)} %all-to-all-done), channel_id=1, source_target_pairs={{0,32},{32,64},{64,96},{96,0},{1,33},{33,65},{65,97},{97,1},{2,34}... | collective-permute-start | bytes 2359304 | tf_op jit(solution)/shard_map/ppermute | solution.py:155
  43.4 3.6 %collective-permute-start.1 = (bf16[2,256,512]{2,1,0:T(8,128)(2,1)S(1)}, bf16[2,256,512]{2,1,0:T(8,128)(2,1)S(1)}, u32[]{:S(2)}, u32[]{:S(2)}) collective-permute-start(bf16[2,256,512]{2,1,0:T(8,128)(2,1)S(1)} %pad_maximum_fusion.f0), channel_id=1, source_target_pairs={{0,4},{4,0},{1,5},{5,1},{2,6},{6,2},{3,7},{7,3},{8,12},{12,8},{9,1... | collective-permute-start | bytes 1572872 | tf_op jit(solution)/shard_map/ppermute | solution.py:159
  47.1 0.8 fusion.6
  47.9 0.0 copy-done.2
  47.9 3.4 %collective-permute-start.6 = (bf16[16,24,512]{2,1,0:T(8,128)(2,1)S(1)}, bf16[16,24,512]{2,1,0:T(8,128)(2,1)S(1)}, u32[]{:S(2)}, u32[]{:S(2)}) collective-permute-start(bf16[16,24,512]{2,1,0:T(8,128)(2,1)S(1)} %get-tuple-element.15), channel_id=1, source_target_pairs={{0,96},{32,0},{64,32},{96,64},{1,97},{33,1},{65,33},{97,65},{2,98}... | collective-permute-start | bytes 1179656 | tf_op jit(solution)/shard_map/ppermute | solution.py:155
  51.2 3.0 %collective-permute-start.2 = (bf16[2,256,512]{2,1,0:T(8,128)(2,1)S(1)}, bf16[2,256,512]{2,1,0:T(8,128)(2,1)S(1)}, u32[]{:S(2)}, u32[]{:S(2)}) collective-permute-start(bf16[2,256,512]{2,1,0:T(8,128)(2,1)S(1)} %pad_maximum_fusion.f0), channel_id=1, source_target_pairs={{0,2},{2,0},{1,3},{3,1},{4,6},{6,4},{5,7},{7,5},{8,10},{10,8},{9,1... | collective-permute-start | bytes 1572872 | tf_op jit(solution)/shard_map/ppermute | solution.py:159
  54.3 3.2 %collective-permute-start.5 = (bf16[16,24,512]{2,1,0:T(8,128)(2,1)}, bf16[16,24,512]{2,1,0:T(8,128)(2,1)}, u32[]{:S(2)}, u32[]{:S(2)}) collective-permute-start(bf16[16,24,512]{2,1,0:T(8,128)(2,1)} %get-tuple-element.16), channel_id=1, source_target_pairs={{0,96},{32,0},{64,32},{96,64},{1,97},{33,1},{65,33},{97,65},{2,98}... | collective-permute-start | bytes 1179656 | tf_op jit(solution)/shard_map/ppermute | solution.py:155
  57.5 0.0 collective-permute-done.6
  57.5 3.5 %collective-permute-start.8 = (bf16[16,24,512]{2,1,0:T(8,128)(2,1)S(1)}, bf16[16,24,512]{2,1,0:T(8,128)(2,1)}, u32[]{:S(2)}, u32[]{:S(2)}) collective-permute-start(bf16[16,24,512]{2,1,0:T(8,128)(2,1)S(1)} %collective-permute-done.6), channel_id=1, source_target_pairs={{0,96},{32,0},{64,32},{96,64},{1,97},{33,1},{65,33},{97,65},{2,98}... | collective-permute-start | bytes 1179656 | tf_op jit(solution)/shard_map/ppermute | solution.py:155
  61.0 0.0 collective-permute-done.1.f1
  61.0 3.0 %collective-permute-start.3 = (bf16[2,256,512]{2,1,0:T(8,128)(2,1)S(1)}, bf16[2,256,512]{2,1,0:T(8,128)(2,1)S(1)}, u32[]{:S(2)}, u32[]{:S(2)}) collective-permute-start(bf16[2,256,512]{2,1,0:T(8,128)(2,1)S(1)} %collective-permute-done.1.f1), channel_id=1, source_target_pairs={{0,2},{2,0},{1,3},{3,1},{4,6},{6,4},{5,7},{7,5},{8,10},{10,8},{9,1... | collective-permute-start | bytes 1572872 | tf_op jit(solution)/shard_map/ppermute | solution.py:159
  64.0 0.0 collective-permute-done.4
  64.0 0.1 fusion.7
  64.1 1.9 %collective-permute-start.7 = (bf16[16,24,512]{2,1,0:T(8,128)(2,1)S(1)}, bf16[16,24,512]{2,1,0:T(8,128)(2,1)}, u32[]{:S(2)}, u32[]{:S(2)}) collective-permute-start(bf16[16,24,512]{2,1,0:T(8,128)(2,1)S(1)} %get-tuple-element.18), channel_id=1, source_target_pairs={{0,32},{32,64},{64,96},{96,0},{1,33},{33,65},{65,97},{97,1},{2,34}... | collective-permute-start | bytes 1179656 | tf_op jit(solution)/shard_map/ppermute | solution.py:155
  66.0 0.0 copy-start.5
  66.0 0.7 copy-done.5
  66.7 0.1 dynamic_slice.3
  66.8 0.1 pad_add_fusion.place_ref
  66.9 0.0 collective-permute-done.5
  66.9 0.0 collective-permute-done.2.f2
  66.9 8.1 %collective-permute-done.8 = bf16[16,24,512]{2,1,0:T(8,128)(2,1)} collective-permute-done((bf16[16,24,512]{2,1,0:T(8,128)(2,1)S(1)}, bf16[16,24,512]{2,1,0:T(8,128)(2,1)}, u32[]{:S(2)}, u32[]{:S(2)}) %collective-permute-start.8) | collective-permute-done | bytes 393248 | tf_op jit(solution)/shard_map/ppermute | solution.py:155
  75.0 0.0 collective-permute-done.3.f3
  75.0 0.0 collective-permute-done.7
  75.0 3.6 %tower.1 = (bf16[4,64,1024]{2,1,0:T(8,128)(2,1)S(1)}, bf16[4,64,1024]{2,1,0:T(8,128)(2,1)S(1)}) custom-call(s32[4]{0:T(128)S(1)} %pad_add_fusion.place_ref, bf16[2,256,512]{2,1,0:T(8,128)(2,1)S(1)} %pad_maximum_fusion.f0, bf16[2,256,512]{2,1,0:T(8,128)(2,1)S(1)} %collective-permute-done.1.f1, bf16[2,256,512]{2,1,0:T(8,128)(2,1)S(1)} %collective-permute-done.2.f2, ...), custom_call_target="tpu_custom_call" | custom-call | tf_op jit(solution)/shard_map/tower/pallas_call | solution.py:89
  78.6 10.9 %collective-permute-start.9 = (bf16[4,64,1024]{2,1,0:T(8,128)(2,1)S(1)}, bf16[4,64,1024]{2,1,0:T(8,128)(2,1)S(1)}, u32[]{:S(2)}, u32[]{:S(2)}) collective-permute-start(bf16[4,64,1024]{2,1,0:T(8,128)(2,1)S(1)} %get-tuple-element.12), channel_id=1, source_target_pairs={{0,1},{1,0},{2,3},{3,2},{4,5},{5,4},{6,7},{7,6},{8,9},{9,8},{10,11... | collective-permute-start | bytes 1572872 | tf_op jit(solution)/shard_map/ppermute | solution.py:159
  89.5 1.5 %collective-permute-done.9 = bf16[4,64,1024]{2,1,0:T(8,128)(2,1)S(1)} collective-permute-done((bf16[4,64,1024]{2,1,0:T(8,128)(2,1)S(1)}, bf16[4,64,1024]{2,1,0:T(8,128)(2,1)S(1)}, u32[]{:S(2)}, u32[]{:S(2)}) %collective-permute-start.9) | collective-permute-done | bytes 524320 | tf_op jit(solution)/shard_map/ppermute | solution.py:159
  91.0 1.0 add_convert_fusion
  92.0 3.5 %all-to-all-start.1 = ((bf16[4,64,1024]{2,1,0:T(8,128)(2,1)}), bf16[4,64,1024]{2,1,0:T(8,128)(2,1)S(1)}, u32[]{:S(2)}, u32[]{:S(2)}) async-start(bf16[4,64,1024]{2,1,0:T(8,128)(2,1)} %add_convert_fusion), calls=%async_computation.1 | async-start | bytes 1048576 | tf_op jit(solution)/shard_map/all_to_all | solution.py:185
  95.5 0.0 copy-start.4
  95.5 0.7 copy-done.4
  96.2 0.2 convert_reduce_fusion
  96.4 0.0 copy-start.1
  96.4 6.8 %all-to-all-done.1.parts_ref = bf16[4,64,1024]{2,1,0:T(8,128)(2,1)S(1)} async-done(((bf16[4,64,1024]{2,1,0:T(8,128)(2,1)}), bf16[4,64,1024]{2,1,0:T(8,128)(2,1)S(1)}, u32[]{:S(2)}, u32[]{:S(2)}) %all-to-all-start.1) | async-done | bytes 524320 | tf_op jit(solution)/shard_map/all_to_all | solution.py:185
  103.2 0.0 copy-done.1
  103.2 0.8 norm.1
  104.1 4.5 %all-to-all-start.2 = ((bf16[4,64,256]{2,1,0:T(8,128)(2,1)}), bf16[4,64,256]{2,1,0:T(8,128)(2,1)S(1)}, u32[]{:S(2)}, u32[]{:S(2)}) async-start(bf16[4,64,256]{2,1,0:T(8,128)(2,1)} %norm.1), calls=%async_computation.2 | async-start | bytes 262144 | tf_op jit(solution)/shard_map/all_to_all | solution.py:187
  108.5 0.1 select_convert_fusion
  108.7 3.5 %all-to-all-done.2 = bf16[4,64,256]{2,1,0:T(8,128)(2,1)S(1)} async-done(((bf16[4,64,256]{2,1,0:T(8,128)(2,1)}), bf16[4,64,256]{2,1,0:T(8,128)(2,1)S(1)}, u32[]{:S(2)}, u32[]{:S(2)}) %all-to-all-start.2) | async-done | bytes 131104 | tf_op jit(solution)/shard_map/all_to_all | solution.py:187
  112.1 0.3 convolution_convert_fusion
  112.5 0.0 copy-start
  112.5 0.1 reshape.70
  112.6 22.9 %all_to_all.20 = bf16[128,4,384]{2,1,0:T(4,128)(2,1)S(1)} all-to-all(bf16[128,4,384]{2,1,0:T(4,128)(2,1)S(1)} %reshape.70), channel_id=1, replica_groups=mesh['zh'=4,'x'=4,'yh'=4,'yl'=2,'zl'=2,'core'=2] {'yl','yh','x','zh'}, dimensions={0} | all-to-all | bytes 786432 | tf_op jit(solution)/shard_map/all_to_all | solution.py:205
  135.5 0.1 reshape.71.rows_ref
  135.6 0.0 copy-done
  135.6 2.7 %write.1 = bf16[2048,256]{1,0:T(8,128)(2,1)} custom-call(bf16[2048,256]{1,0:T(8,128)(2,1)S(1)} %copy-done, bf16[512,384]{1,0:T(8,128)(2,1)S(1)} %reshape.71.rows_ref), custom_call_target="tpu_custom_call" | custom-call | tf_op jit(solution)/shard_map/write/pallas_call | solution.py:142
  (5 shorter events, 0.1 us)
Async XLA Ops:
  1.8 16.6 %copy-start.3 = (bf16[256,512]{1,0:T(8,128)(2,1)S(1)}, bf16[256,512]{1,0:T(8,128)(2,1)}, u32[]{:S(2)}) copy-start(bf16[256,512]{1,0:T(8,128)(2,1)} %param.7) | copy-start | bytes 786436
  1.8 38.5 %all-to-all-start = ((bf16[32,24,512]{2,1,0:T(8,128)(2,1)}), bf16[32,24,512]{2,1,0:T(8,128)(2,1)S(1)}, u32[]{:S(2)}, u32[]{:S(2)}) async-start(bf16[32,24,512]{2,1,0:T(8,128)(2,1)} %bitcast.5), calls=%async_computation | async-start | bytes 1572864 | tf_op jit(solution)/shard_map/all_to_all | solution.py:168
  18.4 4.0 %collective-permute-start = (bf16[256,512]{1,0:T(8,128)(2,1)S(1)}, bf16[256,512]{1,0:T(8,128)(2,1)S(1)}, u32[]{:S(2)}, u32[]{:S(2)}) collective-permute-start(bf16[256,512]{1,0:T(8,128)(2,1)S(1)} %copy-done.3), channel_id=1, source_target_pairs={{0,1},{1,0},{2,3},{3,2},{4,5},{5,4},{6,7},{7,6},{8,9},{9,8},{10,11... | collective-permute-start | bytes 786440 | tf_op jit(solution)/shard_map/ppermute | solution.py:159
  40.3 7.6 %copy-start.2 = (bf16[32,24,512]{2,1,0:T(8,128)(2,1)}, bf16[32,24,512]{2,1,0:T(8,128)(2,1)S(1)}, u32[]{:S(2)}) copy-start(bf16[32,24,512]{2,1,0:T(8,128)(2,1)S(1)} %all-to-all-done) | copy-start | bytes 2359300
  40.3 23.7 %collective-permute-start.4 = (bf16[32,24,512]{2,1,0:T(8,128)(2,1)S(1)}, bf16[32,24,512]{2,1,0:T(8,128)(2,1)S(1)}, u32[]{:S(2)}, u32[]{:S(2)}) collective-permute-start(bf16[32,24,512]{2,1,0:T(8,128)(2,1)S(1)} %all-to-all-done), channel_id=1, source_target_pairs={{0,32},{32,64},{64,96},{96,0},{1,33},{33,65},{65,97},{97,1},{2,34}... | collective-permute-start | bytes 2359304 | tf_op jit(solution)/shard_map/ppermute | solution.py:155
  43.4 17.5 %collective-permute-start.1 = (bf16[2,256,512]{2,1,0:T(8,128)(2,1)S(1)}, bf16[2,256,512]{2,1,0:T(8,128)(2,1)S(1)}, u32[]{:S(2)}, u32[]{:S(2)}) collective-permute-start(bf16[2,256,512]{2,1,0:T(8,128)(2,1)S(1)} %pad_maximum_fusion.f0), channel_id=1, source_target_pairs={{0,4},{4,0},{1,5},{5,1},{2,6},{6,2},{3,7},{7,3},{8,12},{12,8},{9,1... | collective-permute-start | bytes 1572872 | tf_op jit(solution)/shard_map/ppermute | solution.py:159
  47.9 9.6 %collective-permute-start.6 = (bf16[16,24,512]{2,1,0:T(8,128)(2,1)S(1)}, bf16[16,24,512]{2,1,0:T(8,128)(2,1)S(1)}, u32[]{:S(2)}, u32[]{:S(2)}) collective-permute-start(bf16[16,24,512]{2,1,0:T(8,128)(2,1)S(1)} %get-tuple-element.15), channel_id=1, source_target_pairs={{0,96},{32,0},{64,32},{96,64},{1,97},{33,1},{65,33},{97,65},{2,98}... | collective-permute-start | bytes 1179656 | tf_op jit(solution)/shard_map/ppermute | solution.py:155
  51.2 15.6 %collective-permute-start.2 = (bf16[2,256,512]{2,1,0:T(8,128)(2,1)S(1)}, bf16[2,256,512]{2,1,0:T(8,128)(2,1)S(1)}, u32[]{:S(2)}, u32[]{:S(2)}) collective-permute-start(bf16[2,256,512]{2,1,0:T(8,128)(2,1)S(1)} %pad_maximum_fusion.f0), channel_id=1, source_target_pairs={{0,2},{2,0},{1,3},{3,1},{4,6},{6,4},{5,7},{7,5},{8,10},{10,8},{9,1... | collective-permute-start | bytes 1572872 | tf_op jit(solution)/shard_map/ppermute | solution.py:159
  54.3 12.6 %collective-permute-start.5 = (bf16[16,24,512]{2,1,0:T(8,128)(2,1)}, bf16[16,24,512]{2,1,0:T(8,128)(2,1)}, u32[]{:S(2)}, u32[]{:S(2)}) collective-permute-start(bf16[16,24,512]{2,1,0:T(8,128)(2,1)} %get-tuple-element.16), channel_id=1, source_target_pairs={{0,96},{32,0},{64,32},{96,64},{1,97},{33,1},{65,33},{97,65},{2,98}... | collective-permute-start | bytes 1179656 | tf_op jit(solution)/shard_map/ppermute | solution.py:155
  57.5 17.5 %collective-permute-start.8 = (bf16[16,24,512]{2,1,0:T(8,128)(2,1)S(1)}, bf16[16,24,512]{2,1,0:T(8,128)(2,1)}, u32[]{:S(2)}, u32[]{:S(2)}) collective-permute-start(bf16[16,24,512]{2,1,0:T(8,128)(2,1)S(1)} %collective-permute-done.6), channel_id=1, source_target_pairs={{0,96},{32,0},{64,32},{96,64},{1,97},{33,1},{65,33},{97,65},{2,98}... | collective-permute-start | bytes 1179656 | tf_op jit(solution)/shard_map/ppermute | solution.py:155
  61.0 14.0 %collective-permute-start.3 = (bf16[2,256,512]{2,1,0:T(8,128)(2,1)S(1)}, bf16[2,256,512]{2,1,0:T(8,128)(2,1)S(1)}, u32[]{:S(2)}, u32[]{:S(2)}) collective-permute-start(bf16[2,256,512]{2,1,0:T(8,128)(2,1)S(1)} %collective-permute-done.1.f1), channel_id=1, source_target_pairs={{0,2},{2,0},{1,3},{3,1},{4,6},{6,4},{5,7},{7,5},{8,10},{10,8},{9,1... | collective-permute-start | bytes 1572872 | tf_op jit(solution)/shard_map/ppermute | solution.py:159
  64.1 10.9 %collective-permute-start.7 = (bf16[16,24,512]{2,1,0:T(8,128)(2,1)S(1)}, bf16[16,24,512]{2,1,0:T(8,128)(2,1)}, u32[]{:S(2)}, u32[]{:S(2)}) collective-permute-start(bf16[16,24,512]{2,1,0:T(8,128)(2,1)S(1)} %get-tuple-element.18), channel_id=1, source_target_pairs={{0,32},{32,64},{64,96},{96,0},{1,33},{33,65},{65,97},{97,1},{2,34}... | collective-permute-start | bytes 1179656 | tf_op jit(solution)/shard_map/ppermute | solution.py:155
  66.0 0.7 copy-start.5
  78.6 12.4 %collective-permute-start.9 = (bf16[4,64,1024]{2,1,0:T(8,128)(2,1)S(1)}, bf16[4,64,1024]{2,1,0:T(8,128)(2,1)S(1)}, u32[]{:S(2)}, u32[]{:S(2)}) collective-permute-start(bf16[4,64,1024]{2,1,0:T(8,128)(2,1)S(1)} %get-tuple-element.12), channel_id=1, source_target_pairs={{0,1},{1,0},{2,3},{3,2},{4,5},{5,4},{6,7},{7,6},{8,9},{9,8},{10,11... | collective-permute-start | bytes 1572872 | tf_op jit(solution)/shard_map/ppermute | solution.py:159
  92.0 11.2 %all-to-all-start.1 = ((bf16[4,64,1024]{2,1,0:T(8,128)(2,1)}), bf16[4,64,1024]{2,1,0:T(8,128)(2,1)S(1)}, u32[]{:S(2)}, u32[]{:S(2)}) async-start(bf16[4,64,1024]{2,1,0:T(8,128)(2,1)} %add_convert_fusion), calls=%async_computation.1 | async-start | bytes 1048576 | tf_op jit(solution)/shard_map/all_to_all | solution.py:185
  95.5 0.7 copy-start.4
  96.4 6.9 %copy-start.1 = (f32[1024]{0:T(1024)S(1)}, f32[1024]{0:T(1024)}, u32[]{:S(2)}) copy-start(f32[1024]{0:T(1024)} %param.12) | copy-start | bytes 12292
  104.1 8.1 %all-to-all-start.2 = ((bf16[4,64,256]{2,1,0:T(8,128)(2,1)}), bf16[4,64,256]{2,1,0:T(8,128)(2,1)S(1)}, u32[]{:S(2)}, u32[]{:S(2)}) async-start(bf16[4,64,256]{2,1,0:T(8,128)(2,1)} %norm.1), calls=%async_computation.2 | async-start | bytes 262144 | tf_op jit(solution)/shard_map/all_to_all | solution.py:187
  112.5 23.1 %copy-start = (bf16[2048,256]{1,0:T(8,128)(2,1)S(1)}, bf16[2048,256]{1,0:T(8,128)(2,1)}, u32[]{:S(2)}) copy-start(bf16[2048,256]{1,0:T(8,128)(2,1)} %table_ref.1) | copy-start | bytes 3145732

commit v8 on v7

--- a/solution.py
+++ b/solution.py
@@ -26,11 +26,12 @@
 SMEM = pl.BlockSpec(memory_space=pltpu.SMEM)
 
 
-def add_block(x0, tp, offset, first, second, feats, act, w_all):
+def add_block(x0, tp, yl, offset, first, second, feats, act, w_all):
     xk = lax.rem(x0 + offset, 4)
     col = pl.multiple_of(xk * 128, 128)
     act = list(act)
     for dz in range(2):
+        zl = jnp.bitwise_xor(lax.shift_right_logical(tp, 1), dz)
         weights = jnp.concatenate(
             [
                 half[:, jnp.bitwise_xor(tp, dz * 2 + dc), :, 0:16, :].reshape(64, HID)
@@ -40,8 +41,9 @@
             axis=0,
         )
         for dy in range(2):
+            chip = zl * 2 + jnp.bitwise_xor(yl, dy)
             columns = jnp.concatenate(
-                [feats[dz][dy][dc, :, pl.ds(col, 128)] for dc in range(2)], axis=1
+                [feats[chip, dc, :, pl.ds(col, 128)] for dc in range(2)], axis=1
             )
             term = jnp.dot(columns, weights, preferred_element_type=F32)
             act[dy] = term if act[dy] is None else act[dy] + term
@@ -56,14 +58,13 @@
 
 
 def tower_kernel(
-    place_ref, f0, f1, f2, f3, mine, la, lb, ra, rb, fa, fb, bias_ref, give_ref, keep_ref, w_all, hid
+    place_ref, feats, mine, la, lb, ra, rb, fa, fb, bias_ref, give_ref, keep_ref, w_all, hid
 ):
     x0, tp, yl, core = (place_ref[i] for i in range(4))
-    feats = ((f0, f1), (f2, f3))
     act = [None, None]
     blocks = ((0, mine.at[0:2], mine.at[2:4]), (3, la, lb), (1, ra, rb), (2, fa, fb))
     for offset, first, second in blocks:
-        act = add_block(x0, tp, offset, first, second, feats, act, w_all)
+        act = add_block(x0, tp, yl, offset, first, second, feats, act, w_all)
     for dy in range(2):
         v = act[dy] + bias_ref[...]
         hid[dy] = (v * (1.0 / (1.0 + jnp.exp(-v)))).astype(BF16)
@@ -89,12 +90,12 @@
     return pl.pallas_call(
         tower_kernel,
         out_shape=(part, part),
-        in_specs=[SMEM] + [VMEM] * 12,
+        in_specs=[SMEM] + [VMEM] * 9,
         out_specs=(VMEM, VMEM),
         scratch_shapes=[pltpu.VMEM((D_OUT, HID), BF16), pltpu.VMEM((2, SRC, HID), BF16)],
         compiler_params=pltpu.CompilerParams(vmem_limit_bytes=48 << 20),
         name="tower",
-    )(place, *feats, *weights, bias)
+    )(place, feats, *weights, bias)
 
 
 def norm_kernel(parts_ref, bias_ref, out_ref):
@@ -167,16 +168,14 @@
     w = jnp.broadcast_to(w[None], (16, 2, 24, HID)).reshape(32, 24, HID)
     mine = lax.all_to_all(w, PLANE, split_axis=0, concat_axis=0, tiled=True)
     pair = jnp.stack([features, swap(features, "core")])
-    mine, pair = lax.optimization_barrier((mine, pair))
-    near = swap(pair, "yl")
+    copies = jnp.broadcast_to(pair[None], (4, 2, SRC, 512))
+    mine, copies = lax.optimization_barrier((mine, copies))
     left = along_x(mine, 1)
     rb, ra = along_x(mine[16:], -1), along_x(mine[:16], -1)
     la, lb = left[:16], left[16:]
     fa, fb = along_x(la, 1), along_x(rb, -1)
 
-    over = swap(pair, "zl")
-    feats = (pair, near, over, swap(near, "zl"))
-
+    feats = lax.all_to_all(copies, ("zl", "yl"), split_axis=0, concat_axis=0, tiled=True)
     weights = [each.reshape(-1, 4, 2, 24, HID) for each in (mine, la, lb, ra, rb, fa, fb)]
     bias = lax.dynamic_slice_in_dim(bias_in, index["yl"] * HID, HID).reshape(1, HID)
 

time: 141 us -> 142 us (level)
  starting transfers between devices: 63.1 us -> 58.2 us
  waiting for transfers between devices: 38.9 us -> 43.7 us
  blocking collectives: 22.9 us -> 24.4 us
    ppermute x5 -> x2, starting transfers between devices: 23.4 us -> 12.3 us  [swap(): return lax.ppermute(block, axis, [(0, 1), (1, 0)])]
    all_to_all x0 -> x1, starting transfers between devices: none -> 4.45 us  [local(): lax.all_to_all(copies, ('zl', 'yl'), split_axis=0, concat_axis=0, tiled=T...]
    ppermute x5, waiting for transfers between devices: 8.14 us -> 12.5 us  [along_x(): return lax.ppermute(block, 'x', [(i, (i + step) % 4) for i in range(4)])]
    all_to_all x1, blocking collectives: 22.9 us -> 24.4 us  [local(): lax.all_to_all(packed.reshape(OWNERS, CAP, SHARE + META), ROUTE, split_ax...]
    broadcast_in_dim x0 -> x1, local copies, waits for them, and re-layouts: none -> 1.48 us  [local(): copies = jnp.broadcast_to(pair[None], (4, 2, SRC, 512))]
  transfers between devices with their start and end apart: 13 -> 11, of which waited for: 6 -> 8; matrix products, arithmetic and copies ran while one was open for 1% -> 0% of each run, Pallas kernels for 0% -> 0%
where the time goes in v8:
time: 142 us; the launch traced here: 139 us
  starting transfers between devices  58.2 us (41%)
  waiting for transfers between devices  43.7 us (31%)
  blocking collectives  24.4 us (17%)
  Pallas kernels  7.32 us (5%)
  local copies, waits for them, and re-layouts  2.88 us (2%)
  other arithmetic  2.28 us (2%)
    all_to_all x1, blocking collectives, local(): lax.all_to_all(packed.reshape(OWNERS, CAP, SHARE + META), ROUTE, split_ax...  24.4 us
    all_to_all x1, waiting for transfers between devices, local(): mine = lax.all_to_all(w, PLANE, split_axis=0, concat_axis=0, tiled=True)  17.8 us
    all_to_all x1, starting transfers between devices, local(): mine = lax.all_to_all(w, PLANE, split_axis=0, concat_axis=0, tiled=True)  16.5 us
    ppermute x5, starting transfers between devices, along_x(): return lax.ppermute(block, 'x', [(i, (i + step) % 4) for i in range(4)])  16.2 us
    ppermute x5, waiting for transfers between devices, along_x(): return lax.ppermute(block, 'x', [(i, (i + step) % 4) for i in range(4)])  12.5 us
    ppermute x2, starting transfers between devices, swap(): return lax.ppermute(block, axis, [(0, 1), (1, 0)])  12.3 us
    all_to_all x1, waiting for transfers between devices, local(): lax.all_to_all(chip, ('zl', 'yl'), split_axis=0, concat_axis=0, tiled=True)  7.27 us
    all_to_all x1, starting transfers between devices, local(): lax.all_to_all(columns, TP, split_axis=0, concat_axis=0, tiled=True)  4.77 us
  transfers between devices with their start and end apart: 11, of which 8 were waited for; matrix products, arithmetic and copies ran while one was open for 0% of the time, Pallas kernels for 0%

profile of v8, /device:TPU:1, one launch (start us, length us, event | category | flops | bytes accessed | tf_op | source)
XLA Modules:
  0.0 139.3 jit_solution(15596702478822321995)
XLA Ops:
  0.0 0.0 copy-start.2
  0.0 0.8 pad_maximum_fusion.1
  0.9 1.0 broadcast_in_dim.34
  1.8 16.5 %all-to-all-start = ((bf16[32,24,512]{2,1,0:T(8,128)(2,1)}), bf16[32,24,512]{2,1,0:T(8,128)(2,1)S(1)}, u32[]{:S(2)}, u32[]{:S(2)}) async-start(bf16[32,24,512]{2,1,0:T(8,128)(2,1)} %bitcast.5), calls=%async_computation | async-start | bytes 1572864 | tf_op jit(solution)/shard_map/all_to_all | solution.py:169
  18.4 0.0 copy-done.2
  18.4 2.9 %collective-permute-start = (bf16[256,512]{1,0:T(8,128)(2,1)S(1)}, bf16[256,512]{1,0:T(8,128)(2,1)S(1)}, u32[]{:S(2)}, u32[]{:S(2)}) collective-permute-start(bf16[256,512]{1,0:T(8,128)(2,1)S(1)} %copy-done.2), channel_id=1, source_target_pairs={{0,1},{1,0},{2,3},{3,2},{4,5},{5,4},{6,7},{7,6},{8,9},{9,8},{10,11... | collective-permute-start | bytes 786440 | tf_op jit(solution)/shard_map/ppermute | solution.py:160
  21.2 1.1 collective-permute-done
  22.4 0.1 pad_maximum_fusion
  22.4 17.8 %all-to-all-done = bf16[32,24,512]{2,1,0:T(8,128)(2,1)S(1)} async-done(((bf16[32,24,512]{2,1,0:T(8,128)(2,1)}), bf16[32,24,512]{2,1,0:T(8,128)(2,1)S(1)}, u32[]{:S(2)}, u32[]{:S(2)}) %all-to-all-start) | async-done | bytes 786464 | tf_op jit(solution)/shard_map/all_to_all | solution.py:169
  40.2 1.5 %broadcast_in_dim.35 = bf16[4,2,256,512]{3,2,1,0:T(8,128)(2,1)} broadcast(bf16[2,256,512]{2,1,0:T(8,128)(2,1)S(1)} %pad_maximum_fusion), dimensions={1,2,3} | broadcast | bytes 2621440 | tf_op jit(solution)/shard_map/broadcast_in_dim | solution.py:171
  41.7 4.5 %all-to-all-start.1 = ((bf16[4,2,256,512]{3,2,1,0:T(8,128)(2,1)}), bf16[4,2,256,512]{3,2,1,0:T(8,128)(2,1)}, u32[]{:S(2)}, u32[]{:S(2)}) async-start(bf16[4,2,256,512]{3,2,1,0:T(8,128)(2,1)} %broadcast_in_dim.35), calls=%async_computation.1 | async-start | bytes 4194304 | tf_op jit(solution)/shard_map/all_to_all | solution.py:178
  46.2 0.0 copy-start.4
  46.2 3.1 %collective-permute-start.1 = (bf16[32,24,512]{2,1,0:T(8,128)(2,1)S(1)}, bf16[32,24,512]{2,1,0:T(8,128)(2,1)S(1)}, u32[]{:S(2)}, u32[]{:S(2)}) collective-permute-start(bf16[32,24,512]{2,1,0:T(8,128)(2,1)S(1)} %all-to-all-done), channel_id=1, source_target_pairs={{0,32},{32,64},{64,96},{96,0},{1,33},{33,65},{65,97},{97,1},{2,34}... | collective-permute-start | bytes 2359304 | tf_op jit(solution)/shard_map/ppermute | solution.py:156
  49.3 0.1 fusion.6
  49.4 3.4 %collective-permute-start.3 = (bf16[16,24,512]{2,1,0:T(8,128)(2,1)S(1)}, bf16[16,24,512]{2,1,0:T(8,128)(2,1)S(1)}, u32[]{:S(2)}, u32[]{:S(2)}) collective-permute-start(bf16[16,24,512]{2,1,0:T(8,128)(2,1)S(1)} %get-tuple-element.15), channel_id=1, source_target_pairs={{0,96},{32,0},{64,32},{96,64},{1,97},{33,1},{65,33},{97,65},{2,98}... | collective-permute-start | bytes 1179656 | tf_op jit(solution)/shard_map/ppermute | solution.py:156
  52.7 3.2 %collective-permute-start.2 = (bf16[16,24,512]{2,1,0:T(8,128)(2,1)S(1)}, bf16[16,24,512]{2,1,0:T(8,128)(2,1)S(1)}, u32[]{:S(2)}, u32[]{:S(2)}) collective-permute-start(bf16[16,24,512]{2,1,0:T(8,128)(2,1)S(1)} %get-tuple-element.16), channel_id=1, source_target_pairs={{0,96},{32,0},{64,32},{96,64},{1,97},{33,1},{65,33},{97,65},{2,98}... | collective-permute-start | bytes 1179656 | tf_op jit(solution)/shard_map/ppermute | solution.py:156
  55.9 2.5 %collective-permute-done.3 = bf16[16,24,512]{2,1,0:T(8,128)(2,1)S(1)} collective-permute-done((bf16[16,24,512]{2,1,0:T(8,128)(2,1)S(1)}, bf16[16,24,512]{2,1,0:T(8,128)(2,1)S(1)}, u32[]{:S(2)}, u32[]{:S(2)}) %collective-permute-start.3) | collective-permute-done | bytes 393248 | tf_op jit(solution)/shard_map/ppermute | solution.py:156
  58.4 4.5 %collective-permute-start.5 = (bf16[16,24,512]{2,1,0:T(8,128)(2,1)S(1)}, bf16[16,24,512]{2,1,0:T(8,128)(2,1)S(1)}, u32[]{:S(2)}, u32[]{:S(2)}) collective-permute-start(bf16[16,24,512]{2,1,0:T(8,128)(2,1)S(1)} %collective-permute-done.3), channel_id=1, source_target_pairs={{0,96},{32,0},{64,32},{96,64},{1,97},{33,1},{65,33},{97,65},{2,98}... | collective-permute-start | bytes 1179656 | tf_op jit(solution)/shard_map/ppermute | solution.py:156
  62.9 2.1 %collective-permute-done.1 = bf16[32,24,512]{2,1,0:T(8,128)(2,1)S(1)} collective-permute-done((bf16[32,24,512]{2,1,0:T(8,128)(2,1)S(1)}, bf16[32,24,512]{2,1,0:T(8,128)(2,1)S(1)}, u32[]{:S(2)}, u32[]{:S(2)}) %collective-permute-start.1) | collective-permute-done | bytes 786464 | tf_op jit(solution)/shard_map/ppermute | solution.py:156
  65.0 0.1 fusion.7
  65.1 2.0 %collective-permute-start.4 = (bf16[16,24,512]{2,1,0:T(8,128)(2,1)S(1)}, bf16[16,24,512]{2,1,0:T(8,128)(2,1)S(1)}, u32[]{:S(2)}, u32[]{:S(2)}) collective-permute-start(bf16[16,24,512]{2,1,0:T(8,128)(2,1)S(1)} %get-tuple-element.18), channel_id=1, source_target_pairs={{0,32},{32,64},{64,96},{96,0},{1,33},{33,65},{65,97},{97,1},{2,34}... | collective-permute-start | bytes 1179656 | tf_op jit(solution)/shard_map/ppermute | solution.py:156
  67.1 0.0 copy-done.4
  67.1 0.1 dynamic_slice.3
  67.2 0.1 pad_add_fusion.place_ref
  67.3 0.0 collective-permute-done.2
  67.3 7.9 %collective-permute-done.5 = bf16[16,24,512]{2,1,0:T(8,128)(2,1)S(1)} collective-permute-done((bf16[16,24,512]{2,1,0:T(8,128)(2,1)S(1)}, bf16[16,24,512]{2,1,0:T(8,128)(2,1)S(1)}, u32[]{:S(2)}, u32[]{:S(2)}) %collective-permute-start.5) | collective-permute-done | bytes 393248 | tf_op jit(solution)/shard_map/ppermute | solution.py:156
  75.2 0.0 collective-permute-done.4
  75.2 0.0 all-to-all-done.1.feats
  75.2 3.7 %tower.1 = (bf16[4,64,1024]{2,1,0:T(8,128)(2,1)S(1)}, bf16[4,64,1024]{2,1,0:T(8,128)(2,1)S(1)}) custom-call(s32[4]{0:T(128)S(1)} %pad_add_fusion.place_ref, bf16[4,2,256,512]{3,2,1,0:T(8,128)(2,1)} %all-to-all-done.1.feats, bf16[4,4,2,24,512]{4,3,2,1,0:T(8,128)(2,1)S(1)} %bitcast.18, bf16[2,4,2,24,512]{4,3,2,1,0:T(8,128)(2,1)S(1)} %bitcast.20, ...), custom_call_target="tpu_custom_call" | custom-call | tf_op jit(solution)/shard_map/tower/pallas_call | solution.py:90
  78.9 0.0 copy-start.3
  78.9 0.0 copy-start.1
  78.9 9.4 %collective-permute-start.6 = (bf16[4,64,1024]{2,1,0:T(8,128)(2,1)S(1)}, bf16[4,64,1024]{2,1,0:T(8,128)(2,1)S(1)}, u32[]{:S(2)}, u32[]{:S(2)}) collective-permute-start(bf16[4,64,1024]{2,1,0:T(8,128)(2,1)S(1)} %get-tuple-element.12), channel_id=1, source_target_pairs={{0,1},{1,0},{2,3},{3,2},{4,5},{5,4},{6,7},{7,6},{8,9},{9,8},{10,11... | collective-permute-start | bytes 1572872 | tf_op jit(solution)/shard_map/ppermute | solution.py:160
  88.4 1.5 %collective-permute-done.6 = bf16[4,64,1024]{2,1,0:T(8,128)(2,1)S(1)} collective-permute-done((bf16[4,64,1024]{2,1,0:T(8,128)(2,1)S(1)}, bf16[4,64,1024]{2,1,0:T(8,128)(2,1)S(1)}, u32[]{:S(2)}, u32[]{:S(2)}) %collective-permute-start.6) | collective-permute-done | bytes 524320 | tf_op jit(solution)/shard_map/ppermute | solution.py:160
  89.9 1.0 add_convert_fusion
  90.9 4.1 %all-to-all-start.2 = ((bf16[4,64,1024]{2,1,0:T(8,128)(2,1)}), bf16[4,64,1024]{2,1,0:T(8,128)(2,1)S(1)}, u32[]{:S(2)}, u32[]{:S(2)}) async-start(bf16[4,64,1024]{2,1,0:T(8,128)(2,1)} %add_convert_fusion), calls=%async_computation.2 | async-start | bytes 1048576 | tf_op jit(solution)/shard_map/all_to_all | solution.py:184
  95.0 0.0 copy-start
  95.0 0.0 copy-done.3
  95.0 0.2 convert_reduce_fusion
  95.2 7.3 %all-to-all-done.2.parts_ref = bf16[4,64,1024]{2,1,0:T(8,128)(2,1)S(1)} async-done(((bf16[4,64,1024]{2,1,0:T(8,128)(2,1)}), bf16[4,64,1024]{2,1,0:T(8,128)(2,1)S(1)}, u32[]{:S(2)}, u32[]{:S(2)}) %all-to-all-start.2) | async-done | bytes 524320 | tf_op jit(solution)/shard_map/all_to_all | solution.py:184
  102.5 0.0 copy-done.1
  102.5 0.8 norm.1
  103.3 4.8 %all-to-all-start.3 = ((bf16[4,64,256]{2,1,0:T(8,128)(2,1)}), bf16[4,64,256]{2,1,0:T(8,128)(2,1)S(1)}, u32[]{:S(2)}, u32[]{:S(2)}) async-start(bf16[4,64,256]{2,1,0:T(8,128)(2,1)} %norm.1), calls=%async_computation.3 | async-start | bytes 262144 | tf_op jit(solution)/shard_map/all_to_all | solution.py:186
  108.1 0.1 select_convert_fusion
  108.2 3.5 %all-to-all-done.3 = bf16[4,64,256]{2,1,0:T(8,128)(2,1)S(1)} async-done(((bf16[4,64,256]{2,1,0:T(8,128)(2,1)}), bf16[4,64,256]{2,1,0:T(8,128)(2,1)S(1)}, u32[]{:S(2)}, u32[]{:S(2)}) %all-to-all-start.3) | async-done | bytes 131104 | tf_op jit(solution)/shard_map/all_to_all | solution.py:186
  111.7 0.3 convolution_convert_fusion
  112.0 0.1 reshape.71
  112.1 24.4 %all_to_all.25 = bf16[128,4,384]{2,1,0:T(4,128)(2,1)S(1)} all-to-all(bf16[128,4,384]{2,1,0:T(4,128)(2,1)S(1)} %reshape.71), channel_id=1, replica_groups=mesh['zh'=4,'x'=4,'yh'=4,'yl'=2,'zl'=2,'core'=2] {'yl','yh','x','zh'}, dimensions={0} | all-to-all | bytes 786432 | tf_op jit(solution)/shard_map/all_to_all | solution.py:204
  136.5 0.1 reshape.72.rows_ref
  136.6 0.0 copy-done
  136.6 2.7 %write.1 = bf16[2048,256]{1,0:T(8,128)(2,1)} custom-call(bf16[2048,256]{1,0:T(8,128)(2,1)S(1)} %copy-done, bf16[512,384]{1,0:T(8,128)(2,1)S(1)} %reshape.72.rows_ref), custom_call_target="tpu_custom_call" | custom-call | tf_op jit(solution)/shard_map/write/pallas_call | solution.py:143
  (5 shorter events, 0.1 us)
Async XLA Ops:
  0.0 18.4 %copy-start.2 = (bf16[256,512]{1,0:T(8,128)(2,1)S(1)}, bf16[256,512]{1,0:T(8,128)(2,1)}, u32[]{:S(2)}) copy-start(bf16[256,512]{1,0:T(8,128)(2,1)} %param.7) | copy-start | bytes 786436
  1.8 38.4 %all-to-all-start = ((bf16[32,24,512]{2,1,0:T(8,128)(2,1)}), bf16[32,24,512]{2,1,0:T(8,128)(2,1)S(1)}, u32[]{:S(2)}, u32[]{:S(2)}) async-start(bf16[32,24,512]{2,1,0:T(8,128)(2,1)} %bitcast.5), calls=%async_computation | async-start | bytes 1572864 | tf_op jit(solution)/shard_map/all_to_all | solution.py:169
  18.4 4.0 %collective-permute-start = (bf16[256,512]{1,0:T(8,128)(2,1)S(1)}, bf16[256,512]{1,0:T(8,128)(2,1)S(1)}, u32[]{:S(2)}, u32[]{:S(2)}) collective-permute-start(bf16[256,512]{1,0:T(8,128)(2,1)S(1)} %copy-done.2), channel_id=1, source_target_pairs={{0,1},{1,0},{2,3},{3,2},{4,5},{5,4},{6,7},{7,6},{8,9},{9,8},{10,11... | collective-permute-start | bytes 786440 | tf_op jit(solution)/shard_map/ppermute | solution.py:160
  41.7 33.5 %all-to-all-start.1 = ((bf16[4,2,256,512]{3,2,1,0:T(8,128)(2,1)}), bf16[4,2,256,512]{3,2,1,0:T(8,128)(2,1)}, u32[]{:S(2)}, u32[]{:S(2)}) async-start(bf16[4,2,256,512]{3,2,1,0:T(8,128)(2,1)} %broadcast_in_dim.35), calls=%async_computation.1 | async-start | bytes 4194304 | tf_op jit(solution)/shard_map/all_to_all | solution.py:178
  46.2 21.0 %copy-start.4 = (f32[1024]{0:T(1024)S(1)}, f32[1024]{0:T(1024)}, u32[]{:S(2)}) copy-start(f32[1024]{0:T(1024)} %param.10) | copy-start | bytes 12292
  46.2 18.9 %collective-permute-start.1 = (bf16[32,24,512]{2,1,0:T(8,128)(2,1)S(1)}, bf16[32,24,512]{2,1,0:T(8,128)(2,1)S(1)}, u32[]{:S(2)}, u32[]{:S(2)}) collective-permute-start(bf16[32,24,512]{2,1,0:T(8,128)(2,1)S(1)} %all-to-all-done), channel_id=1, source_target_pairs={{0,32},{32,64},{64,96},{96,0},{1,33},{33,65},{65,97},{97,1},{2,34}... | collective-permute-start | bytes 2359304 | tf_op jit(solution)/shard_map/ppermute | solution.py:156
  49.4 9.0 %collective-permute-start.3 = (bf16[16,24,512]{2,1,0:T(8,128)(2,1)S(1)}, bf16[16,24,512]{2,1,0:T(8,128)(2,1)S(1)}, u32[]{:S(2)}, u32[]{:S(2)}) collective-permute-start(bf16[16,24,512]{2,1,0:T(8,128)(2,1)S(1)} %get-tuple-element.15), channel_id=1, source_target_pairs={{0,96},{32,0},{64,32},{96,64},{1,97},{33,1},{65,33},{97,65},{2,98}... | collective-permute-start | bytes 1179656 | tf_op jit(solution)/shard_map/ppermute | solution.py:156
  52.7 14.5 %collective-permute-start.2 = (bf16[16,24,512]{2,1,0:T(8,128)(2,1)S(1)}, bf16[16,24,512]{2,1,0:T(8,128)(2,1)S(1)}, u32[]{:S(2)}, u32[]{:S(2)}) collective-permute-start(bf16[16,24,512]{2,1,0:T(8,128)(2,1)S(1)} %get-tuple-element.16), channel_id=1, source_target_pairs={{0,96},{32,0},{64,32},{96,64},{1,97},{33,1},{65,33},{97,65},{2,98}... | collective-permute-start | bytes 1179656 | tf_op jit(solution)/shard_map/ppermute | solution.py:156
  58.4 16.7 %collective-permute-start.5 = (bf16[16,24,512]{2,1,0:T(8,128)(2,1)S(1)}, bf16[16,24,512]{2,1,0:T(8,128)(2,1)S(1)}, u32[]{:S(2)}, u32[]{:S(2)}) collective-permute-start(bf16[16,24,512]{2,1,0:T(8,128)(2,1)S(1)} %collective-permute-done.3), channel_id=1, source_target_pairs={{0,96},{32,0},{64,32},{96,64},{1,97},{33,1},{65,33},{97,65},{2,98}... | collective-permute-start | bytes 1179656 | tf_op jit(solution)/shard_map/ppermute | solution.py:156
  65.1 10.1 %collective-permute-start.4 = (bf16[16,24,512]{2,1,0:T(8,128)(2,1)S(1)}, bf16[16,24,512]{2,1,0:T(8,128)(2,1)S(1)}, u32[]{:S(2)}, u32[]{:S(2)}) collective-permute-start(bf16[16,24,512]{2,1,0:T(8,128)(2,1)S(1)} %get-tuple-element.18), channel_id=1, source_target_pairs={{0,32},{32,64},{64,96},{96,0},{1,33},{33,65},{65,97},{97,1},{2,34}... | collective-permute-start | bytes 1179656 | tf_op jit(solution)/shard_map/ppermute | solution.py:156
  78.9 16.1 %copy-start.3 = (s32[256]{0:T(256)S(1)}, s32[256]{0:T(256)}, u32[]{:S(2)}) copy-start(s32[256]{0:T(256)} %param.8) | copy-start | bytes 3076
  78.9 23.5 %copy-start.1 = (f32[1024]{0:T(1024)S(1)}, f32[1024]{0:T(1024)}, u32[]{:S(2)}) copy-start(f32[1024]{0:T(1024)} %param.12) | copy-start | bytes 12292
  78.9 11.0 %collective-permute-start.6 = (bf16[4,64,1024]{2,1,0:T(8,128)(2,1)S(1)}, bf16[4,64,1024]{2,1,0:T(8,128)(2,1)S(1)}, u32[]{:S(2)}, u32[]{:S(2)}) collective-permute-start(bf16[4,64,1024]{2,1,0:T(8,128)(2,1)S(1)} %get-tuple-element.12), channel_id=1, source_target_pairs={{0,1},{1,0},{2,3},{3,2},{4,5},{5,4},{6,7},{7,6},{8,9},{9,8},{10,11... | collective-permute-start | bytes 1572872 | tf_op jit(solution)/shard_map/ppermute | solution.py:160
  90.9 11.6 %all-to-all-start.2 = ((bf16[4,64,1024]{2,1,0:T(8,128)(2,1)}), bf16[4,64,1024]{2,1,0:T(8,128)(2,1)S(1)}, u32[]{:S(2)}, u32[]{:S(2)}) async-start(bf16[4,64,1024]{2,1,0:T(8,128)(2,1)} %add_convert_fusion), calls=%async_computation.2 | async-start | bytes 1048576 | tf_op jit(solution)/shard_map/all_to_all | solution.py:184
  95.0 41.6 %copy-start = (bf16[2048,256]{1,0:T(8,128)(2,1)S(1)}, bf16[2048,256]{1,0:T(8,128)(2,1)}, u32[]{:S(2)}) copy-start(bf16[2048,256]{1,0:T(8,128)(2,1)} %table_ref.1) | copy-start | bytes 3145732
  103.3 8.4 %all-to-all-start.3 = ((bf16[4,64,256]{2,1,0:T(8,128)(2,1)}), bf16[4,64,256]{2,1,0:T(8,128)(2,1)S(1)}, u32[]{:S(2)}, u32[]{:S(2)}) async-start(bf16[4,64,256]{2,1,0:T(8,128)(2,1)} %norm.1), calls=%async_computation.3 | async-start | bytes 262144 | tf_op jit(solution)/shard_map/all_to_all | solution.py:186

commit v9 on v8

--- a/solution.py
+++ b/solution.py
@@ -170,9 +170,8 @@
     pair = jnp.stack([features, swap(features, "core")])
     copies = jnp.broadcast_to(pair[None], (4, 2, SRC, 512))
     mine, copies = lax.optimization_barrier((mine, copies))
-    left = along_x(mine, 1)
-    rb, ra = along_x(mine[16:], -1), along_x(mine[:16], -1)
-    la, lb = left[:16], left[16:]
+    la, rb = along_x(mine[:16], 1), along_x(mine[16:], -1)
+    lb, ra = along_x(mine[16:], 1), along_x(mine[:16], -1)
     fa, fb = along_x(la, 1), along_x(rb, -1)
 
     feats = lax.all_to_all(copies, ("zl", "yl"), split_axis=0, concat_axis=0, tiled=True)

time: 142 us -> 142 us (level)
    ppermute x2, starting transfers between devices: 12.3 us -> 9.15 us  [swap(): return lax.ppermute(block, axis, [(0, 1), (1, 0)])]
    ppermute x5 -> x6, starting transfers between devices: 16.2 us -> 18.1 us  [along_x(): return lax.ppermute(block, 'x', [(i, (i + step) % 4) for i in range(4)])]
    ppermute x5 -> x6, waiting for transfers between devices: 12.5 us -> 13.2 us  [along_x(): return lax.ppermute(block, 'x', [(i, (i + step) % 4) for i in range(4)])]
  transfers between devices with their start and end apart: 11 -> 12, of which waited for: 8 -> 8; matrix products, arithmetic and copies ran while one was open for 0% -> 1% of each run, Pallas kernels for 0% -> 0%
where the time goes in v9:
time: 142 us; the launch traced here: 140 us
  starting transfers between devices  56.9 us (40%)
  waiting for transfers between devices  44.4 us (31%)
  blocking collectives  24.6 us (17%)
  Pallas kernels  7.31 us (5%)
  local copies, waits for them, and re-layouts  3.58 us (3%)
  other arithmetic  2.28 us (2%)
    all_to_all x1, blocking collectives, local(): lax.all_to_all(packed.reshape(OWNERS, CAP, SHARE + META), ROUTE, split_ax...  24.6 us
    ppermute x6, starting transfers between devices, along_x(): return lax.ppermute(block, 'x', [(i, (i + step) % 4) for i in range(4)])  18.1 us
    all_to_all x1, waiting for transfers between devices, local(): mine = lax.all_to_all(w, PLANE, split_axis=0, concat_axis=0, tiled=True)  17.8 us
    all_to_all x1, starting transfers between devices, local(): mine = lax.all_to_all(w, PLANE, split_axis=0, concat_axis=0, tiled=True)  16.5 us
    ppermute x6, waiting for transfers between devices, along_x(): return lax.ppermute(block, 'x', [(i, (i + step) % 4) for i in range(4)])  13.2 us
    ppermute x2, starting transfers between devices, swap(): return lax.ppermute(block, axis, [(0, 1), (1, 0)])  9.15 us
    all_to_all x1, waiting for transfers between devices, local(): lax.all_to_all(chip, ('zl', 'yl'), split_axis=0, concat_axis=0, tiled=True)  7.27 us
    all_to_all x1, starting transfers between devices, local(): lax.all_to_all(columns, TP, split_axis=0, concat_axis=0, tiled=True)  4.77 us
  transfers between devices with their start and end apart: 12, of which 8 were waited for; matrix products, arithmetic and copies ran while one was open for 1% of the time, Pallas kernels for 0%

profile of v9, /device:TPU:1, one launch (start us, length us, event | category | flops | bytes accessed | tf_op | source)
XLA Modules:
  0.0 139.6 jit_solution(4191332917513029247)
XLA Ops:
  0.0 0.0 copy-start.2
  0.0 0.8 pad_maximum_fusion.1
  0.9 1.0 broadcast_in_dim.34
  1.8 16.5 %all-to-all-start = ((bf16[32,24,512]{2,1,0:T(8,128)(2,1)}), bf16[32,24,512]{2,1,0:T(8,128)(2,1)S(1)}, u32[]{:S(2)}, u32[]{:S(2)}) async-start(bf16[32,24,512]{2,1,0:T(8,128)(2,1)} %bitcast.5), calls=%async_computation | async-start | bytes 1572864 | tf_op jit(solution)/shard_map/all_to_all | solution.py:169
  18.4 0.0 copy-done.2
  18.4 2.9 %collective-permute-start = (bf16[256,512]{1,0:T(8,128)(2,1)S(1)}, bf16[256,512]{1,0:T(8,128)(2,1)S(1)}, u32[]{:S(2)}, u32[]{:S(2)}) collective-permute-start(bf16[256,512]{1,0:T(8,128)(2,1)S(1)} %copy-done.2), channel_id=1, source_target_pairs={{0,1},{1,0},{2,3},{3,2},{4,5},{5,4},{6,7},{7,6},{8,9},{9,8},{10,11... | collective-permute-start | bytes 786440 | tf_op jit(solution)/shard_map/ppermute | solution.py:160
  21.2 1.1 collective-permute-done
  22.4 0.1 pad_maximum_fusion
  22.4 17.8 %all-to-all-done = bf16[32,24,512]{2,1,0:T(8,128)(2,1)S(1)} async-done(((bf16[32,24,512]{2,1,0:T(8,128)(2,1)}), bf16[32,24,512]{2,1,0:T(8,128)(2,1)S(1)}, u32[]{:S(2)}, u32[]{:S(2)}) %all-to-all-start) | async-done | bytes 786464 | tf_op jit(solution)/shard_map/all_to_all | solution.py:169
  40.2 1.5 %broadcast_in_dim.35 = bf16[4,2,256,512]{3,2,1,0:T(8,128)(2,1)} broadcast(bf16[2,256,512]{2,1,0:T(8,128)(2,1)S(1)} %pad_maximum_fusion), dimensions={1,2,3} | broadcast | bytes 2621440 | tf_op jit(solution)/shard_map/broadcast_in_dim | solution.py:171
  41.7 0.0 copy-start.4
  41.7 4.6 %all-to-all-start.1 = ((bf16[4,2,256,512]{3,2,1,0:T(8,128)(2,1)}), bf16[4,2,256,512]{3,2,1,0:T(8,128)(2,1)}, u32[]{:S(2)}, u32[]{:S(2)}) async-start(bf16[4,2,256,512]{3,2,1,0:T(8,128)(2,1)} %broadcast_in_dim.35), calls=%async_computation.1 | async-start | bytes 4194304 | tf_op jit(solution)/shard_map/all_to_all | solution.py:177
  46.3 0.8 fusion.6
  47.1 4.4 %collective-permute-start.4 = (bf16[16,24,512]{2,1,0:T(8,128)(2,1)}, bf16[16,24,512]{2,1,0:T(8,128)(2,1)S(1)}, u32[]{:S(2)}, u32[]{:S(2)}) collective-permute-start(bf16[16,24,512]{2,1,0:T(8,128)(2,1)} %get-tuple-element.15), channel_id=1, source_target_pairs={{0,96},{32,0},{64,32},{96,64},{1,97},{33,1},{65,33},{97,65},{2,98}... | collective-permute-start | bytes 1179656 | tf_op jit(solution)/shard_map/ppermute | solution.py:156
  51.5 1.9 %collective-permute-start.1 = (bf16[16,24,512]{2,1,0:T(8,128)(2,1)S(1)}, bf16[16,24,512]{2,1,0:T(8,128)(2,1)S(1)}, u32[]{:S(2)}, u32[]{:S(2)}) collective-permute-start(bf16[16,24,512]{2,1,0:T(8,128)(2,1)S(1)} %get-tuple-element.16), channel_id=1, source_target_pairs={{0,32},{32,64},{64,96},{96,0},{1,33},{33,65},{65,97},{97,1},{2,34}... | collective-permute-start | bytes 1179656 | tf_op jit(solution)/shard_map/ppermute | solution.py:156
  53.4 2.1 %collective-permute-start.2 = (bf16[16,24,512]{2,1,0:T(8,128)(2,1)}, bf16[16,24,512]{2,1,0:T(8,128)(2,1)S(1)}, u32[]{:S(2)}, u32[]{:S(2)}) collective-permute-start(bf16[16,24,512]{2,1,0:T(8,128)(2,1)} %get-tuple-element.15), channel_id=1, source_target_pairs={{0,32},{32,64},{64,96},{96,0},{1,33},{33,65},{65,97},{97,1},{2,34}... | collective-permute-start | bytes 1179656 | tf_op jit(solution)/shard_map/ppermute | solution.py:156
  55.5 4.4 %collective-permute-start.3 = (bf16[16,24,512]{2,1,0:T(8,128)(2,1)S(1)}, bf16[16,24,512]{2,1,0:T(8,128)(2,1)S(1)}, u32[]{:S(2)}, u32[]{:S(2)}) collective-permute-start(bf16[16,24,512]{2,1,0:T(8,128)(2,1)S(1)} %get-tuple-element.16), channel_id=1, source_target_pairs={{0,96},{32,0},{64,32},{96,64},{1,97},{33,1},{65,33},{97,65},{2,98}... | collective-permute-start | bytes 1179656 | tf_op jit(solution)/shard_map/ppermute | solution.py:156
  59.9 0.0 collective-permute-done.4
  59.9 3.4 %collective-permute-start.6 = (bf16[16,24,512]{2,1,0:T(8,128)(2,1)S(1)}, bf16[16,24,512]{2,1,0:T(8,128)(2,1)S(1)}, u32[]{:S(2)}, u32[]{:S(2)}) collective-permute-start(bf16[16,24,512]{2,1,0:T(8,128)(2,1)S(1)} %collective-permute-done.4), channel_id=1, source_target_pairs={{0,96},{32,0},{64,32},{96,64},{1,97},{33,1},{65,33},{97,65},{2,98}... | collective-permute-start | bytes 1179656 | tf_op jit(solution)/shard_map/ppermute | solution.py:156
  63.3 0.0 collective-permute-done.1
  63.3 1.9 %collective-permute-start.5 = (bf16[16,24,512]{2,1,0:T(8,128)(2,1)S(1)}, bf16[16,24,512]{2,1,0:T(8,128)(2,1)S(1)}, u32[]{:S(2)}, u32[]{:S(2)}) collective-permute-start(bf16[16,24,512]{2,1,0:T(8,128)(2,1)S(1)} %collective-permute-done.1), channel_id=1, source_target_pairs={{0,32},{32,64},{64,96},{96,0},{1,33},{33,65},{65,97},{97,1},{2,34}... | collective-permute-start | bytes 1179656 | tf_op jit(solution)/shard_map/ppermute | solution.py:156
  65.2 0.0 copy-done.4
  65.3 0.1 dynamic_slice.3
  65.3 0.1 pad_add_fusion.place_ref
  65.4 4.8 %collective-permute-done.2 = bf16[16,24,512]{2,1,0:T(8,128)(2,1)S(1)} collective-permute-done((bf16[16,24,512]{2,1,0:T(8,128)(2,1)}, bf16[16,24,512]{2,1,0:T(8,128)(2,1)S(1)}, u32[]{:S(2)}, u32[]{:S(2)}) %collective-permute-start.2) | collective-permute-done | bytes 393248 | tf_op jit(solution)/shard_map/ppermute | solution.py:156
  70.2 0.0 collective-permute-done.3
  70.2 3.2 %collective-permute-done.6 = bf16[16,24,512]{2,1,0:T(8,128)(2,1)S(1)} collective-permute-done((bf16[16,24,512]{2,1,0:T(8,128)(2,1)S(1)}, bf16[16,24,512]{2,1,0:T(8,128)(2,1)S(1)}, u32[]{:S(2)}, u32[]{:S(2)}) %collective-permute-start.6) | collective-permute-done | bytes 393248 | tf_op jit(solution)/shard_map/ppermute | solution.py:156
  73.4 5.2 %collective-permute-done.5 = bf16[16,24,512]{2,1,0:T(8,128)(2,1)S(1)} collective-permute-done((bf16[16,24,512]{2,1,0:T(8,128)(2,1)S(1)}, bf16[16,24,512]{2,1,0:T(8,128)(2,1)S(1)}, u32[]{:S(2)}, u32[]{:S(2)}) %collective-permute-start.5) | collective-permute-done | bytes 393248 | tf_op jit(solution)/shard_map/ppermute | solution.py:156
  78.6 0.0 all-to-all-done.1.feats
  78.6 3.7 %tower.1 = (bf16[4,64,1024]{2,1,0:T(8,128)(2,1)S(1)}, bf16[4,64,1024]{2,1,0:T(8,128)(2,1)S(1)}) custom-call(s32[4]{0:T(128)S(1)} %pad_add_fusion.place_ref, bf16[4,2,256,512]{3,2,1,0:T(8,128)(2,1)} %all-to-all-done.1.feats, bf16[4,4,2,24,512]{4,3,2,1,0:T(8,128)(2,1)S(1)} %bitcast.18, bf16[2,4,2,24,512]{4,3,2,1,0:T(8,128)(2,1)S(1)} %bitcast.20, ...), custom_call_target="tpu_custom_call" | custom-call | tf_op jit(solution)/shard_map/tower/pallas_call | solution.py:90
  82.3 0.0 copy-start.3
  82.4 0.0 copy-start.1
  82.4 6.3 %collective-permute-start.7 = (bf16[4,64,1024]{2,1,0:T(8,128)(2,1)S(1)}, bf16[4,64,1024]{2,1,0:T(8,128)(2,1)S(1)}, u32[]{:S(2)}, u32[]{:S(2)}) collective-permute-start(bf16[4,64,1024]{2,1,0:T(8,128)(2,1)S(1)} %get-tuple-element.12), channel_id=1, source_target_pairs={{0,1},{1,0},{2,3},{3,2},{4,5},{5,4},{6,7},{7,6},{8,9},{9,8},{10,11... | collective-permute-start | bytes 1572872 | tf_op jit(solution)/shard_map/ppermute | solution.py:160
  88.7 1.5 %collective-permute-done.7 = bf16[4,64,1024]{2,1,0:T(8,128)(2,1)S(1)} collective-permute-done((bf16[4,64,1024]{2,1,0:T(8,128)(2,1)S(1)}, bf16[4,64,1024]{2,1,0:T(8,128)(2,1)S(1)}, u32[]{:S(2)}, u32[]{:S(2)}) %collective-permute-start.7) | collective-permute-done | bytes 524320 | tf_op jit(solution)/shard_map/ppermute | solution.py:160
  90.2 1.0 add_convert_fusion
  91.2 3.8 %all-to-all-start.2 = ((bf16[4,64,1024]{2,1,0:T(8,128)(2,1)}), bf16[4,64,1024]{2,1,0:T(8,128)(2,1)S(1)}, u32[]{:S(2)}, u32[]{:S(2)}) async-start(bf16[4,64,1024]{2,1,0:T(8,128)(2,1)} %add_convert_fusion), calls=%async_computation.2 | async-start | bytes 1048576 | tf_op jit(solution)/shard_map/all_to_all | solution.py:183
  95.0 0.0 copy-start
  95.0 0.0 copy-done.3
  95.0 0.2 convert_reduce_fusion
  95.2 7.3 %all-to-all-done.2.parts_ref = bf16[4,64,1024]{2,1,0:T(8,128)(2,1)S(1)} async-done(((bf16[4,64,1024]{2,1,0:T(8,128)(2,1)}), bf16[4,64,1024]{2,1,0:T(8,128)(2,1)S(1)}, u32[]{:S(2)}, u32[]{:S(2)}) %all-to-all-start.2) | async-done | bytes 524320 | tf_op jit(solution)/shard_map/all_to_all | solution.py:183
  102.5 0.0 copy-done.1
  102.5 0.8 norm.1
  103.3 4.8 %all-to-all-start.3 = ((bf16[4,64,256]{2,1,0:T(8,128)(2,1)}), bf16[4,64,256]{2,1,0:T(8,128)(2,1)S(1)}, u32[]{:S(2)}, u32[]{:S(2)}) async-start(bf16[4,64,256]{2,1,0:T(8,128)(2,1)} %norm.1), calls=%async_computation.3 | async-start | bytes 262144 | tf_op jit(solution)/shard_map/all_to_all | solution.py:185
  108.1 0.1 select_convert_fusion
  108.2 3.5 %all-to-all-done.3 = bf16[4,64,256]{2,1,0:T(8,128)(2,1)S(1)} async-done(((bf16[4,64,256]{2,1,0:T(8,128)(2,1)}), bf16[4,64,256]{2,1,0:T(8,128)(2,1)S(1)}, u32[]{:S(2)}, u32[]{:S(2)}) %all-to-all-start.3) | async-done | bytes 131104 | tf_op jit(solution)/shard_map/all_to_all | solution.py:185
  111.7 0.3 convolution_convert_fusion
  112.0 0.1 reshape.71
  112.1 24.6 %all_to_all.25 = bf16[128,4,384]{2,1,0:T(4,128)(2,1)S(1)} all-to-all(bf16[128,4,384]{2,1,0:T(4,128)(2,1)S(1)} %reshape.71), channel_id=1, replica_groups=mesh['zh'=4,'x'=4,'yh'=4,'yl'=2,'zl'=2,'core'=2] {'yl','yh','x','zh'}, dimensions={0} | all-to-all | bytes 786432 | tf_op jit(solution)/shard_map/all_to_all | solution.py:203
  136.7 0.1 reshape.72.rows_ref
  136.8 0.0 copy-done
  136.8 2.7 %write.1 = bf16[2048,256]{1,0:T(8,128)(2,1)} custom-call(bf16[2048,256]{1,0:T(8,128)(2,1)S(1)} %copy-done, bf16[512,384]{1,0:T(8,128)(2,1)S(1)} %reshape.72.rows_ref), custom_call_target="tpu_custom_call" | custom-call | tf_op jit(solution)/shard_map/write/pallas_call | solution.py:143
  (5 shorter events, 0.1 us)
Async XLA Ops:
  0.0 18.4 %copy-start.2 = (bf16[256,512]{1,0:T(8,128)(2,1)S(1)}, bf16[256,512]{1,0:T(8,128)(2,1)}, u32[]{:S(2)}) copy-start(bf16[256,512]{1,0:T(8,128)(2,1)} %param.7) | copy-start | bytes 786436
  1.8 38.4 %all-to-all-start = ((bf16[32,24,512]{2,1,0:T(8,128)(2,1)}), bf16[32,24,512]{2,1,0:T(8,128)(2,1)S(1)}, u32[]{:S(2)}, u32[]{:S(2)}) async-start(bf16[32,24,512]{2,1,0:T(8,128)(2,1)} %bitcast.5), calls=%async_computation | async-start | bytes 1572864 | tf_op jit(solution)/shard_map/all_to_all | solution.py:169
  18.4 4.0 %collective-permute-start = (bf16[256,512]{1,0:T(8,128)(2,1)S(1)}, bf16[256,512]{1,0:T(8,128)(2,1)S(1)}, u32[]{:S(2)}, u32[]{:S(2)}) collective-permute-start(bf16[256,512]{1,0:T(8,128)(2,1)S(1)} %copy-done.2), channel_id=1, source_target_pairs={{0,1},{1,0},{2,3},{3,2},{4,5},{5,4},{6,7},{7,6},{8,9},{9,8},{10,11... | collective-permute-start | bytes 786440 | tf_op jit(solution)/shard_map/ppermute | solution.py:160
  41.7 23.6 %copy-start.4 = (f32[1024]{0:T(1024)S(1)}, f32[1024]{0:T(1024)}, u32[]{:S(2)}) copy-start(f32[1024]{0:T(1024)} %param.10) | copy-start | bytes 12292
  41.7 36.9 %all-to-all-start.1 = ((bf16[4,2,256,512]{3,2,1,0:T(8,128)(2,1)}), bf16[4,2,256,512]{3,2,1,0:T(8,128)(2,1)}, u32[]{:S(2)}, u32[]{:S(2)}) async-start(bf16[4,2,256,512]{3,2,1,0:T(8,128)(2,1)} %broadcast_in_dim.35), calls=%async_computation.1 | async-start | bytes 4194304 | tf_op jit(solution)/shard_map/all_to_all | solution.py:177
  47.1 12.8 %collective-permute-start.4 = (bf16[16,24,512]{2,1,0:T(8,128)(2,1)}, bf16[16,24,512]{2,1,0:T(8,128)(2,1)S(1)}, u32[]{:S(2)}, u32[]{:S(2)}) collective-permute-start(bf16[16,24,512]{2,1,0:T(8,128)(2,1)} %get-tuple-element.15), channel_id=1, source_target_pairs={{0,96},{32,0},{64,32},{96,64},{1,97},{33,1},{65,33},{97,65},{2,98}... | collective-permute-start | bytes 1179656 | tf_op jit(solution)/shard_map/ppermute | solution.py:156
  51.5 11.8 %collective-permute-start.1 = (bf16[16,24,512]{2,1,0:T(8,128)(2,1)S(1)}, bf16[16,24,512]{2,1,0:T(8,128)(2,1)S(1)}, u32[]{:S(2)}, u32[]{:S(2)}) collective-permute-start(bf16[16,24,512]{2,1,0:T(8,128)(2,1)S(1)} %get-tuple-element.16), channel_id=1, source_target_pairs={{0,32},{32,64},{64,96},{96,0},{1,33},{33,65},{65,97},{97,1},{2,34}... | collective-permute-start | bytes 1179656 | tf_op jit(solution)/shard_map/ppermute | solution.py:156
  53.4 16.8 %collective-permute-start.2 = (bf16[16,24,512]{2,1,0:T(8,128)(2,1)}, bf16[16,24,512]{2,1,0:T(8,128)(2,1)S(1)}, u32[]{:S(2)}, u32[]{:S(2)}) collective-permute-start(bf16[16,24,512]{2,1,0:T(8,128)(2,1)} %get-tuple-element.15), channel_id=1, source_target_pairs={{0,32},{32,64},{64,96},{96,0},{1,33},{33,65},{65,97},{97,1},{2,34}... | collective-permute-start | bytes 1179656 | tf_op jit(solution)/shard_map/ppermute | solution.py:156
  55.5 14.7 %collective-permute-start.3 = (bf16[16,24,512]{2,1,0:T(8,128)(2,1)S(1)}, bf16[16,24,512]{2,1,0:T(8,128)(2,1)S(1)}, u32[]{:S(2)}, u32[]{:S(2)}) collective-permute-start(bf16[16,24,512]{2,1,0:T(8,128)(2,1)S(1)} %get-tuple-element.16), channel_id=1, source_target_pairs={{0,96},{32,0},{64,32},{96,64},{1,97},{33,1},{65,33},{97,65},{2,98}... | collective-permute-start | bytes 1179656 | tf_op jit(solution)/shard_map/ppermute | solution.py:156
  59.9 13.5 %collective-permute-start.6 = (bf16[16,24,512]{2,1,0:T(8,128)(2,1)S(1)}, bf16[16,24,512]{2,1,0:T(8,128)(2,1)S(1)}, u32[]{:S(2)}, u32[]{:S(2)}) collective-permute-start(bf16[16,24,512]{2,1,0:T(8,128)(2,1)S(1)} %collective-permute-done.4), channel_id=1, source_target_pairs={{0,96},{32,0},{64,32},{96,64},{1,97},{33,1},{65,33},{97,65},{2,98}... | collective-permute-start | bytes 1179656 | tf_op jit(solution)/shard_map/ppermute | solution.py:156
  63.3 15.3 %collective-permute-start.5 = (bf16[16,24,512]{2,1,0:T(8,128)(2,1)S(1)}, bf16[16,24,512]{2,1,0:T(8,128)(2,1)S(1)}, u32[]{:S(2)}, u32[]{:S(2)}) collective-permute-start(bf16[16,24,512]{2,1,0:T(8,128)(2,1)S(1)} %collective-permute-done.1), channel_id=1, source_target_pairs={{0,32},{32,64},{64,96},{96,0},{1,33},{33,65},{65,97},{97,1},{2,34}... | collective-permute-start | bytes 1179656 | tf_op jit(solution)/shard_map/ppermute | solution.py:156
  82.3 12.7 %copy-start.3 = (s32[256]{0:T(256)S(1)}, s32[256]{0:T(256)}, u32[]{:S(2)}) copy-start(s32[256]{0:T(256)} %param.8) | copy-start | bytes 3076
  82.4 20.1 %copy-start.1 = (f32[1024]{0:T(1024)S(1)}, f32[1024]{0:T(1024)}, u32[]{:S(2)}) copy-start(f32[1024]{0:T(1024)} %param.12) | copy-start | bytes 12292
  82.4 7.8 %collective-permute-start.7 = (bf16[4,64,1024]{2,1,0:T(8,128)(2,1)S(1)}, bf16[4,64,1024]{2,1,0:T(8,128)(2,1)S(1)}, u32[]{:S(2)}, u32[]{:S(2)}) collective-permute-start(bf16[4,64,1024]{2,1,0:T(8,128)(2,1)S(1)} %get-tuple-element.12), channel_id=1, source_target_pairs={{0,1},{1,0},{2,3},{3,2},{4,5},{5,4},{6,7},{7,6},{8,9},{9,8},{10,11... | collective-permute-start | bytes 1572872 | tf_op jit(solution)/shard_map/ppermute | solution.py:160
  91.2 11.3 %all-to-all-start.2 = ((bf16[4,64,1024]{2,1,0:T(8,128)(2,1)}), bf16[4,64,1024]{2,1,0:T(8,128)(2,1)S(1)}, u32[]{:S(2)}, u32[]{:S(2)}) async-start(bf16[4,64,1024]{2,1,0:T(8,128)(2,1)} %add_convert_fusion), calls=%async_computation.2 | async-start | bytes 1048576 | tf_op jit(solution)/shard_map/all_to_all | solution.py:183
  95.0 41.8 %copy-start = (bf16[2048,256]{1,0:T(8,128)(2,1)S(1)}, bf16[2048,256]{1,0:T(8,128)(2,1)}, u32[]{:S(2)}) copy-start(bf16[2048,256]{1,0:T(8,128)(2,1)} %table_ref.1) | copy-start | bytes 3145732
  103.3 8.4 %all-to-all-start.3 = ((bf16[4,64,256]{2,1,0:T(8,128)(2,1)}), bf16[4,64,256]{2,1,0:T(8,128)(2,1)S(1)}, u32[]{:S(2)}, u32[]{:S(2)}) async-start(bf16[4,64,256]{2,1,0:T(8,128)(2,1)} %norm.1), calls=%async_computation.3 | async-start | bytes 262144 | tf_op jit(solution)/shard_map/all_to_all | solution.py:185

commit v10 on v7

--- a/solution.py
+++ b/solution.py
@@ -137,7 +137,7 @@
 
 
 def write(table, rows):
-    block = 512
+    block = 1024
     spec = pl.BlockSpec((block, SHARE), lambda i: (i, 0))
     return pl.pallas_call(
         write_kernel,

time: 141 us -> 141 us (level)
  no operation moved by 1% of the time
where the time goes in v10:
time: 141 us; the launch traced here: 138 us
  starting transfers between devices  63.1 us (45%)
  waiting for transfers between devices  38.9 us (28%)
  blocking collectives  22.9 us (16%)
  Pallas kernels  6.69 us (5%)
  local copies, waits for them, and re-layouts  3.48 us (2%)
  other arithmetic  2.24 us (2%)
    ppermute x5, starting transfers between devices, swap(): return lax.ppermute(block, axis, [(0, 1), (1, 0)])  23.4 us
    all_to_all x1, blocking collectives, local(): lax.all_to_all(packed.reshape(OWNERS, CAP, SHARE + META), ROUTE, split_ax...  22.9 us
    all_to_all x1, waiting for transfers between devices, local(): mine = lax.all_to_all(w, PLANE, split_axis=0, concat_axis=0, tiled=True)  17.8 us
    all_to_all x1, starting transfers between devices, local(): mine = lax.all_to_all(w, PLANE, split_axis=0, concat_axis=0, tiled=True)  16.6 us
    ppermute x5, starting transfers between devices, along_x(): return lax.ppermute(block, 'x', [(i, (i + step) % 4) for i in range(4)])  15.1 us
    ppermute x5, waiting for transfers between devices, along_x(): return lax.ppermute(block, 'x', [(i, (i + step) % 4) for i in range(4)])  8.14 us
    all_to_all x1, waiting for transfers between devices, local(): lax.all_to_all(chip, ('zl', 'yl'), split_axis=0, concat_axis=0, tiled=True)  6.84 us
    all_to_all x1, starting transfers between devices, local(): lax.all_to_all(columns, TP, split_axis=0, concat_axis=0, tiled=True)  4.49 us
  transfers between devices with their start and end apart: 13, of which 6 were waited for; matrix products, arithmetic and copies ran while one was open for 1% of the time, Pallas kernels for 0%

profile of v10, /device:TPU:1, one launch (start us, length us, event | category | flops | bytes accessed | tf_op | source)
XLA Modules:
  0.0 137.8 jit_solution(15176962855756654595)
XLA Ops:
  0.0 0.8 pad_maximum_fusion.1
  0.8 1.0 broadcast_in_dim.32
  1.8 0.0 copy-start.3
  1.8 16.6 %all-to-all-start = ((bf16[32,24,512]{2,1,0:T(8,128)(2,1)}), bf16[32,24,512]{2,1,0:T(8,128)(2,1)S(1)}, u32[]{:S(2)}, u32[]{:S(2)}) async-start(bf16[32,24,512]{2,1,0:T(8,128)(2,1)} %bitcast.5), calls=%async_computation | async-start | bytes 1572864 | tf_op jit(solution)/shard_map/all_to_all | solution.py:168
  18.4 0.0 copy-done.3
  18.4 2.9 %collective-permute-start = (bf16[256,512]{1,0:T(8,128)(2,1)S(1)}, bf16[256,512]{1,0:T(8,128)(2,1)S(1)}, u32[]{:S(2)}, u32[]{:S(2)}) collective-permute-start(bf16[256,512]{1,0:T(8,128)(2,1)S(1)} %copy-done.3), channel_id=1, source_target_pairs={{0,1},{1,0},{2,3},{3,2},{4,5},{5,4},{6,7},{7,6},{8,9},{9,8},{10,11... | collective-permute-start | bytes 786440 | tf_op jit(solution)/shard_map/ppermute | solution.py:159
  21.3 1.1 collective-permute-done
  22.5 0.1 pad_maximum_fusion.f0
  22.5 17.8 %all-to-all-done = bf16[32,24,512]{2,1,0:T(8,128)(2,1)S(1)} async-done(((bf16[32,24,512]{2,1,0:T(8,128)(2,1)}), bf16[32,24,512]{2,1,0:T(8,128)(2,1)S(1)}, u32[]{:S(2)}, u32[]{:S(2)}) %all-to-all-start) | async-done | bytes 786464 | tf_op jit(solution)/shard_map/all_to_all | solution.py:168
  40.3 0.0 copy-start.2
  40.3 3.1 %collective-permute-start.4 = (bf16[32,24,512]{2,1,0:T(8,128)(2,1)S(1)}, bf16[32,24,512]{2,1,0:T(8,128)(2,1)S(1)}, u32[]{:S(2)}, u32[]{:S(2)}) collective-permute-start(bf16[32,24,512]{2,1,0:T(8,128)(2,1)S(1)} %all-to-all-done), channel_id=1, source_target_pairs={{0,32},{32,64},{64,96},{96,0},{1,33},{33,65},{65,97},{97,1},{2,34}... | collective-permute-start | bytes 2359304 | tf_op jit(solution)/shard_map/ppermute | solution.py:155
  43.4 3.6 %collective-permute-start.1 = (bf16[2,256,512]{2,1,0:T(8,128)(2,1)S(1)}, bf16[2,256,512]{2,1,0:T(8,128)(2,1)S(1)}, u32[]{:S(2)}, u32[]{:S(2)}) collective-permute-start(bf16[2,256,512]{2,1,0:T(8,128)(2,1)S(1)} %pad_maximum_fusion.f0), channel_id=1, source_target_pairs={{0,4},{4,0},{1,5},{5,1},{2,6},{6,2},{3,7},{7,3},{8,12},{12,8},{9,1... | collective-permute-start | bytes 1572872 | tf_op jit(solution)/shard_map/ppermute | solution.py:159
  47.1 0.8 fusion.6
  47.9 0.0 copy-done.2
  47.9 3.4 %collective-permute-start.6 = (bf16[16,24,512]{2,1,0:T(8,128)(2,1)S(1)}, bf16[16,24,512]{2,1,0:T(8,128)(2,1)S(1)}, u32[]{:S(2)}, u32[]{:S(2)}) collective-permute-start(bf16[16,24,512]{2,1,0:T(8,128)(2,1)S(1)} %get-tuple-element.15), channel_id=1, source_target_pairs={{0,96},{32,0},{64,32},{96,64},{1,97},{33,1},{65,33},{97,65},{2,98}... | collective-permute-start | bytes 1179656 | tf_op jit(solution)/shard_map/ppermute | solution.py:155
  51.2 3.0 %collective-permute-start.2 = (bf16[2,256,512]{2,1,0:T(8,128)(2,1)S(1)}, bf16[2,256,512]{2,1,0:T(8,128)(2,1)S(1)}, u32[]{:S(2)}, u32[]{:S(2)}) collective-permute-start(bf16[2,256,512]{2,1,0:T(8,128)(2,1)S(1)} %pad_maximum_fusion.f0), channel_id=1, source_target_pairs={{0,2},{2,0},{1,3},{3,1},{4,6},{6,4},{5,7},{7,5},{8,10},{10,8},{9,1... | collective-permute-start | bytes 1572872 | tf_op jit(solution)/shard_map/ppermute | solution.py:159
  54.3 3.2 %collective-permute-start.5 = (bf16[16,24,512]{2,1,0:T(8,128)(2,1)}, bf16[16,24,512]{2,1,0:T(8,128)(2,1)}, u32[]{:S(2)}, u32[]{:S(2)}) collective-permute-start(bf16[16,24,512]{2,1,0:T(8,128)(2,1)} %get-tuple-element.16), channel_id=1, source_target_pairs={{0,96},{32,0},{64,32},{96,64},{1,97},{33,1},{65,33},{97,65},{2,98}... | collective-permute-start | bytes 1179656 | tf_op jit(solution)/shard_map/ppermute | solution.py:155
  57.5 0.0 collective-permute-done.6
  57.5 3.5 %collective-permute-start.8 = (bf16[16,24,512]{2,1,0:T(8,128)(2,1)S(1)}, bf16[16,24,512]{2,1,0:T(8,128)(2,1)}, u32[]{:S(2)}, u32[]{:S(2)}) collective-permute-start(bf16[16,24,512]{2,1,0:T(8,128)(2,1)S(1)} %collective-permute-done.6), channel_id=1, source_target_pairs={{0,96},{32,0},{64,32},{96,64},{1,97},{33,1},{65,33},{97,65},{2,98}... | collective-permute-start | bytes 1179656 | tf_op jit(solution)/shard_map/ppermute | solution.py:155
  61.0 0.0 collective-permute-done.1.f1
  61.0 3.0 %collective-permute-start.3 = (bf16[2,256,512]{2,1,0:T(8,128)(2,1)S(1)}, bf16[2,256,512]{2,1,0:T(8,128)(2,1)S(1)}, u32[]{:S(2)}, u32[]{:S(2)}) collective-permute-start(bf16[2,256,512]{2,1,0:T(8,128)(2,1)S(1)} %collective-permute-done.1.f1), channel_id=1, source_target_pairs={{0,2},{2,0},{1,3},{3,1},{4,6},{6,4},{5,7},{7,5},{8,10},{10,8},{9,1... | collective-permute-start | bytes 1572872 | tf_op jit(solution)/shard_map/ppermute | solution.py:159
  64.0 0.0 collective-permute-done.4
  64.0 0.1 fusion.7
  64.1 1.9 %collective-permute-start.7 = (bf16[16,24,512]{2,1,0:T(8,128)(2,1)S(1)}, bf16[16,24,512]{2,1,0:T(8,128)(2,1)}, u32[]{:S(2)}, u32[]{:S(2)}) collective-permute-start(bf16[16,24,512]{2,1,0:T(8,128)(2,1)S(1)} %get-tuple-element.18), channel_id=1, source_target_pairs={{0,32},{32,64},{64,96},{96,0},{1,33},{33,65},{65,97},{97,1},{2,34}... | collective-permute-start | bytes 1179656 | tf_op jit(solution)/shard_map/ppermute | solution.py:155
  66.0 0.0 copy-start.5
  66.0 0.7 copy-done.5
  66.7 0.1 dynamic_slice.3
  66.8 0.1 pad_add_fusion.place_ref
  66.9 0.0 collective-permute-done.5
  66.9 0.0 collective-permute-done.2.f2
  66.9 8.1 %collective-permute-done.8 = bf16[16,24,512]{2,1,0:T(8,128)(2,1)} collective-permute-done((bf16[16,24,512]{2,1,0:T(8,128)(2,1)S(1)}, bf16[16,24,512]{2,1,0:T(8,128)(2,1)}, u32[]{:S(2)}, u32[]{:S(2)}) %collective-permute-start.8) | collective-permute-done | bytes 393248 | tf_op jit(solution)/shard_map/ppermute | solution.py:155
  75.0 0.0 collective-permute-done.3.f3
  75.0 0.0 collective-permute-done.7
  75.0 3.6 %tower.1 = (bf16[4,64,1024]{2,1,0:T(8,128)(2,1)S(1)}, bf16[4,64,1024]{2,1,0:T(8,128)(2,1)S(1)}) custom-call(s32[4]{0:T(128)S(1)} %pad_add_fusion.place_ref, bf16[2,256,512]{2,1,0:T(8,128)(2,1)S(1)} %pad_maximum_fusion.f0, bf16[2,256,512]{2,1,0:T(8,128)(2,1)S(1)} %collective-permute-done.1.f1, bf16[2,256,512]{2,1,0:T(8,128)(2,1)S(1)} %collective-permute-done.2.f2, ...), custom_call_target="tpu_custom_call" | custom-call | tf_op jit(solution)/shard_map/tower/pallas_call | solution.py:89
  78.6 10.9 %collective-permute-start.9 = (bf16[4,64,1024]{2,1,0:T(8,128)(2,1)S(1)}, bf16[4,64,1024]{2,1,0:T(8,128)(2,1)S(1)}, u32[]{:S(2)}, u32[]{:S(2)}) collective-permute-start(bf16[4,64,1024]{2,1,0:T(8,128)(2,1)S(1)} %get-tuple-element.12), channel_id=1, source_target_pairs={{0,1},{1,0},{2,3},{3,2},{4,5},{5,4},{6,7},{7,6},{8,9},{9,8},{10,11... | collective-permute-start | bytes 1572872 | tf_op jit(solution)/shard_map/ppermute | solution.py:159
  89.5 1.5 %collective-permute-done.9 = bf16[4,64,1024]{2,1,0:T(8,128)(2,1)S(1)} collective-permute-done((bf16[4,64,1024]{2,1,0:T(8,128)(2,1)S(1)}, bf16[4,64,1024]{2,1,0:T(8,128)(2,1)S(1)}, u32[]{:S(2)}, u32[]{:S(2)}) %collective-permute-start.9) | collective-permute-done | bytes 524320 | tf_op jit(solution)/shard_map/ppermute | solution.py:159
  91.0 1.0 add_convert_fusion
  92.0 3.5 %all-to-all-start.1 = ((bf16[4,64,1024]{2,1,0:T(8,128)(2,1)}), bf16[4,64,1024]{2,1,0:T(8,128)(2,1)S(1)}, u32[]{:S(2)}, u32[]{:S(2)}) async-start(bf16[4,64,1024]{2,1,0:T(8,128)(2,1)} %add_convert_fusion), calls=%async_computation.1 | async-start | bytes 1048576 | tf_op jit(solution)/shard_map/all_to_all | solution.py:185
  95.5 0.0 copy-start.4
  95.5 0.7 copy-done.4
  96.2 0.2 convert_reduce_fusion
  96.4 0.0 copy-start.1
  96.4 6.8 %all-to-all-done.1.parts_ref = bf16[4,64,1024]{2,1,0:T(8,128)(2,1)S(1)} async-done(((bf16[4,64,1024]{2,1,0:T(8,128)(2,1)}), bf16[4,64,1024]{2,1,0:T(8,128)(2,1)S(1)}, u32[]{:S(2)}, u32[]{:S(2)}) %all-to-all-start.1) | async-done | bytes 524320 | tf_op jit(solution)/shard_map/all_to_all | solution.py:185
  103.2 0.0 copy-done.1
  103.2 0.8 norm.1
  104.1 4.5 %all-to-all-start.2 = ((bf16[4,64,256]{2,1,0:T(8,128)(2,1)}), bf16[4,64,256]{2,1,0:T(8,128)(2,1)S(1)}, u32[]{:S(2)}, u32[]{:S(2)}) async-start(bf16[4,64,256]{2,1,0:T(8,128)(2,1)} %norm.1), calls=%async_computation.2 | async-start | bytes 262144 | tf_op jit(solution)/shard_map/all_to_all | solution.py:187
  108.5 0.1 select_convert_fusion
  108.7 3.5 %all-to-all-done.2 = bf16[4,64,256]{2,1,0:T(8,128)(2,1)S(1)} async-done(((bf16[4,64,256]{2,1,0:T(8,128)(2,1)}), bf16[4,64,256]{2,1,0:T(8,128)(2,1)S(1)}, u32[]{:S(2)}, u32[]{:S(2)}) %all-to-all-start.2) | async-done | bytes 131104 | tf_op jit(solution)/shard_map/all_to_all | solution.py:187
  112.1 0.3 convolution_convert_fusion
  112.5 0.0 copy-start
  112.5 0.1 reshape.70
  112.6 22.9 %all_to_all.20 = bf16[128,4,384]{2,1,0:T(4,128)(2,1)S(1)} all-to-all(bf16[128,4,384]{2,1,0:T(4,128)(2,1)S(1)} %reshape.70), channel_id=1, replica_groups=mesh['zh'=4,'x'=4,'yh'=4,'yl'=2,'zl'=2,'core'=2] {'yl','yh','x','zh'}, dimensions={0} | all-to-all | bytes 786432 | tf_op jit(solution)/shard_map/all_to_all | solution.py:205
  135.5 0.1 reshape.71.rows_ref
  135.6 0.0 copy-done
  135.6 2.2 %write.1 = bf16[2048,256]{1,0:T(8,128)(2,1)} custom-call(bf16[2048,256]{1,0:T(8,128)(2,1)S(1)} %copy-done, bf16[512,384]{1,0:T(8,128)(2,1)S(1)} %reshape.71.rows_ref), custom_call_target="tpu_custom_call" | custom-call | tf_op jit(solution)/shard_map/write/pallas_call | solution.py:142
  (5 shorter events, 0.1 us)
Async XLA Ops:
  1.8 16.6 %copy-start.3 = (bf16[256,512]{1,0:T(8,128)(2,1)S(1)}, bf16[256,512]{1,0:T(8,128)(2,1)}, u32[]{:S(2)}) copy-start(bf16[256,512]{1,0:T(8,128)(2,1)} %param.7) | copy-start | bytes 786436
  1.8 38.5 %all-to-all-start = ((bf16[32,24,512]{2,1,0:T(8,128)(2,1)}), bf16[32,24,512]{2,1,0:T(8,128)(2,1)S(1)}, u32[]{:S(2)}, u32[]{:S(2)}) async-start(bf16[32,24,512]{2,1,0:T(8,128)(2,1)} %bitcast.5), calls=%async_computation | async-start | bytes 1572864 | tf_op jit(solution)/shard_map/all_to_all | solution.py:168
  18.4 4.0 %collective-permute-start = (bf16[256,512]{1,0:T(8,128)(2,1)S(1)}, bf16[256,512]{1,0:T(8,128)(2,1)S(1)}, u32[]{:S(2)}, u32[]{:S(2)}) collective-permute-start(bf16[256,512]{1,0:T(8,128)(2,1)S(1)} %copy-done.3), channel_id=1, source_target_pairs={{0,1},{1,0},{2,3},{3,2},{4,5},{5,4},{6,7},{7,6},{8,9},{9,8},{10,11... | collective-permute-start | bytes 786440 | tf_op jit(solution)/shard_map/ppermute | solution.py:159
  40.3 7.6 %copy-start.2 = (bf16[32,24,512]{2,1,0:T(8,128)(2,1)}, bf16[32,24,512]{2,1,0:T(8,128)(2,1)S(1)}, u32[]{:S(2)}) copy-start(bf16[32,24,512]{2,1,0:T(8,128)(2,1)S(1)} %all-to-all-done) | copy-start | bytes 2359300
  40.3 23.7 %collective-permute-start.4 = (bf16[32,24,512]{2,1,0:T(8,128)(2,1)S(1)}, bf16[32,24,512]{2,1,0:T(8,128)(2,1)S(1)}, u32[]{:S(2)}, u32[]{:S(2)}) collective-permute-start(bf16[32,24,512]{2,1,0:T(8,128)(2,1)S(1)} %all-to-all-done), channel_id=1, source_target_pairs={{0,32},{32,64},{64,96},{96,0},{1,33},{33,65},{65,97},{97,1},{2,34}... | collective-permute-start | bytes 2359304 | tf_op jit(solution)/shard_map/ppermute | solution.py:155
  43.4 17.5 %collective-permute-start.1 = (bf16[2,256,512]{2,1,0:T(8,128)(2,1)S(1)}, bf16[2,256,512]{2,1,0:T(8,128)(2,1)S(1)}, u32[]{:S(2)}, u32[]{:S(2)}) collective-permute-start(bf16[2,256,512]{2,1,0:T(8,128)(2,1)S(1)} %pad_maximum_fusion.f0), channel_id=1, source_target_pairs={{0,4},{4,0},{1,5},{5,1},{2,6},{6,2},{3,7},{7,3},{8,12},{12,8},{9,1... | collective-permute-start | bytes 1572872 | tf_op jit(solution)/shard_map/ppermute | solution.py:159
  47.9 9.6 %collective-permute-start.6 = (bf16[16,24,512]{2,1,0:T(8,128)(2,1)S(1)}, bf16[16,24,512]{2,1,0:T(8,128)(2,1)S(1)}, u32[]{:S(2)}, u32[]{:S(2)}) collective-permute-start(bf16[16,24,512]{2,1,0:T(8,128)(2,1)S(1)} %get-tuple-element.15), channel_id=1, source_target_pairs={{0,96},{32,0},{64,32},{96,64},{1,97},{33,1},{65,33},{97,65},{2,98}... | collective-permute-start | bytes 1179656 | tf_op jit(solution)/shard_map/ppermute | solution.py:155
  51.2 15.6 %collective-permute-start.2 = (bf16[2,256,512]{2,1,0:T(8,128)(2,1)S(1)}, bf16[2,256,512]{2,1,0:T(8,128)(2,1)S(1)}, u32[]{:S(2)}, u32[]{:S(2)}) collective-permute-start(bf16[2,256,512]{2,1,0:T(8,128)(2,1)S(1)} %pad_maximum_fusion.f0), channel_id=1, source_target_pairs={{0,2},{2,0},{1,3},{3,1},{4,6},{6,4},{5,7},{7,5},{8,10},{10,8},{9,1... | collective-permute-start | bytes 1572872 | tf_op jit(solution)/shard_map/ppermute | solution.py:159
  54.3 12.6 %collective-permute-start.5 = (bf16[16,24,512]{2,1,0:T(8,128)(2,1)}, bf16[16,24,512]{2,1,0:T(8,128)(2,1)}, u32[]{:S(2)}, u32[]{:S(2)}) collective-permute-start(bf16[16,24,512]{2,1,0:T(8,128)(2,1)} %get-tuple-element.16), channel_id=1, source_target_pairs={{0,96},{32,0},{64,32},{96,64},{1,97},{33,1},{65,33},{97,65},{2,98}... | collective-permute-start | bytes 1179656 | tf_op jit(solution)/shard_map/ppermute | solution.py:155
  57.5 17.5 %collective-permute-start.8 = (bf16[16,24,512]{2,1,0:T(8,128)(2,1)S(1)}, bf16[16,24,512]{2,1,0:T(8,128)(2,1)}, u32[]{:S(2)}, u32[]{:S(2)}) collective-permute-start(bf16[16,24,512]{2,1,0:T(8,128)(2,1)S(1)} %collective-permute-done.6), channel_id=1, source_target_pairs={{0,96},{32,0},{64,32},{96,64},{1,97},{33,1},{65,33},{97,65},{2,98}... | collective-permute-start | bytes 1179656 | tf_op jit(solution)/shard_map/ppermute | solution.py:155
  61.0 14.0 %collective-permute-start.3 = (bf16[2,256,512]{2,1,0:T(8,128)(2,1)S(1)}, bf16[2,256,512]{2,1,0:T(8,128)(2,1)S(1)}, u32[]{:S(2)}, u32[]{:S(2)}) collective-permute-start(bf16[2,256,512]{2,1,0:T(8,128)(2,1)S(1)} %collective-permute-done.1.f1), channel_id=1, source_target_pairs={{0,2},{2,0},{1,3},{3,1},{4,6},{6,4},{5,7},{7,5},{8,10},{10,8},{9,1... | collective-permute-start | bytes 1572872 | tf_op jit(solution)/shard_map/ppermute | solution.py:159
  64.1 10.9 %collective-permute-start.7 = (bf16[16,24,512]{2,1,0:T(8,128)(2,1)S(1)}, bf16[16,24,512]{2,1,0:T(8,128)(2,1)}, u32[]{:S(2)}, u32[]{:S(2)}) collective-permute-start(bf16[16,24,512]{2,1,0:T(8,128)(2,1)S(1)} %get-tuple-element.18), channel_id=1, source_target_pairs={{0,32},{32,64},{64,96},{96,0},{1,33},{33,65},{65,97},{97,1},{2,34}... | collective-permute-start | bytes 1179656 | tf_op jit(solution)/shard_map/ppermute | solution.py:155
  66.0 0.7 copy-start.5
  78.6 12.4 %collective-permute-start.9 = (bf16[4,64,1024]{2,1,0:T(8,128)(2,1)S(1)}, bf16[4,64,1024]{2,1,0:T(8,128)(2,1)S(1)}, u32[]{:S(2)}, u32[]{:S(2)}) collective-permute-start(bf16[4,64,1024]{2,1,0:T(8,128)(2,1)S(1)} %get-tuple-element.12), channel_id=1, source_target_pairs={{0,1},{1,0},{2,3},{3,2},{4,5},{5,4},{6,7},{7,6},{8,9},{9,8},{10,11... | collective-permute-start | bytes 1572872 | tf_op jit(solution)/shard_map/ppermute | solution.py:159
  92.0 11.2 %all-to-all-start.1 = ((bf16[4,64,1024]{2,1,0:T(8,128)(2,1)}), bf16[4,64,1024]{2,1,0:T(8,128)(2,1)S(1)}, u32[]{:S(2)}, u32[]{:S(2)}) async-start(bf16[4,64,1024]{2,1,0:T(8,128)(2,1)} %add_convert_fusion), calls=%async_computation.1 | async-start | bytes 1048576 | tf_op jit(solution)/shard_map/all_to_all | solution.py:185
  95.5 0.7 copy-start.4
  96.4 6.9 %copy-start.1 = (f32[1024]{0:T(1024)S(1)}, f32[1024]{0:T(1024)}, u32[]{:S(2)}) copy-start(f32[1024]{0:T(1024)} %param.12) | copy-start | bytes 12292
  104.1 8.1 %all-to-all-start.2 = ((bf16[4,64,256]{2,1,0:T(8,128)(2,1)}), bf16[4,64,256]{2,1,0:T(8,128)(2,1)S(1)}, u32[]{:S(2)}, u32[]{:S(2)}) async-start(bf16[4,64,256]{2,1,0:T(8,128)(2,1)} %norm.1), calls=%async_computation.2 | async-start | bytes 262144 | tf_op jit(solution)/shard_map/all_to_all | solution.py:187
  112.5 23.1 %copy-start = (bf16[2048,256]{1,0:T(8,128)(2,1)S(1)}, bf16[2048,256]{1,0:T(8,128)(2,1)}, u32[]{:S(2)}) copy-start(bf16[2048,256]{1,0:T(8,128)(2,1)} %table_ref.1) | copy-start | bytes 3145732
